TPU v7x, 32 devices: a whole 2x2x4 slice. The times are simulated.
32 devices in a mesh: ctx: 8 (over z, x), tp: 4 (over y, core).
Axes of the slice: x: 2, y: 2, z: 4, core: 2. Of those that a mesh axis runs over, the one named last changes fastest.
Arguments:
- query_key_value_input: bfloat16 [3, 8192, 2048], P(None, 'tp', 'ctx'), may hold values from -6 to 6
- featurizer_weights: float32 [3, 7, 8192], P(None, None, 'tp'), may hold values from -2.4 to 2.4
- channel_skip_scale: float32 [8192], P(('tp', 'ctx')), may hold values from -4 to 4
- group_long_filters: float32 [512, 2048], P(('tp', 'ctx')), may hold values from -1 to 1, as said below
- frozen_weight: bfloat16 [4096, 8192], P('ctx', 'tp'), may hold values from -4 to 4
- down_update_weight: bfloat16 [16, 8192], P(None, 'tp'), may hold values from -0.0625 to 0.0625
- up_update_weight: bfloat16 [4096, 16], P('ctx'), may hold values from -1.5 to 1.5
- magnitude: float32 [4096], replicated, may hold values from 0.5 to 2
Outputs:
- projected: bfloat16 [4096, 2048], P('tp', 'ctx')
Inputs may be any that keep to these rules, and one draw needn't show every extreme that they name: `group_long_filters`: row g is the filter of channels g * 16 to g * 16 + 16 - 1 over lags 0 to 2047.
All inputs are finite; a program needn't handle non-finite values.
Results may differ from a plain program's by a relative error of at most 0.007.
Values may be sent and summed in bfloat16 or wider, within the bound.
No kernel may reach another device: no remote copies, remote signals or barrier semaphores. Data moves between devices by JAX's collectives and lax.ppermute only.
A program may use at most 192 MiB of HBM per device.

v0:
```python
import math

import jax
import jax.numpy as jnp
from jax import lax
from jax.sharding import PartitionSpec as P

OUTPUT_FEATURES = 4096
GROUP = 16
TAPS = 7


EPSILON = 1e-06


def shifted(block, axis, distance):
    devices = range(lax.axis_size(axis))
    route = [(i - distance, i) for i in devices if i - distance in devices]
    return lax.ppermute(block, axis, route)


def rotation_matrix(count, direction):
    index = jnp.arange(count, dtype=jnp.int32)
    product = index[:, None] * index[None, :] % count
    angle = product.astype(jnp.float32) * (2.0 * math.pi / count)
    cosine = jnp.cos(angle)
    sine = jnp.sin(angle) * direction
    upper = jnp.concatenate([cosine, -sine], axis=1)
    lower = jnp.concatenate([sine, cosine], axis=1)
    return jnp.concatenate([upper, lower], axis=0)


def twiddle_table(rows_count, cols_count):
    rows_index = jnp.arange(rows_count, dtype=jnp.int32)[:, None]
    cols_index = jnp.arange(cols_count, dtype=jnp.int32)[None, :]
    angle = (rows_index * cols_index).astype(jnp.float32) * (
        2.0 * math.pi / (rows_count * cols_count)
    )
    return (jnp.cos(angle), jnp.sin(angle))


def along_rows(real_part, imag_part, matrix, accuracy):
    count = real_part.shape[-2]
    stacked = jnp.concatenate([real_part, imag_part], axis=-2)
    result = jnp.einsum("...ab,ac->...cb", stacked, matrix, precision=accuracy)
    return (result[..., :count, :], result[..., count:, :])


def along_last(real_part, imag_part, matrix, accuracy):
    count = real_part.shape[-1]
    stacked = jnp.concatenate([real_part, imag_part], axis=-1)
    result = jnp.einsum("...b,bd->...d", stacked, matrix, precision=accuracy)
    return (result[..., :count], result[..., count:])


def forward_transform(real_part, imag_part, tables, accuracy):
    first_forward, second_forward, first_inverse, second_inverse, twiddle_cos, twiddle_sin = tables
    rows_real, rows_imag = along_rows(real_part, imag_part, first_forward, accuracy)
    turned_real = rows_real * twiddle_cos + rows_imag * twiddle_sin
    turned_imag = rows_imag * twiddle_cos - rows_real * twiddle_sin
    return along_last(turned_real, turned_imag, second_forward, accuracy)


def inverse_transform(real_part, imag_part, tables, accuracy):
    first_forward, second_forward, first_inverse, second_inverse, twiddle_cos, twiddle_sin = tables
    last_real, last_imag = along_last(real_part, imag_part, second_inverse, accuracy)
    turned_real = last_real * twiddle_cos - last_imag * twiddle_sin
    turned_imag = last_imag * twiddle_cos + last_real * twiddle_sin
    out_real, out_imag = along_rows(turned_real, turned_imag, first_inverse, accuracy)
    total = twiddle_cos.shape[0] * twiddle_cos.shape[1]
    return (out_real / total, out_imag / total)


def on_device(
    query_key_value_input,
    featurizer_weights,
    channel_skip_scale,
    group_long_filters,
    frozen_weight,
    down_update_weight,
    up_update_weight,
    magnitude,
):
    width = query_key_value_input.shape[1]
    tokens_here = query_key_value_input.shape[2]
    ctx_count = lax.axis_size("ctx")
    tail_tokens = query_key_value_input[:, :, tokens_here - (TAPS - 1) :]
    previous = shifted(tail_tokens, "ctx", 1)
    extended = jnp.concatenate([previous, query_key_value_input], axis=-1).astype(jnp.float32)
    featured = jnp.zeros((3, width, tokens_here), jnp.float32)
    for offset in range(TAPS):
        starting = TAPS - 1 - offset
        featured = (
            featured
            + featurizer_weights[:, offset, :, None]
            * extended[:, :, starting : starting + tokens_here]
        )
    query = featured[0]
    mixture = (featured[1] * featured[2]).astype(jnp.bfloat16)
    groups_here = width // GROUP
    half_group = GROUP // 2
    mixture_blocks = mixture.reshape(groups_here, half_group, 2, tokens_here)
    length = tokens_here * ctx_count
    total = 2 * length
    first_len = max(
        (divisor for divisor in range(1, math.isqrt(total) + 1) if total % divisor == 0)
    )
    second_len = total // first_len
    twiddle_cos, twiddle_sin = twiddle_table(first_len, second_len)
    tables = (
        rotation_matrix(first_len, 1.0),
        rotation_matrix(second_len, 1.0),
        rotation_matrix(first_len, -1.0),
        rotation_matrix(second_len, -1.0),
        twiddle_cos,
        twiddle_sin,
    )
    local_groups = group_long_filters.shape[0]
    filter_padded = jnp.concatenate(
        [group_long_filters, jnp.zeros_like(group_long_filters)], axis=-1
    )
    filter_real = filter_padded.reshape(local_groups, first_len, second_len)
    response_real, response_imag = forward_transform(
        filter_real, jnp.zeros_like(filter_real), tables, lax.Precision.HIGHEST
    )
    items = lax.all_to_all(mixture_blocks, "ctx", split_axis=0, concat_axis=3, tiled=True)
    values = items.astype(jnp.float32)
    lead_shape = values.shape[:2]
    signal_real = values[:, :, 0]
    signal_imag = values[:, :, 1]
    padding = jnp.zeros_like(signal_real)
    signal_real = jnp.concatenate([signal_real, padding], axis=-1).reshape(
        lead_shape + (first_len, second_len)
    )
    signal_imag = jnp.concatenate([signal_imag, padding], axis=-1).reshape(
        lead_shape + (first_len, second_len)
    )
    spectrum_real, spectrum_imag = forward_transform(
        signal_real, signal_imag, tables, lax.Precision.HIGH
    )
    product_real = spectrum_real * response_real[:, None] - spectrum_imag * response_imag[:, None]
    product_imag = spectrum_real * response_imag[:, None] + spectrum_imag * response_real[:, None]
    result_real, result_imag = inverse_transform(
        product_real, product_imag, tables, lax.Precision.HIGH
    )
    result_real = result_real.reshape(lead_shape + (total,))[..., :length]
    result_imag = result_imag.reshape(lead_shape + (total,))[..., :length]
    convolved = jnp.stack([result_real, result_imag], axis=2)
    skip_local = channel_skip_scale.reshape(local_groups, half_group, 2)[:, :, :, None]
    summed = (convolved + skip_local * items.astype(jnp.float32)).astype(jnp.bfloat16)
    returned = lax.all_to_all(summed, "ctx", split_axis=3, concat_axis=0, tiled=True)
    gating = (query * returned.reshape(width, tokens_here).astype(jnp.float32)).astype(jnp.bfloat16)
    lowrank_update = jnp.dot(
        up_update_weight, down_update_weight, preferred_element_type=jnp.float32
    )
    merged = (frozen_weight.astype(jnp.float32) + lowrank_update).astype(jnp.bfloat16)
    merged_wide = lax.optimization_barrier(merged).astype(jnp.float32)
    row_sums = jnp.sum(merged_wide * merged_wide, axis=1)
    tp_index = lax.axis_index("tp")
    rows_out = OUTPUT_FEATURES // lax.axis_size("tp")
    complete = lax.psum(row_sums, "tp")
    every_norm = lax.all_gather(complete, "ctx", axis=0, tiled=True)
    partial_value = jnp.dot(
        lax.all_gather(merged, "ctx", axis=0, tiled=True),
        gating,
        preferred_element_type=jnp.float32,
    )
    output_block = lax.psum_scatter(partial_value, "tp", scatter_dimension=0, tiled=True)
    norms_here = lax.dynamic_slice_in_dim(every_norm, tp_index * rows_out, rows_out)
    scaling = lax.dynamic_slice_in_dim(magnitude, tp_index * rows_out, rows_out) / jnp.sqrt(
        norms_here + EPSILON
    )
    return (output_block * scaling[:, None]).astype(jnp.bfloat16)


def solution(mesh):
    placed = (
        P(None, "tp", "ctx"),
        P(None, None, "tp"),
        P(("tp", "ctx")),
        P(("tp", "ctx"), None),
        P("ctx", "tp"),
        P(None, "tp"),
        P("ctx", None),
        P(),
    )
    return jax.shard_map(
        on_device, mesh=mesh, in_specs=placed, out_specs=P("tp", "ctx"), check_vma=False
    )
```

profile of v0, /device:TPU:0, one launch (start us, length us, event | category | flops | bytes accessed | tf_op | source)
XLA Modules:
  0.0 362.2 jit_solution(11203948291518945920)
XLA Ops:
  7.4 3.8 %add_convert_fusion = bf16[512,2048]{1,0:T(8,128)(2,1)} fusion(bf16[512,2048]{1,0:T(8,128)(2,1)} %param.12, bf16[512,16]{0,1:T(8,128)(2,1)} %param.14, bf16[16,2048]{1,0:T(8,128)(2,1)S(1)} %copy-done), kind=kOutput, calls=%fused_computation.39 | convolution fusion | flops 36700160 | bytes 4276224 | tf_op jit(solution)/shard_map/dot_general | solution.py:153
  14.6 5.5 %collective-permute-start = (bf16[3,2048,6]{1,2,0:T(8,128)(2,1)S(1)}, bf16[3,2048,6]{1,2,0:T(8,128)(2,1)}, u32[]{:S(2)}, u32[]{:S(2)}) collective-permute-start(bf16[3,2048,6]{1,2,0:T(8,128)(2,1)S(1)} %copy.139), channel_id=1, source_target_pairs={{0,4},{4,8},{8,12},{12,16},{16,20},{20,24},{24,28},{1,5},{5,9},{9,... | collective-permute-start | bytes 221192 | tf_op jit(solution)/shard_map/ppermute | solution.py:19
  21.7 2.4 copy.107
  24.1 7.0 %maximum_convert_fusion = f32[3,2048,262]{2,1,0:T(8,128)} fusion(bf16[3,2048,256]{2,1,0:T(8,128)(2,1)S(1)} %copy-done.3, bf16[3,2048,6]{2,1,0:T(8,128)(2,1)} %copy.107), kind=kLoop, calls=%fused_computation.17 | loop fusion | flops 6438912 | bytes 9658368 | tf_op jit(solution)/shard_map/convert_element_type | solution.py:89
  31.1 37.8 %fusion.4 = f32[3,2048,256]{2,1,0:T(8,128)} fusion(f32[3,2048,262]{2,1,0:T(8,128)} %maximum_convert_fusion, f32[3,2048]{1,0:T(4,128)S(1)} %get-tuple-element.28, f32[3,2048]{1,0:T(4,128)S(1)} %get-tuple-element.29, f32[3,2048]{1,0:T(4,128)S(1)} %get-tuple-element.30, f32[3,2048]{1,0:T(4,128)S(1)} %get-tuple-element.31, f32[3,2048]{1,0:T(4,128)S(1)} %get-tuple-element.32, ...), kind=kLoop, calls=%fused_computation.5 | loop fusion | flops 20447232 | bytes 50503680 | tf_op jit(solution)/shard_map/add | solution.py:94
  68.8 2.5 fusion.28
  73.0 7.0 %all-to-all-start = ((bf16[128,8,2,256]{3,1,2,0:T(8,128)(2,1)}), bf16[128,8,2,256]{3,1,2,0:T(8,128)(2,1)S(1)}, u32[]{:S(2)}, u32[]{:S(2)}) async-start(bf16[128,8,2,256]{3,1,2,0:T(8,128)(2,1)} %copy.108), calls=%async_computation | async-start | bytes 2097152 | tf_op jit(solution)/shard_map/all_to_all | solution.py:126
  86.2 32.5 %all-to-all-done = bf16[128,8,2,256]{3,1,2,0:T(8,128)(2,1)S(1)} async-done(((bf16[128,8,2,256]{3,1,2,0:T(8,128)(2,1)}), bf16[128,8,2,256]{3,1,2,0:T(8,128)(2,1)S(1)}, u32[]{:S(2)}, u32[]{:S(2)}) %all-to-all-start) | async-done | bytes 1048608 | tf_op jit(solution)/shard_map/all_to_all | solution.py:126
  121.1 4.7 %reshape.91 = f32[16,8,64,64]{3,2,1,0:T(8,128)} reshape(f32[16,8,4096]{2,1,0:T(8,128)} %concatenate.61) | data formatting | bytes 4194304 | tf_op jit(solution)/shard_map/reshape | solution.py:132
  125.8 5.4 %copy.110 = f32[16,8,64,64]{2,3,1,0:T(8,128)} copy(f32[16,8,64,64]{3,2,1,0:T(8,128)} %reshape.91) | data formatting | bytes 4194304 | tf_op jit(solution)/shard_map/reshape | solution.py:132
  132.8 4.6 %reshape.92 = f32[16,8,64,64]{3,2,1,0:T(8,128)} reshape(f32[16,8,4096]{2,1,0:T(8,128)} %concatenate.62) | data formatting | bytes 4194304 | tf_op jit(solution)/shard_map/reshape | solution.py:135
  137.5 5.3 %copy.111 = f32[16,8,64,64]{2,3,1,0:T(8,128)} copy(f32[16,8,64,64]{3,2,1,0:T(8,128)} %reshape.92) | data formatting | bytes 4194304 | tf_op jit(solution)/shard_map/reshape | solution.py:135
  142.8 5.7 %fusion.25 = f32[16,8,128,64]{2,3,1,0:T(8,128)S(1)} fusion(f32[16,8,64,64]{2,3,1,0:T(8,128)} %copy.111, f32[16,8,64,64]{2,3,1,0:T(8,128)} %copy.110, f32[64,64]{1,0:T(8,128)S(1)} %get-tuple-element.27, f32[64,64]{1,0:T(8,128)S(1)} %get-tuple-element.26, f32[64,64]{1,0:T(8,128)S(1)} %fusion.56), kind=kOutput, calls=%fused_computation.41 | convolution fusion | flops 806404096 | bytes 8437760 | tf_op jit(solution)/shard_map/...ab,ac->...cb/dot_general | solution.py:45
  149.8 6.8 %fusion = f32[16,8,64,128]{3,2,1,0:T(8,128)S(1)} fusion(f32[16,8,64,64]{2,3,1,0:T(8,128)S(1)} %get-tuple-element.10, f32[16,8,64,64]{2,3,1,0:T(8,128)S(1)} %get-tuple-element.9, f32[64,64]{1,0:T(8,128)S(1)} %get-tuple-element.27, f32[64,64]{1,0:T(8,128)S(1)} %get-tuple-element.26, f32[64,64]{1,0:T(8,128)S(1)} %fusion.56), kind=kOutput, calls=%fused_computation | convolution fusion | flops 806404096 | bytes 8437760 | tf_op jit(solution)/shard_map/...b,bd->...d/dot_general | solution.py:52
  158.4 6.7 %fusion.14 = f32[16,8,64,128]{2,3,1,0:T(8,128)S(1)} fusion(f32[16,8,64,64]{3,2,1,0:T(8,128)S(1)} %get-tuple-element.8, f32[16,8,64,64]{3,2,1,0:T(8,128)S(1)} %get-tuple-element.7, f32[64,64]{1,0:T(8,128)S(1)} %get-tuple-element.27, f32[64,64]{1,0:T(8,128)S(1)} %get-tuple-element.34, f32[64,64]{1,0:T(8,128)S(1)} %get-tuple-element.35), kind=kOutput, calls=%fused_computation.24 | convolution fusion | flops 806404096 | bytes 8437760 | tf_op jit(solution)/shard_map/...b,bd->...d/dot_general | solution.py:52
  167.2 2.5 fusion.22
  169.7 4.7 %slice_multiply_fusion.8 = (f32[16,8,64,64]{2,3,1,0:T(8,128)}, f32[16,8,64,64]{2,3,1,0:T(8,128)}) fusion(f32[16,8,128,64]{2,3,1,0:T(8,128)S(1)} %fusion.22), kind=kLoop, calls=%fused_computation.19 | loop fusion | flops 1048576 | bytes 8388608 | tf_op jit(solution)/shard_map/div | solution.py:71
  174.4 5.4 %copy.122 = f32[16,8,64,64]{3,2,1,0:T(8,128)} copy(f32[16,8,64,64]{2,3,1,0:T(8,128)} %get-tuple-element.12) | data formatting | bytes 4194304 | tf_op jit(solution)/shard_map/div | solution.py:71
  179.8 4.8 %reshape.95 = f32[16,8,4096]{2,1,0:T(8,128)} reshape(f32[16,8,64,64]{3,2,1,0:T(8,128)} %copy.122) | data formatting | bytes 4194304 | tf_op jit(solution)/shard_map/reshape | solution.py:147
  184.6 5.3 %copy.121 = f32[16,8,64,64]{3,2,1,0:T(8,128)} copy(f32[16,8,64,64]{2,3,1,0:T(8,128)} %get-tuple-element.11) | data formatting | bytes 4194304 | tf_op jit(solution)/shard_map/div | solution.py:71
  189.9 4.8 %reshape.94 = f32[16,8,4096]{2,1,0:T(8,128)} reshape(f32[16,8,64,64]{3,2,1,0:T(8,128)} %copy.121) | data formatting | bytes 4194304 | tf_op jit(solution)/shard_map/reshape | solution.py:146
  197.7 8.8 %copy.124 = bf16[16,8,2,2048]{0,1,2,3:T(8,128)(2,1)} copy(bf16[16,8,2,2048]{3,1,2,0:T(8,128)(2,1)S(1)} %fusion.31) | data formatting | bytes 2097152 | tf_op jit(solution)/shard_map/convert_element_type | solution.py:150
  206.5 10.8 %reshape.107 = bf16[8,2,32768]{2,1,0:T(2,128)(2,1)S(1)} reshape(bf16[2048,2,8,16]{3,2,1,0:T(8,128)(2,1)} %bitcast.85) | data formatting | bytes 2097152
  217.3 57.5 %all_to_all.8 = bf16[8,2,32768]{2,1,0:T(2,128)(2,1)S(1)} all-to-all(bf16[8,2,32768]{2,1,0:T(2,128)(2,1)S(1)} %reshape.107), channel_id=1, replica_groups=mesh['ctx'=8,'tp'=4] {'ctx'}, dimensions={0} | all-to-all | bytes 2097152 | tf_op jit(solution)/shard_map/all_to_all | solution.py:151
  274.8 7.6 %reshape.108 = bf16[2048,2,8,16]{3,2,1,0:T(8,128)(2,1)} reshape(bf16[8,2,32768]{2,1,0:T(2,128)(2,1)S(1)} %all_to_all.8) | data formatting | bytes 2097152
  282.3 9.1 %copy.125 = bf16[16,8,2,2048]{3,1,2,0:T(8,128)(2,1)S(1)} copy(bf16[16,8,2,2048]{0,1,2,3:T(8,128)(2,1)} %bitcast.86) | data formatting | bytes 2097152 | tf_op jit(solution)/shard_map/all_to_all | solution.py:151
  293.4 2.5 reshape.97
  295.8 13.6 %fusion.32 = f32[4096,256]{1,0:T(8,128)} fusion(bf16[4096,2048]{1,0:T(8,128)(2,1)} %all-gather.3.cloned.1.call-done, f32[2048,256]{1,0:T(8,128)} %reshape.97, f32[3,2048,256]{2,1,0:T(8,128)} %fusion.4), kind=kOutput, calls=%fused_computation.50 | convolution fusion | flops 4296015872 | bytes 25165824 | tf_op jit(solution)/shard_map/dot_general | solution.py:163
  311.5 5.7 %psum.7 = f32[512]{0:T(512)S(1)} all-reduce(f32[512]{0:T(512)S(1)} %multiply_reduce_fusion), channel_id=1, replica_groups=mesh['ctx'=8,'tp'=4] {'tp'}, use_global_device_ids=true, to_apply=%region_2.3 | all-reduce | flops 512 | bytes 4096 | tf_op jit(solution)/shard_map/psum | solution.py:161
  317.1 26.0 %all-gather = f32[8,1,512]{2,1,0:T(1,128)S(1)} all-gather(f32[1,1,512]{2,1,0:T(1,128)S(1)} %bitcast.95), channel_id=1, replica_groups=mesh['ctx'=8,'tp'=4] {'ctx'}, dimensions={0}, use_global_device_ids=true | all-gather | bytes 18432 | tf_op jit(solution)/shard_map/all_gather | solution.py:162
  343.8 8.9 %reduce-scatter.2.cloned.1.call-done = f32[1024,256]{1,0:T(8,128)} async-done(((f32[4096,256]{1,0:T(8,128)}), f32[1024,256]{1,0:T(8,128)}) %reduce-scatter.2.cloned.1.call-update) | async-done | bytes 1048592 | tf_op jit(solution)/shard_map/reduce_scatter | solution.py:168
  352.7 2.2 multiply_convert_fusion
  (65 shorter events, 30.1 us)
Async XLA Ops:
  6.5 0.8 copy-start
  6.5 4.7 %copy-start.3 = (bf16[3,2048,256]{2,1,0:T(8,128)(2,1)S(1)}, bf16[3,2048,256]{2,1,0:T(8,128)(2,1)}, u32[]{:S(2)}) copy-start(bf16[3,2048,256]{2,1,0:T(8,128)(2,1)} %param.8) | copy-start | bytes 9437188
  6.5 289.3 %all-gather.3.cloned.1.call-start = ((), (), s32[]{:S(2)}) async-start(), calls=%async_computation.3 | async-start | bytes 18874368 | tf_op jit(solution)/shard_map/all_gather | solution.py:164
  11.2 8.9 %copy-start.6 = (f32[3,7,2048]{2,1,0:T(8,128)S(1)}, f32[3,7,2048]{2,1,0:T(8,128)}, u32[]{:S(2)}) copy-start(f32[3,7,2048]{2,1,0:T(8,128)} %param.9) | copy-start | bytes 516100
  14.6 7.0 %collective-permute-start = (bf16[3,2048,6]{1,2,0:T(8,128)(2,1)S(1)}, bf16[3,2048,6]{1,2,0:T(8,128)(2,1)}, u32[]{:S(2)}, u32[]{:S(2)}) collective-permute-start(bf16[3,2048,6]{1,2,0:T(8,128)(2,1)S(1)} %copy.139), channel_id=1, source_target_pairs={{0,4},{4,8},{8,12},{12,16},{16,20},{20,24},{24,28},{1,5},{5,9},{9,... | collective-permute-start | bytes 221192 | tf_op jit(solution)/shard_map/ppermute | solution.py:19
  71.3 9.6 %copy-start.7 = (f32[16,2048]{1,0:T(8,128)S(1)}, f32[16,2048]{1,0:T(8,128)}, u32[]{:S(2)}) copy-start(f32[16,2048]{1,0:T(8,128)} %param.11) | copy-start | bytes 393220
  71.8 9.7 %copy-start.8 = (f32[256]{0:T(256)S(1)}, f32[256]{0:T(256)}, u32[]{:S(2)}) copy-start(f32[256]{0:T(256)} %param.10) | copy-start | bytes 3076
  73.0 45.7 %all-to-all-start = ((bf16[128,8,2,256]{3,1,2,0:T(8,128)(2,1)}), bf16[128,8,2,256]{3,1,2,0:T(8,128)(2,1)S(1)}, u32[]{:S(2)}, u32[]{:S(2)}) async-start(bf16[128,8,2,256]{3,1,2,0:T(8,128)(2,1)} %copy.108), calls=%async_computation | async-start | bytes 2097152 | tf_op jit(solution)/shard_map/all_to_all | solution.py:126
  80.0 272.7 %reduce-scatter.2.cloned.1.call-start = ((), (), s32[]{:S(2)}) async-start(), calls=%async_computation.4 | async-start | bytes 5242880 | tf_op jit(solution)/shard_map/reduce_scatter | solution.py:168
  149.8 6.8 %copy-start.4 = (f32[16,64,64]{2,1,0:T(8,128)S(1)}, f32[16,64,64]{2,1,0:T(8,128)}, u32[]{:S(2)}) copy-start(f32[16,64,64]{2,1,0:T(8,128)} %get-tuple-element.17) | copy-start | bytes 786436
  149.8 6.8 %copy-start.5 = (f32[16,64,64]{2,1,0:T(8,128)S(1)}, f32[16,64,64]{2,1,0:T(8,128)}, u32[]{:S(2)}) copy-start(f32[16,64,64]{2,1,0:T(8,128)} %get-tuple-element.18) | copy-start | bytes 786436
  295.8 59.1 %copy-start.1 = (bf16[16,2048]{1,0:T(8,128)(2,1)S(1)}, bf16[16,2048]{1,0:T(8,128)(2,1)}, u32[]{:S(2)}) copy-start(bf16[16,2048]{1,0:T(8,128)(2,1)} %param.13) | copy-start | bytes 196612
  309.4 1.6 copy-start.2
Sparse Core Ops, SparseCore 0:
  11.3 271.2 all-gather.2
  309.5 43.1 reduce-scatter.1
where the time goes:
time: 369 us; the launch traced here: 362 us
  local copies, waits for them, and re-layouts  99.3 us (27%)
  blocking collectives  89.1 us (24%)
  other arithmetic  62.3 us (17%)
  waiting for transfers between devices  42.8 us (12%)
  matrix products  41.4 us (11%)
  between operations  14.2 us (4%)
  starting transfers between devices  13 us (4%)
    all_to_all x1, blocking collectives, on_device(): lax.all_to_all(summed, 'ctx', split_axis=3, concat_axis=0, tiled=True)  57.5 us
    add x1, other arithmetic, on_device(): featured + featurizer_weights[:, offset, :, None] * extended[:, :, starti...  37.8 us
    all_to_all x1, waiting for transfers between devices, on_device(): lax.all_to_all(mixture_blocks, 'ctx', split_axis=0, concat_axis=3, tiled=...  32.5 us
    all_gather x1, blocking collectives, on_device(): every_norm = lax.all_gather(complete, 'ctx', axis=0, tiled=True)  26 us
    unnamed x25, local copies, waits for them, and re-layouts  22.6 us
    dot_general x3, matrix products, along_last(): result = jnp.einsum('...b,bd->...d', stacked, matrix, precision=accuracy)  15.3 us
    dot_general x1, matrix products, on_device(): jnp.dot(lax.all_gather(merged, 'ctx', axis=0, tiled=True), gating, prefer...  13.6 us
    div x2, local copies, waits for them, and re-layouts, inverse_transform(): return (out_real / total, out_imag / total)  10.7 us
  transfers between devices with their start and end apart: 4, of which 3 were waited for; matrix products, arithmetic and copies ran while one was open for 50% of the time, Pallas kernels for 0%

commit v1 on v0

v1 whole, which is shorter than its diff:
```python
import functools

import jax
import jax.numpy as jnp
from jax import lax
from jax.experimental import pallas as pl
from jax.experimental.pallas import tpu as pltpu
from jax.sharding import PartitionSpec as P

GROUP = 16
TAPS = 7
EPSILON = 1e-06
MIB = 1 << 20
BF16 = jnp.bfloat16
F32 = jnp.float32


def exchange(block, axis, distance):
    count = lax.axis_size(axis)
    return lax.ppermute(block, axis, [(i, i ^ distance) for i in range(count)])


def whole_spec(shape):
    return pl.BlockSpec(shape, lambda *_: (0,) * len(shape))


def featurize_kernel(first, count, where_ref, input_ref, taps_ref, halo_ref, *refs):
    out_refs, (taps_turned, halo_turned) = refs[:-2], refs[-2:]
    step = pl.program_id(0)
    block, tokens = input_ref.shape[1:]
    lanes = taps_ref.shape[2]
    taps_turned[...] = jnp.concatenate(
        [taps_ref[i, j : j + 1, :] for i in range(3) for j in range(TAPS)]
        + [jnp.zeros((128 - 3 * TAPS, lanes), F32)],
        axis=0,
    ).T
    halo_rows = halo_ref[...].astype(F32)
    halo_turned[...] = jnp.concatenate(
        [halo_rows, jnp.zeros((128 - halo_rows.shape[0], lanes), F32)], axis=0
    ).T
    dest = jnp.bitwise_xor(step + first, where_ref[0])
    here = pl.ds(pl.multiple_of(lax.rem(dest * block, lanes), block), block)
    taps, halo = taps_turned[here, :], halo_turned[here, :]
    lane = lax.broadcasted_iota(jnp.int32, (block, 128), 1)
    features = []
    for i in range(3):
        values = input_ref[i].astype(F32)
        before = pltpu.roll(halo, (128 - (TAPS - 1) - (TAPS - 1) * i) % 128, 1)
        tiles = [before] + [values[:, s : s + 128] for s in range(0, tokens, 128)]
        sums = [tiles[n + 1] * taps[:, i * TAPS : i * TAPS + 1] for n in range(tokens // 128)]
        for j in range(1, TAPS):
            turned = [pltpu.roll(tile, j, 1) for tile in tiles]
            weight = taps[:, i * TAPS + j : i * TAPS + j + 1]
            for n in range(tokens // 128):
                sums[n] = sums[n] + weight * jnp.where(lane < j, turned[n], turned[n + 1])
        features.append(jnp.concatenate(sums, axis=1))
    mixture = (features[1] * features[2]).astype(BF16)
    query = features[0].astype(BF16)
    for n in range(count):

        @pl.when(step == n)
        def _():
            out_refs[n][...] = mixture
            out_refs[count + n][...] = query


def featurize(where, values, taps, halo, ctx_count, first, count):
    width, tokens = values.shape[1:]
    block = width // ctx_count
    lanes = max(block, 128)
    shape = jax.ShapeDtypeStruct((block, tokens), BF16)

    def rows(step, where_ref):
        return jnp.bitwise_xor(step + first, where_ref[0])

    def lanes_of(step, where_ref):
        return rows(step, where_ref) * block // lanes

    outs = pl.pallas_call(
        functools.partial(featurize_kernel, first, count),
        grid_spec=pltpu.PrefetchScalarGridSpec(
            num_scalar_prefetch=1,
            grid=(count,),
            in_specs=[
                pl.BlockSpec((3, block, tokens), lambda s, w: (0, rows(s, w), 0)),
                pl.BlockSpec((3, TAPS, lanes), lambda s, w: (0, 0, lanes_of(s, w))),
                pl.BlockSpec((halo.shape[0], lanes), lambda s, w: (0, lanes_of(s, w))),
            ],
            out_specs=[whole_spec(shape.shape)] * (2 * count),
            scratch_shapes=[pltpu.VMEM((lanes, 128), F32)] * 2,
        ),
        out_shape=[shape] * (2 * count),
        compiler_params=pltpu.CompilerParams(vmem_limit_bytes=32 * MIB),
        name="featurize",
    )(where, values, taps, halo)
    return outs[:count], outs[count:]


def convolve_kernel(ctx_count, where_ref, filters_ref, skip_ref, *refs):
    mixture_refs, out_refs = refs[:ctx_count], refs[ctx_count : 2 * ctx_count]
    left_ref, total_ref = refs[2 * ctx_count :]
    group = pl.program_id(0)
    me = where_ref[0]
    tokens = mixture_refs[0].shape[1]

    def rows_of(k):
        return pl.ds(pl.multiple_of(jnp.bitwise_xor(me, k) * GROUP, GROUP), GROUP)

    for k in range(ctx_count):
        left_ref[rows_of(k), :] = mixture_refs[k][...]
    total_ref[...] = jnp.zeros_like(total_ref)

    def add_lags(d, rows, taps):
        spread = jnp.broadcast_to(taps, (tokens, 2 * tokens))
        turned = pltpu.roll(spread, 0, 1, stride=1, stride_axis=0)[:, tokens:]
        product = jnp.dot(left_ref[:rows, :], turned.astype(BF16), preferred_element_type=F32)
        place = pl.ds(d * GROUP, rows)
        total_ref[place, :] = total_ref[place, :] + product

    zeros = jnp.zeros((1, tokens), F32)
    here = pl.ds(group, 1)
    first = jnp.concatenate([zeros, filters_ref[here, :tokens]], axis=1)
    add_lags(0, ctx_count * GROUP, first)
    if ctx_count <= 8:
        for d in range(1, ctx_count):
            lags = filters_ref[here, (d - 1) * tokens : (d + 1) * tokens]
            add_lags(d, (ctx_count - d) * GROUP, lags)
    else:

        @pl.loop(1, ctx_count)
        def _(d):
            start = pl.multiple_of((d - 1) * tokens, tokens)
            add_lags(d, ctx_count * GROUP, filters_ref[here, pl.ds(start, 2 * tokens)])

    skip = skip_ref[...]
    skip = jnp.concatenate([skip] * (tokens // 128), axis=1)
    for k in range(ctx_count):
        wide = mixture_refs[k][...].astype(F32)
        out_refs[k][...] = (total_ref[rows_of(k), :] + skip * wide).astype(BF16)


def convolve(where, filters, skip, mixtures):
    ctx_count = len(mixtures)
    block, tokens = mixtures[0].shape
    groups = filters.shape[0]
    total_rows = ctx_count * GROUP * (1 if ctx_count <= 8 else 2)
    rows = pl.BlockSpec((GROUP, tokens), lambda g, w: (g, 0))
    return pl.pallas_call(
        functools.partial(convolve_kernel, ctx_count),
        grid_spec=pltpu.PrefetchScalarGridSpec(
            num_scalar_prefetch=1,
            grid=(groups,),
            in_specs=[
                whole_spec(filters.shape),
                pl.BlockSpec((GROUP, 128), lambda g, w: (g, 0)),
            ]
            + [rows] * ctx_count,
            out_specs=[rows] * ctx_count,
            scratch_shapes=[
                pltpu.VMEM((ctx_count * GROUP, tokens), BF16),
                pltpu.VMEM((total_rows, tokens), F32),
            ],
        ),
        out_shape=[jax.ShapeDtypeStruct((block, tokens), BF16)] * ctx_count,
        compiler_params=pltpu.CompilerParams(vmem_limit_bytes=40 * MIB),
        name="convolve",
    )(where, filters, skip, *mixtures)


def gate_kernel(half, where_ref, query_ref, far_query_ref, summed_ref, far_summed_ref, out_ref):
    tokens = query_ref.shape[1]
    upper = (where_ref[0] >= half).astype(jnp.int32)
    near = query_ref[...].astype(F32) * summed_ref[...].astype(F32)
    far = far_query_ref[...].astype(F32) * far_summed_ref[...].astype(F32)
    near_place = pl.ds(pl.multiple_of(upper * tokens, tokens), tokens)
    far_place = pl.ds(pl.multiple_of((1 - upper) * tokens, tokens), tokens)
    out_ref[:, near_place] = near.astype(BF16)
    out_ref[:, far_place] = far.astype(BF16)


def gate(where, half, query, far_query, summed, far_summed):
    block, tokens = query.shape
    return pl.pallas_call(
        functools.partial(gate_kernel, half),
        grid_spec=pltpu.PrefetchScalarGridSpec(
            num_scalar_prefetch=1,
            grid=(1,),
            in_specs=[whole_spec((block, tokens))] * 4,
            out_specs=whole_spec((block, 2 * tokens)),
        ),
        out_shape=jax.ShapeDtypeStruct((block, 2 * tokens), BF16),
        compiler_params=pltpu.CompilerParams(vmem_limit_bytes=16 * MIB),
        name="gate",
    )(where, query, far_query, summed, far_summed)


def project_kernel(pieces, chunks, where_ref, *refs):
    weight_refs, gating_refs = refs[:pieces], refs[pieces : pieces + chunks]
    keep_ref, send_ref, gating_ref = refs[pieces + chunks :]
    me, low, core = where_ref[0], where_ref[1], where_ref[2]
    rows, width = weight_refs[0].shape
    block = width // chunks
    tile = min(rows, 256)
    for k in range(chunks):
        place = pl.ds(pl.multiple_of(jnp.bitwise_xor(me, k) * block, block), block)
        gating_ref[place, :] = gating_refs[k][...]
    for p in range(pieces):
        place = jnp.bitwise_xor(low, p)
        mine = (place >= pieces // 2).astype(jnp.int32) == core
        within = jnp.bitwise_and(place, pieces // 2 - 1) * rows

        @pl.loop(0, rows // tile)
        def _(r):
            start = pl.multiple_of(r * tile, tile)
            total = jnp.dot(
                weight_refs[p][pl.ds(start, tile), :],
                gating_ref[...],
                preferred_element_type=F32,
            )
            target = pl.ds(pl.multiple_of(within + start, tile), tile)

            @pl.when(mine)
            def _():
                keep_ref[target, :] = total

            @pl.when(jnp.logical_not(mine))
            def _():
                send_ref[target, :] = total


def project(where, weights, gatings):
    rows = weights[0].shape[0]
    tokens = gatings[0].shape[1]
    pieces = len(weights)
    out = jax.ShapeDtypeStruct((pieces // 2 * rows, tokens), F32)
    return pl.pallas_call(
        functools.partial(project_kernel, pieces, len(gatings)),
        grid_spec=pltpu.PrefetchScalarGridSpec(
            num_scalar_prefetch=1,
            grid=(1,),
            in_specs=[whole_spec(a.shape) for a in (*weights, *gatings)],
            out_specs=[whole_spec(out.shape)] * 2,
            scratch_shapes=[pltpu.VMEM((weights[0].shape[1], tokens), BF16)],
        ),
        out_shape=[out] * 2,
        compiler_params=pltpu.CompilerParams(vmem_limit_bytes=56 * MIB),
        name="project",
    )(where, *weights, *gatings)


def on_device(
    query_key_value_input,
    featurizer_weights,
    channel_skip_scale,
    group_long_filters,
    frozen_weight,
    down_update_weight,
    up_update_weight,
    magnitude,
):
    width, tokens = query_key_value_input.shape[1:]
    ctx_count = lax.axis_size("ctx")
    tp_count = lax.axis_size("tp")
    half = ctx_count // 2
    rows = frozen_weight.shape[0]
    me = lax.axis_index("ctx")
    tp_index = lax.axis_index("tp")
    low = jnp.bitwise_and(me, half - 1)
    high = me // half
    core = jnp.bitwise_and(tp_index, 1)
    upper_tp = tp_index // 2
    where = jnp.stack([me, low, core]).astype(jnp.int32)

    halo = jnp.swapaxes(query_key_value_input[:, :, tokens - (TAPS - 1) :], 1, 2)
    halo = halo.reshape(3 * (TAPS - 1), width)
    halo = lax.ppermute(halo, "ctx", [(i, i + 1) for i in range(ctx_count - 1)])

    update = jnp.dot(up_update_weight, down_update_weight, preferred_element_type=F32)
    merged = (frozen_weight.astype(F32) + update).astype(BF16)
    weights = [merged]
    norms = jnp.sum(jnp.square(lax.optimization_barrier(merged).astype(F32)), axis=1)[None, :]
    for distance in (1, 2):
        norms = norms + exchange(norms, "tp", distance)
    norms = [norms]
    distance = half // 2
    while distance:
        weights = weights + [exchange(piece, "ctx", distance) for piece in weights]
        norms = norms + [exchange(piece, "ctx", distance) for piece in norms]
        distance //= 2
    order = [0]
    distance = half // 2
    while distance:
        order = order + [index + distance for index in order]
        distance //= 2
    weights = [weights[order.index(p)] for p in range(half)]
    norms = [norms[order.index(p)] for p in range(half)]

    mixtures, queries = [], []
    for first in (0, half):
        some_mixtures, some_queries = featurize(
            where, query_key_value_input, featurizer_weights, halo, ctx_count, first, half
        )
        mixtures += some_mixtures
        queries += some_queries
    mixtures = mixtures[:1] + [exchange(mixtures[k], "ctx", k) for k in range(1, ctx_count)]
    queries = queries[:1] + [exchange(queries[k], "ctx", k) for k in range(1, ctx_count)]

    block = width // ctx_count
    skip = jnp.broadcast_to(channel_skip_scale[:, None], (block, 128))
    summed = convolve(where, group_long_filters, skip, mixtures)
    gatings = [
        gate(where, half, queries[m], queries[m + half], summed[m], summed[m + half])
        for m in range(half)
    ]
    gatings = [gatings[0]] + [
        exchange(gatings[k % half], "ctx", k) for k in range(1, ctx_count)
    ]
    keep, send = project(where, weights, gatings)
    partial = keep + exchange(send, "tp", 1)

    stacked = jnp.stack(norms).reshape(half, rows)
    stacked = stacked[jnp.bitwise_xor(jnp.arange(half), low)].reshape(half * rows)
    owned = half * rows // 2
    norms_here = lax.dynamic_slice_in_dim(stacked, core * owned, owned)
    magnitude_here = lax.dynamic_slice_in_dim(magnitude, (high * 2 + core) * owned, owned)
    scaling = magnitude_here / jnp.sqrt(norms_here + EPSILON)
    scaled = partial * scaling[:, None]
    near = lax.dynamic_slice_in_dim(scaled, high * tokens, tokens, axis=1)
    far = lax.dynamic_slice_in_dim(scaled, (1 - high) * tokens, tokens, axis=1)

    def place(h, l, y, c):
        return (h * half + l) * tp_count + y * 2 + c

    sites = [(h, l, c) for h in range(2) for l in range(half) for c in range(2)]
    both = ("ctx", "tp")
    from_near = lax.ppermute(
        near.astype(BF16),
        both,
        [(place(h, l, 1 - h, c), place(h, l, h, c)) for h, l, c in sites],
    )
    from_far = lax.ppermute(
        far.astype(BF16),
        both,
        [(place(h, l, h, c), place(1 - h, l, h, c)) for h, l, c in sites],
    )
    from_diagonal = lax.ppermute(
        far.astype(BF16),
        both,
        [(place(h, l, 1 - h, c), place(1 - h, l, h, c)) for h, l, c in sites],
    )
    own = jnp.where(upper_tp == high, near, from_far.astype(F32))
    other = jnp.where(upper_tp == high, from_near, from_diagonal).astype(F32)
    return (own + other).astype(BF16)


def solution(mesh):
    placed = (
        P(None, "tp", "ctx"),
        P(None, None, "tp"),
        P(("tp", "ctx")),
        P(("tp", "ctx"), None),
        P("ctx", "tp"),
        P(None, "tp"),
        P("ctx", None),
        P(),
    )
    return jax.shard_map(
        on_device, mesh=mesh, in_specs=placed, out_specs=P("tp", "ctx"), check_vma=False
    )
```

time: 369 us -> 303 us (0.82)
  the two profiles are of different devices: /device:TPU:0 before, /device:TPU:7 now
where the time goes in v1:
time: 303 us; the launch traced here: 302 us
  waiting for transfers between devices  141 us (47%)
  starting transfers between devices  93.6 us (31%)
  Pallas kernels  46.8 us (15%)
  local copies, waits for them, and re-layouts  8.68 us (3%)
  other arithmetic  7.45 us (2%)
  matrix products  3.81 us (1%)
    ppermute x30, starting transfers between devices, exchange(): return lax.ppermute(block, axis, [(i, i ^ distance) for i in range(count)])  79.4 us
    ppermute x30, waiting for transfers between devices, exchange(): return lax.ppermute(block, axis, [(i, i ^ distance) for i in range(count)])  78.4 us
    ppermute x1, waiting for transfers between devices, on_device(): halo = lax.ppermute(halo, 'ctx', [(i, i + 1) for i in range(ctx_count - 1)])  39.5 us
    pallas_call x2, Pallas kernels, featurize(): pl.pallas_call(functools.partial(featurize_kernel, first, count), grid_sp...  23.3 us
    ppermute x1, waiting for transfers between devices, on_device(): lax.ppermute(far.astype(BF16), both, [(place(h, l, h, c), place(1 - h, l,...  16.6 us
    pallas_call x1, Pallas kernels, project(): pl.pallas_call(functools.partial(project_kernel, pieces, len(gatings)), g...  12.7 us
    pallas_call x1, Pallas kernels, convolve(): pl.pallas_call(functools.partial(convolve_kernel, ctx_count), grid_spec=p...  8.46 us
    ppermute x1, waiting for transfers between devices, on_device(): lax.ppermute(far.astype(BF16), both, [(place(h, l, 1 - h, c), place(1 - h...  6.77 us
  transfers between devices with their start and end apart: 34, of which 16 were waited for; matrix products, arithmetic and copies ran while one was open for 3% of the time, Pallas kernels for 11%

profile of v1, /device:TPU:7, one launch (start us, length us, event | category | flops | bytes accessed | tf_op | source)
XLA Modules:
  0.0 301.9 jit_solution(15327057578222828167)
XLA Ops:
  0.8 3.8 %add_convert_fusion.refs_0_ = bf16[512,2048]{1,0:T(8,128)(2,1)} fusion(bf16[512,2048]{1,0:T(8,128)(2,1)} %param.12, bf16[512,16]{0,1:T(8,128)(2,1)} %param.14, bf16[16,2048]{1,0:T(8,128)(2,1)S(1)} %copy-done), kind=kOutput, calls=%fused_computation.2 | convolution fusion | flops 36700160 | bytes 4276224 | tf_op jit(solution)/shard_map/dot_general | solution.py:278
  6.2 45.3 %collective-permute-done.1.refs_2_ = bf16[512,2048]{1,0:T(8,128)(2,1)} collective-permute-done((bf16[512,2048]{1,0:T(8,128)(2,1)}, bf16[512,2048]{1,0:T(8,128)(2,1)}, u32[]{:S(2)}, u32[]{:S(2)}) %collective-permute-start.1) | collective-permute-done | bytes 2097184 | tf_op jit(solution)/shard_map/ppermute | solution.py:20
  55.8 4.1 %collective-permute-start.3 = (bf16[18,2048]{1,0:T(8,128)(2,1)}, bf16[18,2048]{1,0:T(8,128)(2,1)S(1)}, u32[]{:S(2)}, u32[]{:S(2)}) collective-permute-start(bf16[18,2048]{1,0:T(8,128)(2,1)} %reshape.27), channel_id=1, source_target_pairs={{0,4},{4,8},{8,12},{12,16},{16,20},{20,24},{24,28},{1,5},{5,9},{9,... | collective-permute-start | bytes 221192 | tf_op jit(solution)/shard_map/ppermute | solution.py:276
  60.0 39.5 %collective-permute-done.3.halo_ref = bf16[18,2048]{1,0:T(8,128)(2,1)S(1)} collective-permute-done((bf16[18,2048]{1,0:T(8,128)(2,1)}, bf16[18,2048]{1,0:T(8,128)(2,1)S(1)}, u32[]{:S(2)}, u32[]{:S(2)}) %collective-permute-start.3) | collective-permute-done | bytes 73760 | tf_op jit(solution)/shard_map/ppermute | solution.py:276
  99.5 11.6 %featurize.2 = (bf16[256,256]{1,0:T(8,128)(2,1)S(1)}, bf16[256,256]{1,0:T(8,128)(2,1)S(1)}, bf16[256,256]{1,0:T(8,128)(2,1)S(1)}, bf16[256,256]{1,0:T(8,128)(2,1...) custom-call(s32[3]{0:T(128)S(1)} %pad_add_fusion.where_ref, ...), custom_call_target="tpu_custom_call" | custom-call | tf_op jit(solution)/shard_map/featurize/pallas_call | solution.py:79
  113.9 11.7 %featurize.3 = (bf16[256,256]{1,0:T(8,128)(2,1)S(1)}, bf16[256,256]{1,0:T(8,128)(2,1)S(1)}, bf16[256,256]{1,0:T(8,128)(2,1)S(1)}, bf16[256,256]{1,0:T(8,128)(2,1...) custom-call(s32[3]{0:T(128)S(1)} %pad_add_fusion.where_ref, ...), custom_call_target="tpu_custom_call" | custom-call | tf_op jit(solution)/shard_map/featurize/pallas_call | solution.py:79
  125.5 2.4 collective-permute-start.8
  127.9 3.2 %collective-permute-start.10 = (bf16[256,256]{1,0:T(8,128)(2,1)S(1)}, bf16[256,256]{1,0:T(8,128)(2,1)S(1)}, u32[]{:S(2)}, u32[]{:S(2)}) collective-permute-start(bf16[256,256]{1,0:T(8,128)(2,1)S(1)} %get-tuple-element.39), channel_id=1, source_target_pairs={{0,24},{4,28},{8,16},{12,20},{16,8},{20,12},{24,0},{28,4},{1,25},{... | collective-permute-start | bytes 393224 | tf_op jit(solution)/shard_map/ppermute | solution.py:20
  131.7 11.1 %collective-permute-start.11 = (bf16[256,256]{1,0:T(8,128)(2,1)S(1)}, bf16[256,256]{1,0:T(8,128)(2,1)S(1)}, u32[]{:S(2)}, u32[]{:S(2)}) collective-permute-start(bf16[256,256]{1,0:T(8,128)(2,1)S(1)} %get-tuple-element.40), channel_id=1, source_target_pairs={{0,28},{4,24},{8,20},{12,16},{16,12},{20,8},{24,4},{28,0},{1,29},{... | collective-permute-start | bytes 393224 | tf_op jit(solution)/shard_map/ppermute | solution.py:20
  144.4 3.1 %collective-permute-start.13 = (bf16[256,256]{1,0:T(8,128)(2,1)S(1)}, bf16[256,256]{1,0:T(8,128)(2,1)S(1)}, u32[]{:S(2)}, u32[]{:S(2)}) collective-permute-start(bf16[256,256]{1,0:T(8,128)(2,1)S(1)} %get-tuple-element.44), channel_id=1, source_target_pairs={{0,20},{4,16},{8,28},{12,24},{16,4},{20,0},{24,12},{28,8},{1,21},{... | collective-permute-start | bytes 393224 | tf_op jit(solution)/shard_map/ppermute | solution.py:20
  147.5 5.5 %collective-permute-start.15 = (bf16[256,256]{1,0:T(8,128)(2,1)S(1)}, bf16[256,256]{1,0:T(8,128)(2,1)S(1)}, u32[]{:S(2)}, u32[]{:S(2)}) collective-permute-start(bf16[256,256]{1,0:T(8,128)(2,1)S(1)} %get-tuple-element.47), channel_id=1, source_target_pairs={{0,8},{4,12},{8,0},{12,4},{16,24},{20,28},{24,16},{28,20},{1,9},{5... | collective-permute-start | bytes 393224 | tf_op jit(solution)/shard_map/ppermute | solution.py:20
  156.3 8.5 %convolve.1 = (bf16[256,256]{1,0:T(8,128)(2,1)S(1)}, bf16[256,256]{1,0:T(8,128)(2,1)S(1)}, bf16[256,256]{1,0:T(8,128)(2,1)S(1)}, bf16[256,256]{1,0:T(8,128)(2,1)...) custom-call(s32[3]{0:T(128)S(1)} %pad_add_fusion.where_ref, ...), custom_call_target="tpu_custom_call" | custom-call | tf_op jit(solution)/shard_map/convolve/pallas_call | solution.py:148
  165.4 2.2 collective-permute-start.14
  167.6 3.7 %collective-permute-start.19 = (bf16[256,256]{1,0:T(8,128)(2,1)S(1)}, bf16[256,256]{1,0:T(8,128)(2,1)S(1)}, u32[]{:S(2)}, u32[]{:S(2)}) collective-permute-start(bf16[256,256]{1,0:T(8,128)(2,1)S(1)} %get-tuple-element.52), channel_id=1, source_target_pairs={{0,28},{4,24},{8,20},{12,16},{16,12},{20,8},{24,4},{28,0},{1,29},{... | collective-permute-start | bytes 393224 | tf_op jit(solution)/shard_map/ppermute | solution.py:20
  172.2 2.0 collective-permute-done.19.far_query_ref
  174.2 7.1 %collective-permute-start.17 = (bf16[256,512]{1,0:T(8,128)(2,1)S(1)}, bf16[256,512]{1,0:T(8,128)(2,1)S(1)}, u32[]{:S(2)}, u32[]{:S(2)}) collective-permute-start(bf16[256,512]{1,0:T(8,128)(2,1)S(1)} %gate.6), channel_id=1, source_target_pairs={{0,8},{4,12},{8,0},{12,4},{16,24},{20,28},{24,16},{28,20},{1,9},{5... | collective-permute-start | bytes 786440 | tf_op jit(solution)/shard_map/ppermute | solution.py:20
  184.1 3.2 %collective-permute-start.21 = (bf16[256,512]{1,0:T(8,128)(2,1)S(1)}, bf16[256,512]{1,0:T(8,128)(2,1)S(1)}, u32[]{:S(2)}, u32[]{:S(2)}) collective-permute-start(bf16[256,512]{1,0:T(8,128)(2,1)S(1)} %gate.4.refs_4_), channel_id=1, source_target_pairs={{0,16},{4,20},{8,24},{12,28},{16,0},{20,4},{24,8},{28,12},{1,17},{... | collective-permute-start | bytes 786440 | tf_op jit(solution)/shard_map/ppermute | solution.py:20
  188.4 8.1 %collective-permute-start.22 = (bf16[256,512]{1,0:T(8,128)(2,1)S(1)}, bf16[256,512]{1,0:T(8,128)(2,1)S(1)}, u32[]{:S(2)}, u32[]{:S(2)}) collective-permute-start(bf16[256,512]{1,0:T(8,128)(2,1)S(1)} %gate.5), channel_id=1, source_target_pairs={{0,20},{4,16},{8,28},{12,24},{16,4},{20,0},{24,12},{28,8},{1,21},{... | collective-permute-start | bytes 786440 | tf_op jit(solution)/shard_map/ppermute | solution.py:20
  196.5 2.9 collective-permute-done.20.refs_7_
  199.4 4.7 %collective-permute-start.23 = (bf16[256,512]{1,0:T(8,128)(2,1)S(1)}, bf16[256,512]{1,0:T(8,128)(2,1)S(1)}, u32[]{:S(2)}, u32[]{:S(2)}) collective-permute-start(bf16[256,512]{1,0:T(8,128)(2,1)S(1)} %gate.6), channel_id=1, source_target_pairs={{0,24},{4,28},{8,16},{12,20},{16,8},{20,12},{24,0},{28,4},{1,25},{... | collective-permute-start | bytes 786440 | tf_op jit(solution)/shard_map/ppermute | solution.py:20
  204.1 1.8 collective-permute-start.24
  206.0 18.6 %collective-permute-done.22.refs_9_ = bf16[256,512]{1,0:T(8,128)(2,1)S(1)} collective-permute-done((bf16[256,512]{1,0:T(8,128)(2,1)S(1)}, bf16[256,512]{1,0:T(8,128)(2,1)S(1)}, u32[]{:S(2)}, u32[]{:S(2)}) %collective-permute-start.22) | collective-permute-done | bytes 262176 | tf_op jit(solution)/shard_map/ppermute | solution.py:20
  225.5 12.7 %project.1 = (f32[1024,512]{1,0:T(8,128)}, f32[1024,512]{1,0:T(8,128)}) custom-call(s32[3]{0:T(128)} %copy-done.5, bf16[512,2048]{1,0:T(8,128)(2,1)} %add_convert_fusion.refs_0_, bf16[512,2048]{1,0:T(8,128)(2,1)} %collective-permute-done.refs_1_, bf16[512,2048]{1,0:T(8,128)(2,1)} %collective-permute-done.1.refs_2_, ...), custom_call_target="tpu_custom_call" | custom-call | tf_op jit(solution)/shard_map/project/pallas_call | solution.py:236
  239.9 2.1 multiply_reduce_fusion
  244.0 2.2 collective-permute-done.27
  246.2 10.6 %collective-permute-start.29 = (f32[1,512]{1,0:T(1,128)S(1)}, f32[1,512]{1,0:T(1,128)S(1)}, u32[]{:S(2)}, u32[]{:S(2)}) collective-permute-start(f32[1,512]{1,0:T(1,128)S(1)} %add.53), channel_id=1, source_target_pairs={{0,8},{4,12},{8,0},{12,4},{16,24},{20,28},{24,16},{28,20},{1,9},{5... | collective-permute-start | bytes 6152 | tf_op jit(solution)/shard_map/ppermute | solution.py:20
  262.9 2.5 add_multiply_fusion
  267.6 4.1 %collective-permute-start.32 = (bf16[1024,256]{1,0:T(8,128)(2,1)}, bf16[1024,256]{1,0:T(8,128)(2,1)}, u32[]{:S(2)}, u32[]{:S(2)}) collective-permute-start(bf16[1024,256]{1,0:T(8,128)(2,1)} %get-tuple-element.57), channel_id=1, source_target_pairs={{2,0},{3,1},{6,4},{7,5},{10,8},{11,9},{14,12},{15,13},{16,18},{17,... | collective-permute-start | bytes 1572872 | tf_op jit(solution)/shard_map/ppermute | solution.py:336
  271.7 4.7 %collective-permute-start.33 = (bf16[1024,256]{1,0:T(8,128)(2,1)S(1)}, bf16[1024,256]{1,0:T(8,128)(2,1)}, u32[]{:S(2)}, u32[]{:S(2)}) collective-permute-start(bf16[1024,256]{1,0:T(8,128)(2,1)S(1)} %get-tuple-element.58), channel_id=1, source_target_pairs={{2,16},{3,17},{6,20},{7,21},{10,24},{11,25},{14,28},{15,29},{16,2}... | collective-permute-start | bytes 1572872 | tf_op jit(solution)/shard_map/ppermute | solution.py:346
  276.4 16.6 %collective-permute-done.31 = bf16[1024,256]{1,0:T(8,128)(2,1)S(1)} collective-permute-done((bf16[1024,256]{1,0:T(8,128)(2,1)S(1)}, bf16[1024,256]{1,0:T(8,128)(2,1)S(1)}, u32[]{:S(2)}, u32[]{:S(2)}) %collective-permute-start.31) | collective-permute-done | bytes 524320 | tf_op jit(solution)/shard_map/ppermute | solution.py:341
  293.0 6.8 %collective-permute-done.33 = bf16[1024,256]{1,0:T(8,128)(2,1)} collective-permute-done((bf16[1024,256]{1,0:T(8,128)(2,1)S(1)}, bf16[1024,256]{1,0:T(8,128)(2,1)}, u32[]{:S(2)}, u32[]{:S(2)}) %collective-permute-start.33) | collective-permute-done | bytes 524320 | tf_op jit(solution)/shard_map/ppermute | solution.py:346
  299.8 2.1 add_convert_fusion.1
  (92 shorter events, 33.3 us)
Async XLA Ops:
  4.7 46.8 %collective-permute-start.1 = (bf16[512,2048]{1,0:T(8,128)(2,1)}, bf16[512,2048]{1,0:T(8,128)(2,1)}, u32[]{:S(2)}, u32[]{:S(2)}) collective-permute-start(bf16[512,2048]{1,0:T(8,128)(2,1)} %add_convert_fusion.refs_0_), channel_id=1, source_target_pairs={{0,8},{4,12},{8,0},{12,4},{16,24},{20,28},{24,16},{28,20},{1,9},{5... | collective-permute-start | bytes 6291464 | tf_op jit(solution)/shard_map/ppermute | solution.py:20
  6.0 218.7 %collective-permute-start = (bf16[512,2048]{1,0:T(8,128)(2,1)}, bf16[512,2048]{1,0:T(8,128)(2,1)}, u32[]{:S(2)}, u32[]{:S(2)}) collective-permute-start(bf16[512,2048]{1,0:T(8,128)(2,1)} %add_convert_fusion.refs_0_), channel_id=1, source_target_pairs={{0,4},{4,0},{8,12},{12,8},{16,20},{20,16},{24,28},{28,24},{1,5},{5... | collective-permute-start | bytes 6291464 | tf_op jit(solution)/shard_map/ppermute | solution.py:20
  51.5 173.2 %collective-permute-start.2 = (bf16[512,2048]{1,0:T(8,128)(2,1)}, bf16[512,2048]{1,0:T(8,128)(2,1)}, u32[]{:S(2)}, u32[]{:S(2)}) collective-permute-start(bf16[512,2048]{1,0:T(8,128)(2,1)} %collective-permute-done.1.refs_2_), channel_id=1, source_target_pairs={{0,4},{4,0},{8,12},{12,8},{16,20},{20,16},{24,28},{28,24},{1,5},{5... | collective-permute-start | bytes 6291464 | tf_op jit(solution)/shard_map/ppermute | solution.py:20
  55.8 43.7 %collective-permute-start.3 = (bf16[18,2048]{1,0:T(8,128)(2,1)}, bf16[18,2048]{1,0:T(8,128)(2,1)S(1)}, u32[]{:S(2)}, u32[]{:S(2)}) collective-permute-start(bf16[18,2048]{1,0:T(8,128)(2,1)} %reshape.27), channel_id=1, source_target_pairs={{0,4},{4,8},{8,12},{12,16},{16,20},{20,24},{24,28},{1,5},{5,9},{9,... | collective-permute-start | bytes 221192 | tf_op jit(solution)/shard_map/ppermute | solution.py:276
  111.2 14.4 %collective-permute-start.5 = (bf16[256,256]{1,0:T(8,128)(2,1)S(1)}, bf16[256,256]{1,0:T(8,128)(2,1)S(1)}, u32[]{:S(2)}, u32[]{:S(2)}) collective-permute-start(bf16[256,256]{1,0:T(8,128)(2,1)S(1)} %get-tuple-element.34), channel_id=1, source_target_pairs={{0,4},{4,0},{8,12},{12,8},{16,20},{20,16},{24,28},{28,24},{1,5},{5... | collective-permute-start | bytes 393224 | tf_op jit(solution)/shard_map/ppermute | solution.py:20
  111.2 16.7 %collective-permute-start.6 = (bf16[256,256]{1,0:T(8,128)(2,1)S(1)}, bf16[256,256]{1,0:T(8,128)(2,1)S(1)}, u32[]{:S(2)}, u32[]{:S(2)}) collective-permute-start(bf16[256,256]{1,0:T(8,128)(2,1)S(1)} %get-tuple-element.35), channel_id=1, source_target_pairs={{0,8},{4,12},{8,0},{12,4},{16,24},{20,28},{24,16},{28,20},{1,9},{5... | collective-permute-start | bytes 393224 | tf_op jit(solution)/shard_map/ppermute | solution.py:20
  112.6 15.3 %collective-permute-start.7 = (bf16[256,256]{1,0:T(8,128)(2,1)S(1)}, bf16[256,256]{1,0:T(8,128)(2,1)S(1)}, u32[]{:S(2)}, u32[]{:S(2)}) collective-permute-start(bf16[256,256]{1,0:T(8,128)(2,1)S(1)} %get-tuple-element.36), channel_id=1, source_target_pairs={{0,12},{4,8},{8,4},{12,0},{16,28},{20,24},{24,20},{28,16},{1,13},{... | collective-permute-start | bytes 393224 | tf_op jit(solution)/shard_map/ppermute | solution.py:20
  125.5 6.2 %collective-permute-start.8 = (bf16[256,256]{1,0:T(8,128)(2,1)S(1)}, bf16[256,256]{1,0:T(8,128)(2,1)S(1)}, u32[]{:S(2)}, u32[]{:S(2)}) collective-permute-start(bf16[256,256]{1,0:T(8,128)(2,1)S(1)} %get-tuple-element.37), channel_id=1, source_target_pairs={{0,16},{4,20},{8,24},{12,28},{16,0},{20,4},{24,8},{28,12},{1,17},{... | collective-permute-start | bytes 393224 | tf_op jit(solution)/shard_map/ppermute | solution.py:20
  127.9 14.9 %collective-permute-start.9 = (bf16[256,256]{1,0:T(8,128)(2,1)S(1)}, bf16[256,256]{1,0:T(8,128)(2,1)S(1)}, u32[]{:S(2)}, u32[]{:S(2)}) collective-permute-start(bf16[256,256]{1,0:T(8,128)(2,1)S(1)} %get-tuple-element.38), channel_id=1, source_target_pairs={{0,20},{4,16},{8,28},{12,24},{16,4},{20,0},{24,12},{28,8},{1,21},{... | collective-permute-start | bytes 393224 | tf_op jit(solution)/shard_map/ppermute | solution.py:20
  127.9 16.5 %collective-permute-start.10 = (bf16[256,256]{1,0:T(8,128)(2,1)S(1)}, bf16[256,256]{1,0:T(8,128)(2,1)S(1)}, u32[]{:S(2)}, u32[]{:S(2)}) collective-permute-start(bf16[256,256]{1,0:T(8,128)(2,1)S(1)} %get-tuple-element.39), channel_id=1, source_target_pairs={{0,24},{4,28},{8,16},{12,20},{16,8},{20,12},{24,0},{28,4},{1,25},{... | collective-permute-start | bytes 393224 | tf_op jit(solution)/shard_map/ppermute | solution.py:20
  131.7 15.8 %collective-permute-start.11 = (bf16[256,256]{1,0:T(8,128)(2,1)S(1)}, bf16[256,256]{1,0:T(8,128)(2,1)S(1)}, u32[]{:S(2)}, u32[]{:S(2)}) collective-permute-start(bf16[256,256]{1,0:T(8,128)(2,1)S(1)} %get-tuple-element.40), channel_id=1, source_target_pairs={{0,28},{4,24},{8,20},{12,16},{16,12},{20,8},{24,4},{28,0},{1,29},{... | collective-permute-start | bytes 393224 | tf_op jit(solution)/shard_map/ppermute | solution.py:20
  142.8 10.3 %collective-permute-start.12 = (bf16[256,256]{1,0:T(8,128)(2,1)S(1)}, bf16[256,256]{1,0:T(8,128)(2,1)S(1)}, u32[]{:S(2)}, u32[]{:S(2)}) collective-permute-start(bf16[256,256]{1,0:T(8,128)(2,1)S(1)} %get-tuple-element.43), channel_id=1, source_target_pairs={{0,4},{4,0},{8,12},{12,8},{16,20},{20,16},{24,28},{28,24},{1,5},{5... | collective-permute-start | bytes 393224 | tf_op jit(solution)/shard_map/ppermute | solution.py:20
  144.4 10.2 %collective-permute-start.13 = (bf16[256,256]{1,0:T(8,128)(2,1)S(1)}, bf16[256,256]{1,0:T(8,128)(2,1)S(1)}, u32[]{:S(2)}, u32[]{:S(2)}) collective-permute-start(bf16[256,256]{1,0:T(8,128)(2,1)S(1)} %get-tuple-element.44), channel_id=1, source_target_pairs={{0,20},{4,16},{8,28},{12,24},{16,4},{20,0},{24,12},{28,8},{1,21},{... | collective-permute-start | bytes 393224 | tf_op jit(solution)/shard_map/ppermute | solution.py:20
  147.5 17.8 %collective-permute-start.15 = (bf16[256,256]{1,0:T(8,128)(2,1)S(1)}, bf16[256,256]{1,0:T(8,128)(2,1)S(1)}, u32[]{:S(2)}, u32[]{:S(2)}) collective-permute-start(bf16[256,256]{1,0:T(8,128)(2,1)S(1)} %get-tuple-element.47), channel_id=1, source_target_pairs={{0,8},{4,12},{8,0},{12,4},{16,24},{20,28},{24,16},{28,20},{1,9},{5... | collective-permute-start | bytes 393224 | tf_op jit(solution)/shard_map/ppermute | solution.py:20
  153.1 14.5 %collective-permute-start.16 = (bf16[256,256]{1,0:T(8,128)(2,1)S(1)}, bf16[256,256]{1,0:T(8,128)(2,1)S(1)}, u32[]{:S(2)}, u32[]{:S(2)}) collective-permute-start(bf16[256,256]{1,0:T(8,128)(2,1)S(1)} %get-tuple-element.48), channel_id=1, source_target_pairs={{0,24},{4,28},{8,16},{12,20},{16,8},{20,12},{24,0},{28,4},{1,25},{... | collective-permute-start | bytes 393224 | tf_op jit(solution)/shard_map/ppermute | solution.py:20
  154.6 16.6 %collective-permute-start.18 = (bf16[256,256]{1,0:T(8,128)(2,1)S(1)}, bf16[256,256]{1,0:T(8,128)(2,1)S(1)}, u32[]{:S(2)}, u32[]{:S(2)}) collective-permute-start(bf16[256,256]{1,0:T(8,128)(2,1)S(1)} %get-tuple-element.51), channel_id=1, source_target_pairs={{0,12},{4,8},{8,4},{12,0},{16,28},{20,24},{24,20},{28,16},{1,13},{... | collective-permute-start | bytes 393224 | tf_op jit(solution)/shard_map/ppermute | solution.py:20
  165.4 18.7 %collective-permute-start.14 = (bf16[256,512]{1,0:T(8,128)(2,1)S(1)}, bf16[256,512]{1,0:T(8,128)(2,1)S(1)}, u32[]{:S(2)}, u32[]{:S(2)}) collective-permute-start(bf16[256,512]{1,0:T(8,128)(2,1)S(1)} %gate.5), channel_id=1, source_target_pairs={{0,4},{4,0},{8,12},{12,8},{16,20},{20,16},{24,28},{28,24},{1,5},{5... | collective-permute-start | bytes 786440 | tf_op jit(solution)/shard_map/ppermute | solution.py:20
  167.6 6.6 %collective-permute-start.19 = (bf16[256,256]{1,0:T(8,128)(2,1)S(1)}, bf16[256,256]{1,0:T(8,128)(2,1)S(1)}, u32[]{:S(2)}, u32[]{:S(2)}) collective-permute-start(bf16[256,256]{1,0:T(8,128)(2,1)S(1)} %get-tuple-element.52), channel_id=1, source_target_pairs={{0,28},{4,24},{8,20},{12,16},{16,12},{20,8},{24,4},{28,0},{1,29},{... | collective-permute-start | bytes 393224 | tf_op jit(solution)/shard_map/ppermute | solution.py:20
  171.2 11.4 %collective-permute-start.4 = (bf16[256,256]{1,0:T(8,128)(2,1)S(1)}, bf16[256,256]{1,0:T(8,128)(2,1)S(1)}, u32[]{:S(2)}, u32[]{:S(2)}) collective-permute-start(bf16[256,256]{1,0:T(8,128)(2,1)S(1)} %get-tuple-element.32), channel_id=1, source_target_pairs={{0,16},{4,20},{8,24},{12,28},{16,0},{20,4},{24,8},{28,12},{1,17},{... | collective-permute-start | bytes 393224 | tf_op jit(solution)/shard_map/ppermute | solution.py:20
  174.2 14.2 %collective-permute-start.17 = (bf16[256,512]{1,0:T(8,128)(2,1)S(1)}, bf16[256,512]{1,0:T(8,128)(2,1)S(1)}, u32[]{:S(2)}, u32[]{:S(2)}) collective-permute-start(bf16[256,512]{1,0:T(8,128)(2,1)S(1)} %gate.6), channel_id=1, source_target_pairs={{0,8},{4,12},{8,0},{12,4},{16,24},{20,28},{24,16},{28,20},{1,9},{5... | collective-permute-start | bytes 786440 | tf_op jit(solution)/shard_map/ppermute | solution.py:20
  182.6 16.8 %collective-permute-start.20 = (bf16[256,512]{1,0:T(8,128)(2,1)S(1)}, bf16[256,512]{1,0:T(8,128)(2,1)S(1)}, u32[]{:S(2)}, u32[]{:S(2)}) collective-permute-start(bf16[256,512]{1,0:T(8,128)(2,1)S(1)} %gate.7), channel_id=1, source_target_pairs={{0,12},{4,8},{8,4},{12,0},{16,28},{20,24},{24,20},{28,16},{1,13},{... | collective-permute-start | bytes 786440 | tf_op jit(solution)/shard_map/ppermute | solution.py:20
  184.1 20.1 %collective-permute-start.21 = (bf16[256,512]{1,0:T(8,128)(2,1)S(1)}, bf16[256,512]{1,0:T(8,128)(2,1)S(1)}, u32[]{:S(2)}, u32[]{:S(2)}) collective-permute-start(bf16[256,512]{1,0:T(8,128)(2,1)S(1)} %gate.4.refs_4_), channel_id=1, source_target_pairs={{0,16},{4,20},{8,24},{12,28},{16,0},{20,4},{24,8},{28,12},{1,17},{... | collective-permute-start | bytes 786440 | tf_op jit(solution)/shard_map/ppermute | solution.py:20
  188.4 36.2 %collective-permute-start.22 = (bf16[256,512]{1,0:T(8,128)(2,1)S(1)}, bf16[256,512]{1,0:T(8,128)(2,1)S(1)}, u32[]{:S(2)}, u32[]{:S(2)}) collective-permute-start(bf16[256,512]{1,0:T(8,128)(2,1)S(1)} %gate.5), channel_id=1, source_target_pairs={{0,20},{4,16},{8,28},{12,24},{16,4},{20,0},{24,12},{28,8},{1,21},{... | collective-permute-start | bytes 786440 | tf_op jit(solution)/shard_map/ppermute | solution.py:20
  199.4 25.2 %collective-permute-start.23 = (bf16[256,512]{1,0:T(8,128)(2,1)S(1)}, bf16[256,512]{1,0:T(8,128)(2,1)S(1)}, u32[]{:S(2)}, u32[]{:S(2)}) collective-permute-start(bf16[256,512]{1,0:T(8,128)(2,1)S(1)} %gate.6), channel_id=1, source_target_pairs={{0,24},{4,28},{8,16},{12,20},{16,8},{20,12},{24,0},{28,4},{1,25},{... | collective-permute-start | bytes 786440 | tf_op jit(solution)/shard_map/ppermute | solution.py:20
  204.1 20.5 %collective-permute-start.24 = (bf16[256,512]{1,0:T(8,128)(2,1)S(1)}, bf16[256,512]{1,0:T(8,128)(2,1)S(1)}, u32[]{:S(2)}, u32[]{:S(2)}) collective-permute-start(bf16[256,512]{1,0:T(8,128)(2,1)S(1)} %gate.7), channel_id=1, source_target_pairs={{0,28},{4,24},{8,20},{12,16},{16,12},{20,8},{24,4},{28,0},{1,29},{... | collective-permute-start | bytes 786440 | tf_op jit(solution)/shard_map/ppermute | solution.py:20
  238.2 23.3 %collective-permute-start.25 = (f32[1024,512]{1,0:T(8,128)}, f32[1024,512]{1,0:T(8,128)S(1)}, u32[]{:S(2)}, u32[]{:S(2)}) collective-permute-start(f32[1024,512]{1,0:T(8,128)} %get-tuple-element.56), channel_id=1, source_target_pairs={{0,1},{1,0},{2,3},{3,2},{4,5},{5,4},{6,7},{7,6},{8,9},{9,8},{10,11... | collective-permute-start | bytes 6291464 | tf_op jit(solution)/shard_map/ppermute | solution.py:20
  243.7 2.4 collective-permute-start.27
  246.2 11.6 %collective-permute-start.29 = (f32[1,512]{1,0:T(1,128)S(1)}, f32[1,512]{1,0:T(1,128)S(1)}, u32[]{:S(2)}, u32[]{:S(2)}) collective-permute-start(f32[1,512]{1,0:T(1,128)S(1)} %add.53), channel_id=1, source_target_pairs={{0,8},{4,12},{8,0},{12,4},{16,24},{20,28},{24,16},{28,20},{1,9},{5... | collective-permute-start | bytes 6152 | tf_op jit(solution)/shard_map/ppermute | solution.py:20
  257.8 2.4 collective-permute-start.30
  266.3 26.7 %collective-permute-start.31 = (bf16[1024,256]{1,0:T(8,128)(2,1)S(1)}, bf16[1024,256]{1,0:T(8,128)(2,1)S(1)}, u32[]{:S(2)}, u32[]{:S(2)}) collective-permute-start(bf16[1024,256]{1,0:T(8,128)(2,1)S(1)} %get-tuple-element.58), channel_id=1, source_target_pairs={{0,16},{1,17},{4,20},{5,21},{8,24},{9,25},{12,28},{13,29},{18,2},{... | collective-permute-start | bytes 1572872 | tf_op jit(solution)/shard_map/ppermute | solution.py:341
  267.6 25.4 %collective-permute-start.32 = (bf16[1024,256]{1,0:T(8,128)(2,1)}, bf16[1024,256]{1,0:T(8,128)(2,1)}, u32[]{:S(2)}, u32[]{:S(2)}) collective-permute-start(bf16[1024,256]{1,0:T(8,128)(2,1)} %get-tuple-element.57), channel_id=1, source_target_pairs={{2,0},{3,1},{6,4},{7,5},{10,8},{11,9},{14,12},{15,13},{16,18},{17,... | collective-permute-start | bytes 1572872 | tf_op jit(solution)/shard_map/ppermute | solution.py:336
  271.7 28.1 %collective-permute-start.33 = (bf16[1024,256]{1,0:T(8,128)(2,1)S(1)}, bf16[1024,256]{1,0:T(8,128)(2,1)}, u32[]{:S(2)}, u32[]{:S(2)}) collective-permute-start(bf16[1024,256]{1,0:T(8,128)(2,1)S(1)} %get-tuple-element.58), channel_id=1, source_target_pairs={{2,16},{3,17},{6,20},{7,21},{10,24},{11,25},{14,28},{15,29},{16,2}... | collective-permute-start | bytes 1572872 | tf_op jit(solution)/shard_map/ppermute | solution.py:346
  (17 other events, 532.2 us)

commit v2 on v0

v2 whole, which is shorter than its diff:
```python
import functools

import jax
import jax.numpy as jnp
from jax import lax
from jax.experimental import pallas as pl
from jax.experimental.pallas import tpu as pltpu
from jax.sharding import PartitionSpec as P

GROUP = 16
TAPS = 7
EPSILON = 1e-06
MIB = 1 << 20
VMEM_LIMIT = 24 * MIB
BF16 = jnp.bfloat16
F32 = jnp.float32


def exchange(block, axis, distance):
    count = lax.axis_size(axis)
    return lax.ppermute(block, axis, [(i, i ^ distance) for i in range(count)])


def whole_spec(shape):
    return pl.BlockSpec(shape, lambda *_: (0,) * len(shape))


def tail_kernel(input_ref, out_ref):
    rows = []
    for i in range(3):
        turned = input_ref[i].astype(F32).T
        rows.append(turned[turned.shape[0] - 8 :])
    rows.append(jnp.zeros_like(rows[0]))
    out_ref[...] = jnp.concatenate(rows, axis=0).astype(BF16)


def last_tokens(values):
    width, tokens = values.shape[1:]
    lanes = min(width, 512)
    return pl.pallas_call(
        tail_kernel,
        grid=(width // lanes,),
        in_specs=[pl.BlockSpec((3, lanes, 128), lambda c: (0, c, tokens // 128 - 1))],
        out_specs=pl.BlockSpec((32, lanes), lambda c: (0, c)),
        out_shape=jax.ShapeDtypeStruct((32, width), BF16),
        compiler_params=pltpu.CompilerParams(vmem_limit_bytes=VMEM_LIMIT),
        name="last_tokens",
    )(values)


def merge_kernel(cuts, frozen_ref, down_ref, up_ref, *refs):
    norms_ref, part_refs = refs[-1], refs[-1 - len(cuts) + 1 : -1]
    for part_ref, start, end in zip(part_refs, cuts, cuts[1:]):
        update = jnp.dot(up_ref[start:end, :], down_ref[...], preferred_element_type=F32)
        merged = (frozen_ref[start:end, :].astype(F32) + update).astype(BF16)
        part_ref[...] = merged
        squares = jnp.square(merged.astype(F32))
        norms_ref[start:end, :] = jnp.broadcast_to(
            jnp.sum(squares, axis=1, keepdims=True), (end - start, 128)
        )


def merge(cuts, frozen, down, up, *others):
    rows, width = frozen.shape
    return pl.pallas_call(
        functools.partial(merge_kernel, cuts),
        in_specs=[pl.BlockSpec(memory_space=pltpu.VMEM)] * 3
        + [pl.BlockSpec(memory_space=pl.ANY)] * len(others),
        out_shape=[
            jax.ShapeDtypeStruct((end - start, width), BF16) for start, end in zip(cuts, cuts[1:])
        ]
        + [jax.ShapeDtypeStruct((rows, 128), F32)],
        compiler_params=pltpu.CompilerParams(vmem_limit_bytes=VMEM_LIMIT),
        name="merge",
    )(frozen, down, up, *others)


def featurize_kernel(input_ref, taps_ref, halo_ref, mixture_ref, query_ref, held):
    block, tokens = input_ref.shape[1:]
    lanes = min(block, 128)
    shift = lax.rem(pl.program_id(0) * block, taps_ref.shape[2])
    for start in range(0, block, lanes):
        channels = slice(start, start + lanes)
        weights = []
        for i in range(3):
            taps = jnp.concatenate([taps_ref[i], jnp.zeros((1, taps_ref.shape[2]), F32)], axis=0)
            halo = halo_ref[...].astype(F32)[8 * i : 8 * i + 8]
            if block < 128:
                taps = pltpu.roll(taps, 128 - shift, 1)
                halo = pltpu.roll(halo, 128 - shift, 1)
            weights.append(taps[:, channels])
            held[i, :8, :] = halo[:, channels]
            held[i, 8:, :] = input_ref[i, channels, :].astype(F32).T
        for place in range(0, tokens, 128):
            sums = []
            for i in range(3):
                total = weights[i][0:1, :] * held[i, 8 + place : 136 + place, :]
                for j in range(1, TAPS):
                    total += weights[i][j : j + 1, :] * held[i, 8 + place - j : 136 + place - j, :]
                sums.append(total)
            here = (0, channels, slice(place, place + 128))
            mixture_ref[here] = (sums[1] * sums[2]).T.astype(BF16)
            query_ref[here] = sums[0].T.astype(BF16)


def featurize(values, taps, halo, ctx_count):
    width, tokens = values.shape[1:]
    block = width // ctx_count
    lanes = max(block, 128)
    shape = jax.ShapeDtypeStruct((ctx_count, block, tokens), BF16)
    out_spec = pl.BlockSpec((1, block, tokens), lambda d: (d, 0, 0))
    return pl.pallas_call(
        featurize_kernel,
        grid=(ctx_count,),
        in_specs=[
            pl.BlockSpec((3, block, tokens), lambda d: (0, d, 0)),
            pl.BlockSpec((3, TAPS, lanes), lambda d: (0, 0, d * block // lanes)),
            pl.BlockSpec((32, lanes), lambda d: (0, d * block // lanes)),
        ],
        out_specs=[out_spec] * 2,
        out_shape=[shape] * 2,
        scratch_shapes=[pltpu.VMEM((3, 8 + tokens, min(block, 128)), F32)],
        compiler_params=pltpu.CompilerParams(vmem_limit_bytes=VMEM_LIMIT),
        cost_estimate=pl.CostEstimate(
            flops=6 * TAPS * width * tokens, bytes_accessed=10 * MIB, transcendentals=0
        ),
        name="featurize",
    )(values, taps, halo)


def convolve_kernel(ctx_count, filters_ref, skip_ref, mixture_ref, added_ref, out_ref, total_ref):
    group = pl.program_id(0)
    tokens = mixture_ref.shape[2]

    @pl.when(group < filters_ref.shape[0])
    def _():
        left = mixture_ref[...].reshape(ctx_count * GROUP, tokens)

        def product(rows, taps):
            spread = jnp.broadcast_to(taps, (tokens, 2 * tokens))
            turned = pltpu.roll(spread, 0, 1, stride=1, stride_axis=0)[:, tokens:]
            return jnp.dot(left[:rows], turned.astype(BF16), preferred_element_type=F32)

        here = pl.ds(group, 1)
        first = jnp.concatenate([jnp.zeros((1, tokens), F32), filters_ref[here, :tokens]], axis=1)
        rows = ctx_count * GROUP
        total_ref[:rows, :] = product(rows, first)
        if ctx_count <= 8:
            for d in range(1, ctx_count):
                lags = filters_ref[here, (d - 1) * tokens : (d + 1) * tokens]
                total_ref[d * GROUP :, :] += product(rows - d * GROUP, lags)
        else:

            @pl.loop(1, ctx_count)
            def _(d):
                start = pl.multiple_of((d - 1) * tokens, tokens)
                place = pl.ds(pl.multiple_of(d * GROUP, GROUP), rows)
                lags = filters_ref[here, pl.ds(start, 2 * tokens)]
                total_ref[place, :] = total_ref[place, :] + product(rows, lags)

        skip = jnp.concatenate([skip_ref[...]] * (tokens // 128), axis=1)
        for j in range(ctx_count):
            wide = mixture_ref[j].astype(F32)
            total = total_ref[j * GROUP : (j + 1) * GROUP, :]
            out_ref[j] = (total + skip * wide).astype(BF16)

    @pl.when(group == filters_ref.shape[0])
    def _():
        for j in range(ctx_count):
            out_ref[j] = added_ref[...]


def convolve(filters, skip, mixture, added):
    ctx_count, block, tokens = mixture.shape
    groups = filters.shape[0]
    total_rows = ctx_count * GROUP * (1 if ctx_count <= 8 else 2)
    return pl.pallas_call(
        functools.partial(convolve_kernel, ctx_count),
        grid=(groups + 1,),
        in_specs=[
            whole_spec(filters.shape),
            pl.BlockSpec((GROUP, 128), lambda g: (jnp.minimum(g, groups - 1), 0)),
            pl.BlockSpec(
                (ctx_count, GROUP, tokens), lambda g: (0, jnp.minimum(g, groups - 1), 0)
            ),
            whole_spec(added.shape),
        ],
        out_specs=pl.BlockSpec((ctx_count, GROUP, tokens), lambda g: (0, g, 0)),
        scratch_shapes=[pltpu.VMEM((total_rows, tokens), F32)],
        out_shape=jax.ShapeDtypeStruct((ctx_count, block + GROUP, tokens), BF16),
        compiler_params=pltpu.CompilerParams(vmem_limit_bytes=VMEM_LIMIT),
        cost_estimate=pl.CostEstimate(
            flops=8 * block * (ctx_count * tokens) ** 2, bytes_accessed=20 * MIB, transcendentals=0
        ),
        name="convolve",
    )(filters, skip, mixture, added)


def gate_kernel(query_ref, summed_ref, out_ref):
    out_ref[...] = (query_ref[0].astype(F32) * summed_ref[0].astype(F32)).astype(BF16)


def gate(query, summed):
    ctx_count, block, tokens = query.shape
    spec = pl.BlockSpec((1, block, tokens), lambda d: (d, 0, 0))
    return pl.pallas_call(
        gate_kernel,
        grid=(ctx_count,),
        in_specs=[spec] * 2,
        out_specs=pl.BlockSpec((block, tokens), lambda d: (d, 0)),
        out_shape=jax.ShapeDtypeStruct((ctx_count * block, tokens), BF16),
        compiler_params=pltpu.CompilerParams(vmem_limit_bytes=VMEM_LIMIT),
        name="gate",
    )(query, summed)


def stage_kernel(*refs):
    *piece_refs, out_ref, sems = refs
    copies, at = [], 0
    for n, piece_ref in enumerate(piece_refs):
        rows = piece_ref.shape[0]
        copies.append(pltpu.make_async_copy(piece_ref, out_ref.at[pl.ds(at, rows), :], sems.at[n]))
        at += rows
    for copy in copies:
        copy.start()
    for copy in copies:
        copy.wait()


def stage_rows(pieces):
    rows = sum(piece.shape[0] for piece in pieces)
    return pl.pallas_call(
        stage_kernel,
        in_specs=[pl.BlockSpec(memory_space=pl.ANY)] * len(pieces),
        out_specs=pl.BlockSpec(memory_space=pltpu.VMEM),
        out_shape=jax.ShapeDtypeStruct((rows, pieces[0].shape[1]), BF16),
        scratch_shapes=[pltpu.SemaphoreType.DMA((len(pieces),))],
        compiler_params=pltpu.CompilerParams(vmem_limit_bytes=VMEM_LIMIT),
        name="stage_rows",
    )(*pieces)


def project_kernel(layout, places, where_ref, weight_ref, gating_ref, scaling_ref, *refs):
    keep_ref, send_ref = refs[-2:]
    low, core = where_ref[1], where_ref[2]
    tokens = keep_ref.shape[1]
    block = 2 * keep_ref.shape[0] // places
    total = jnp.dot(weight_ref[...], gating_ref[...], preferred_element_type=F32)
    at = 0
    for offset, rows, p in layout:
        place = jnp.bitwise_xor(low, p)
        mine = place // (places // 2) == core
        target = pl.ds(pl.multiple_of((place & (places // 2 - 1)) * block + offset, 16), rows)
        source = pl.ds(pl.multiple_of(place * block + offset, 16), rows)
        scaling = jnp.concatenate([scaling_ref[source, :]] * (tokens // 128), axis=1)
        scaled = total[at : at + rows] * scaling

        @pl.when(mine)
        def _():
            keep_ref[target, :] = scaled

        @pl.when(jnp.logical_not(mine))
        def _():
            send_ref[target, :] = scaled.astype(BF16)

        at += rows


def project(where, places, layout, weight, gating, scaling, *others):
    width, tokens = gating.shape
    total_rows = weight.shape[0]
    out = jax.ShapeDtypeStruct((total_rows // 2, tokens), F32)
    sent = jax.ShapeDtypeStruct((total_rows // 2, tokens), BF16)
    return pl.pallas_call(
        functools.partial(project_kernel, layout, places),
        grid_spec=pltpu.PrefetchScalarGridSpec(
            num_scalar_prefetch=1,
            grid=(1,),
            in_specs=[pl.BlockSpec(memory_space=pltpu.VMEM)] * 3
            + [pl.BlockSpec(memory_space=pl.ANY)] * len(others),
            out_specs=[pl.BlockSpec(memory_space=pltpu.VMEM)] * 2,
        ),
        out_shape=[out, sent],
        compiler_params=pltpu.CompilerParams(vmem_limit_bytes=28 * MIB),
        cost_estimate=pl.CostEstimate(
            flops=2 * total_rows * tokens * width, bytes_accessed=8 * MIB, transcendentals=0
        ),
        name="project",
    )(where, weight, gating, scaling, *others)


def after(value, *others):
    return lax.optimization_barrier((value, *others))[0]


def rows_with(norms, tokens):
    flat = norms.reshape(-1)
    flat = jnp.pad(flat, (0, -flat.shape[0] % tokens)).reshape(-1, tokens)
    pieces = []
    for _ in range(3):
        piece = lax.optimization_barrier(flat.astype(BF16))
        pieces.append(piece)
        flat = flat - piece.astype(F32)
    added = jnp.concatenate(pieces)
    return jnp.pad(added, ((0, GROUP - added.shape[0]), (0, 0)))


def norms_of(received, block, rows):
    ctx_count, _, tokens = received.shape
    lines = -(-rows // tokens)
    added = received[:, block : block + 3 * lines].astype(F32)
    added = added.reshape(ctx_count, 3, lines * tokens)
    return (added[:, 0] + (added[:, 1] + added[:, 2]))[:, :rows].reshape(ctx_count * rows)


def on_device(
    query_key_value_input,
    featurizer_weights,
    channel_skip_scale,
    group_long_filters,
    frozen_weight,
    down_update_weight,
    up_update_weight,
    magnitude,
):
    width, tokens = query_key_value_input.shape[1:]
    ctx_count = lax.axis_size("ctx")
    tp_count = lax.axis_size("tp")
    half = ctx_count // 2
    rows = frozen_weight.shape[0]
    me = lax.axis_index("ctx")
    tp_index = lax.axis_index("tp")
    low = jnp.bitwise_and(me, half - 1)
    high = me // half
    core = jnp.bitwise_and(tp_index, 1)
    upper_tp = tp_index // 2
    where = jnp.stack([me, low, core, high]).astype(jnp.int32)

    tail = last_tokens(query_key_value_input)
    halo = lax.ppermute(tail, "ctx", [(i, i + 1) for i in range(ctx_count - 1)])

    cuts = (0, rows * 3 // 8 // 16 * 16, rows * 5 // 8 // 16 * 16, rows)
    *parts, norms = merge(cuts, frozen_weight, down_update_weight, up_update_weight, tail)
    norms = norms[:, 0][None, :]
    norms = norms + sum(exchange(norms, "tp", distance) for distance in range(1, tp_count))

    taps = after(featurizer_weights, *parts)
    mixture, query = featurize(query_key_value_input, taps, halo, ctx_count)
    own_mixture = mixture
    mixture = lax.all_to_all(own_mixture, "ctx", split_axis=0, concat_axis=0, tiled=True)

    distances = []
    while 1 << len(distances) < half:
        distances.insert(0, 1 << len(distances))
    coarse, rest = distances[0], distances[1:]
    pieces, layout = [], []

    def finish(held, order, path, offset, length):
        for distance in path[:-1]:
            received = exchange(held, "ctx", distance)
            held = jnp.concatenate([held, received], axis=0)
            order = order + [index + distance for index in order]
        received = exchange(held, "ctx", path[-1])
        pieces.extend([held, received])
        layout.extend((offset, length, index) for index in order)
        layout.extend((offset, length, index + path[-1]) for index in order)
        return received

    part = after(parts[0], own_mixture)
    far_part = exchange(part, "ctx", coarse)
    got = finish(part, [0], rest, 0, cuts[1])
    block = width // ctx_count
    skip = jnp.broadcast_to(channel_skip_scale[:, None], (block, 128))
    summed = convolve(group_long_filters, skip, mixture, rows_with(norms, tokens))
    sent = after(summed, far_part, got)
    received = lax.all_to_all(sent, "ctx", split_axis=0, concat_axis=0, tiled=True)
    part = after(parts[1], sent)
    other_part = exchange(part, "ctx", coarse)
    got = finish(part, [0], rest, cuts[1], cuts[2] - cuts[1])
    gating = gate(after(query, received, got, other_part), received)
    far_gating = exchange(gating, "ctx", half)
    finish(after(far_part, gating), [coarse], rest, 0, cuts[1])
    finish(after(other_part, gating), [coarse], rest, cuts[1], cuts[2] - cuts[1])
    part = after(parts[2], gating)
    length = cuts[3] - cuts[2]
    if len(rest) == 1:
        upper = length // 3 // 16 * 16
        coarse_part, fine_part = exchange(part, "ctx", coarse), exchange(part, "ctx", rest[0])
        last = exchange(coarse_part[:upper], "ctx", rest[0])
        other = exchange(fine_part[upper:], "ctx", coarse)
        pieces.extend([part, coarse_part, fine_part, last, other])
        for index in (0, coarse, rest[0]):
            layout.append((cuts[2], length, index))
        layout.append((cuts[2], upper, coarse + rest[0]))
        layout.append((cuts[2] + upper, length - upper, coarse + rest[0]))
    else:
        finish(part, [0], distances, cuts[2], length)
    weight = stage_rows(pieces)

    first = high * half * rows
    norms_here = lax.dynamic_slice_in_dim(norms_of(received, block, rows), first, half * rows)
    magnitude_here = lax.dynamic_slice_in_dim(magnitude, first, half * rows)
    scaling = magnitude_here / jnp.sqrt(norms_here + EPSILON)
    scaling = jnp.broadcast_to(scaling[:, None], (half * rows, 128))

    def place(h, l, y, c):
        return (h * half + l) * tp_count + y * 2 + c

    sites = [(h, l, c) for h in range(2) for l in range(half) for c in range(2)]
    both = ("ctx", "tp")
    sums = []
    for gated in (gating, far_gating):
        keep, send = project(where, half, tuple(layout), weight, gated, scaling, *sums)
        sums.append((keep + exchange(send, "tp", 1).astype(F32)).astype(BF16))
    near, far = sums
    from_near = lax.ppermute(
        near, both, [(place(h, l, 1 - h, c), place(h, l, h, c)) for h, l, c in sites]
    )
    from_far = lax.ppermute(
        far, both, [(place(h, l, h, c), place(1 - h, l, h, c)) for h, l, c in sites]
    )
    from_diagonal = lax.ppermute(
        far, both, [(place(h, l, 1 - h, c), place(1 - h, l, h, c)) for h, l, c in sites]
    )
    own = jnp.where(upper_tp == high, near, from_far).astype(F32)
    other = jnp.where(upper_tp == high, from_near, from_diagonal).astype(F32)
    return (own + other).astype(BF16)


def solution(mesh):
    placed = (
        P(None, "tp", "ctx"),
        P(None, None, "tp"),
        P(("tp", "ctx")),
        P(("tp", "ctx"), None),
        P("ctx", "tp"),
        P(None, "tp"),
        P("ctx", None),
        P(),
    )
    return jax.shard_map(
        on_device, mesh=mesh, in_specs=placed, out_specs=P("tp", "ctx"), check_vma=False
    )
```

time: 369 us -> 202 us (0.55)
  the two profiles are of different devices: /device:TPU:0 before, /device:TPU:7 now
where the time goes in v2:
time: 202 us; the launch traced here: 200 us
  waiting for transfers between devices  118 us (58%)
  starting transfers between devices  37 us (18%)
  Pallas kernels  27.3 us (14%)
  local copies, waits for them, and re-layouts  15.3 us (8%)
  other arithmetic  2.2 us (1%)
    ppermute x16, waiting for transfers between devices, exchange(): return lax.ppermute(block, axis, [(i, i ^ distance) for i in range(count)])  73.7 us
    all_to_all x1, waiting for transfers between devices, on_device(): lax.all_to_all(own_mixture, 'ctx', split_axis=0, concat_axis=0, tiled=True)  18.6 us
    ppermute x1, waiting for transfers between devices, on_device(): lax.ppermute(far, both, [(place(h, l, 1 - h, c), place(1 - h, l, h, c)) f...  17.6 us
    ppermute x16, starting transfers between devices, exchange(): return lax.ppermute(block, axis, [(i, i ^ distance) for i in range(count)])  16.5 us
    unnamed x49, local copies, waits for them, and re-layouts  12.8 us
    pallas_call x1, Pallas kernels, convolve(): pl.pallas_call(functools.partial(convolve_kernel, ctx_count), grid=(group...  9.72 us
    pallas_call x2, Pallas kernels, project(): pl.pallas_call(functools.partial(project_kernel, layout, places), grid_sp...  7.76 us
    pallas_call x1, Pallas kernels, featurize(): pl.pallas_call(featurize_kernel, grid=(ctx_count,), in_specs=[pl.BlockSpe...  5.33 us
  transfers between devices with their start and end apart: 22, of which 13 were waited for; matrix products, arithmetic and copies ran while one was open for 2% of the time, Pallas kernels for 8%

profile of v2, /device:TPU:7, one launch (start us, length us, event | category | flops | bytes accessed | tf_op | source)
XLA Modules:
  0.0 200.2 jit_solution(11606328633064104416)
XLA Ops:
  0.0 1.9 copy-done
  2.9 3.2 %collective-permute-start = (bf16[32,2048]{1,0:T(8,128)(2,1)S(1)}, bf16[32,2048]{1,0:T(8,128)(2,1)S(1)}, u32[]{:S(2)}, u32[]{:S(2)}) collective-permute-start(bf16[32,2048]{1,0:T(8,128)(2,1)S(1)} %last_tokens.1.refs_0_), channel_id=1, source_target_pairs={{0,4},{4,8},{8,12},{12,16},{16,20},{20,24},{24,28},{1,5},{5,9},{9,... | collective-permute-start | bytes 393224 | tf_op jit(solution)/shard_map/ppermute | solution.py:340
  6.3 1.6 copy-done.2
  10.6 5.3 %featurize.1 = (bf16[8,256,256]{2,1,0:T(8,128)(2,1)S(1)}, bf16[8,256,256]{2,1,0:T(8,128)(2,1)S(1)}) custom-call(bf16[3,2048,256]{2,1,0:T(8,128)(2,1)S(1)} %copy-done.1, f32[3,7,2048]{2,1,0:T(8,128)S(1)} %copy-done.19, bf16[32,2048]{1,0:T(8,128)(2,1)S(1)} %collective-permute-done.halo_ref), custom_call_target="tpu_custom_call" | custom-call | flops 22020096 | bytes 10485760 | tf_op jit(solution)/shard_map/featurize/pallas_call | solution.py:112
  17.9 4.9 %all-to-all-start = ((bf16[8,256,256]{2,1,0:T(8,128)(2,1)}), bf16[8,256,256]{2,1,0:T(8,128)(2,1)S(1)}, u32[]{:S(2)}, u32[]{:S(2)}) async-start(bf16[8,256,256]{2,1,0:T(8,128)(2,1)} %copy-done.5), calls=%async_computation | async-start | bytes 2097152 | tf_op jit(solution)/shard_map/all_to_all | solution.py:350
  23.0 1.9 collective-permute-start.4
  24.9 1.2 collective-permute-start.3
  26.1 1.5 collective-permute-done.3
  27.7 1.2 collective-permute-start.5
  29.2 18.6 %all-to-all-done.mixture_ref = bf16[8,256,256]{2,1,0:T(8,128)(2,1)S(1)} async-done(((bf16[8,256,256]{2,1,0:T(8,128)(2,1)}), bf16[8,256,256]{2,1,0:T(8,128)(2,1)S(1)}, u32[]{:S(2)}, u32[]{:S(2)}) %all-to-all-start) | async-done | bytes 1048608 | tf_op jit(solution)/shard_map/all_to_all | solution.py:350
  47.9 9.7 %convolve.1 = bf16[8,272,256]{2,1,0:T(8,128)(2,1)} custom-call(f32[16,2048]{1,0:T(8,128)S(1)} %copy-done.21, f32[256,128]{1,0:T(8,128)S(1)} %broadcast_in_dim.4.skip_ref, bf16[8,256,256]{2,1,0:T(8,128)(2,1)S(1)} %all-to-all-done.mixture_ref, bf16[16,256]{1,0:T(8,128)(2,1)S(1)} %fusion.5.added_ref), custom_call_target="tpu_custom_call" | custom-call | flops 8589934592 | bytes 20971520 | tf_op jit(solution)/shard_map/convolve/pallas_call | solution.py:177
  58.2 4.2 %all-to-all-start.1 = ((bf16[8,272,256]{2,1,0:T(8,128)(2,1)}), bf16[8,272,256]{2,1,0:T(8,128)(2,1)S(1)}, u32[]{:S(2)}, u32[]{:S(2)}) async-start(bf16[8,272,256]{2,1,0:T(8,128)(2,1)} %convolve.1), calls=%async_computation.1 | async-start | bytes 2228224 | tf_op jit(solution)/shard_map/all_to_all | solution.py:376
  62.4 1.2 collective-permute-start.7
  63.9 28.6 %collective-permute-done.7.refs_6_ = bf16[128,2048]{1,0:T(8,128)(2,1)S(1)} collective-permute-done((bf16[128,2048]{1,0:T(8,128)(2,1)}, bf16[128,2048]{1,0:T(8,128)(2,1)S(1)}, u32[]{:S(2)}, u32[]{:S(2)}) %collective-permute-start.7) | collective-permute-done | bytes 524320 | tf_op jit(solution)/shard_map/ppermute | solution.py:21
  94.1 1.4 collective-permute-start.8
  95.5 2.4 %collective-permute-start.15 = (bf16[2048,256]{1,0:T(8,128)(2,1)S(1)}, bf16[2048,256]{1,0:T(8,128)(2,1)}, u32[]{:S(2)}, u32[]{:S(2)}) collective-permute-start(bf16[2048,256]{1,0:T(8,128)(2,1)S(1)} %gate.1.gating_ref), channel_id=1, source_target_pairs={{0,16},{4,20},{8,24},{12,28},{16,0},{20,4},{24,8},{28,12},{1,17},{... | collective-permute-start | bytes 3145736 | tf_op jit(solution)/shard_map/ppermute | solution.py:21
  98.4 12.8 %collective-permute-done.11.refs_10_ = bf16[192,2048]{1,0:T(8,128)(2,1)S(1)} collective-permute-done((bf16[192,2048]{1,0:T(8,128)(2,1)}, bf16[192,2048]{1,0:T(8,128)(2,1)S(1)}, u32[]{:S(2)}, u32[]{:S(2)}) %collective-permute-start.11) | collective-permute-done | bytes 786464 | tf_op jit(solution)/shard_map/ppermute | solution.py:21
  112.1 15.6 %collective-permute-done.10.refs_9_ = bf16[192,2048]{1,0:T(8,128)(2,1)} collective-permute-done((bf16[192,2048]{1,0:T(8,128)(2,1)}, bf16[192,2048]{1,0:T(8,128)(2,1)}, u32[]{:S(2)}, u32[]{:S(2)}) %collective-permute-start.10) | collective-permute-done | bytes 786464 | tf_op jit(solution)/shard_map/ppermute | solution.py:21
  128.7 2.8 %collective-permute-start.12 = (bf16[64,2048]{1,0:T(8,128)(2,1)S(1)}, bf16[64,2048]{1,0:T(8,128)(2,1)S(1)}, u32[]{:S(2)}, u32[]{:S(2)}) collective-permute-start(bf16[64,2048]{1,0:T(8,128)(2,1)S(1)} %slice.28), channel_id=1, source_target_pairs={{0,4},{4,0},{8,12},{12,8},{16,20},{20,16},{24,28},{28,24},{1,5},{5... | collective-permute-start | bytes 786440 | tf_op jit(solution)/shard_map/ppermute | solution.py:21
  132.2 7.1 %collective-permute-done.9.refs_7_ = bf16[128,2048]{1,0:T(8,128)(2,1)} collective-permute-done((bf16[128,2048]{1,0:T(8,128)(2,1)}, bf16[128,2048]{1,0:T(8,128)(2,1)}, u32[]{:S(2)}, u32[]{:S(2)}) %collective-permute-start.9) | collective-permute-done | bytes 524320 | tf_op jit(solution)/shard_map/ppermute | solution.py:21
  139.3 5.6 %collective-permute-done.12.refs_11_ = bf16[64,2048]{1,0:T(8,128)(2,1)S(1)} collective-permute-done((bf16[64,2048]{1,0:T(8,128)(2,1)S(1)}, bf16[64,2048]{1,0:T(8,128)(2,1)S(1)}, u32[]{:S(2)}, u32[]{:S(2)}) %collective-permute-start.12) | collective-permute-done | bytes 262176 | tf_op jit(solution)/shard_map/ppermute | solution.py:21
  149.6 2.4 %stage_rows.1.weight_ref = bf16[2048,2048]{1,0:T(8,128)(2,1)S(1)} custom-call(bf16[192,2048]{1,0:T(8,128)(2,1)S(1)} %copy-done.8, bf16[192,2048]{1,0:T(8,128)(2,1)} %collective-permute-done.1.refs_1_, bf16[128,2048]{1,0:T(8,128)(2,1)S(1)} %copy-done.12, bf16[128,2048]{1,0:T(8,128)(2,1)S(1)} %copy-done.16, bf16[192,2048]{1,0:T(8,128)(2,1)} %collective-permute-done.5.refs_4_, ...), custom_call_target="tpu_custom_call" | custom-call | tf_op jit(solution)/shard_map/stage_rows/pallas_call | solution.py:232
  152.3 3.3 %project.2 = (f32[1024,256]{1,0:T(8,128)S(1)}, bf16[1024,256]{1,0:T(8,128)(2,1)S(1)}) custom-call(s32[4]{0:T(128)S(1)} %pad_add_fusion.where_ref, bf16[2048,2048]{1,0:T(8,128)(2,1)S(1)} %stage_rows.1.weight_ref, bf16[2048,256]{1,0:T(8,128)(2,1)S(1)} %gate.1.gating_ref, f32[2048,128]{1,0:T(8,128)S(1)} %broadcast_in_dim.5.scaling_ref), custom_call_target="tpu_custom_call" | custom-call | flops 2147483648 | bytes 8388608 | tf_op jit(solution)/shard_map/project/pallas_call | solution.py:274
  155.6 2.8 %collective-permute-start.14 = (bf16[1024,256]{1,0:T(8,128)(2,1)S(1)}, bf16[1024,256]{1,0:T(8,128)(2,1)S(1)}, u32[]{:S(2)}, u32[]{:S(2)}) collective-permute-start(bf16[1024,256]{1,0:T(8,128)(2,1)S(1)} %get-tuple-element.38), channel_id=1, source_target_pairs={{0,1},{1,0},{2,3},{3,2},{4,5},{5,4},{6,7},{7,6},{8,9},{9,8},{10,11... | collective-permute-start | bytes 1572872 | tf_op jit(solution)/shard_map/ppermute | solution.py:21
  158.4 1.5 collective-permute-done.14
  160.1 4.5 %project.3 = (f32[1024,256]{1,0:T(8,128)S(1)}, bf16[1024,256]{1,0:T(8,128)(2,1)S(1)}) custom-call(s32[4]{0:T(128)S(1)} %pad_add_fusion.where_ref, bf16[2048,2048]{1,0:T(8,128)(2,1)S(1)} %stage_rows.1.weight_ref, bf16[2048,256]{1,0:T(8,128)(2,1)} %collective-permute-done.15.gating_ref, f32[2048,128]{1,0:T(8,128)S(1)} %broadcast_in_dim.5.scaling_ref, ...), custom_call_target="tpu_custom_call" | custom-call | flops 2147483648 | bytes 8388608 | tf_op jit(solution)/shard_map/project/pallas_call | solution.py:274
  165.0 2.2 %collective-permute-start.18 = (bf16[1024,256]{1,0:T(8,128)(2,1)S(1)}, bf16[1024,256]{1,0:T(8,128)(2,1)S(1)}, u32[]{:S(2)}, u32[]{:S(2)}) collective-permute-start(bf16[1024,256]{1,0:T(8,128)(2,1)S(1)} %add_convert_fusion.2.refs_0_), channel_id=1, source_target_pairs={{2,0},{3,1},{6,4},{7,5},{10,8},{11,9},{14,12},{15,13},{16,18},{17,... | collective-permute-start | bytes 1572872 | tf_op jit(solution)/shard_map/ppermute | solution.py:416
  167.4 4.7 %collective-permute-start.19 = (bf16[1024,256]{1,0:T(8,128)(2,1)S(1)}, bf16[1024,256]{1,0:T(8,128)(2,1)S(1)}, u32[]{:S(2)}, u32[]{:S(2)}) collective-permute-start(bf16[1024,256]{1,0:T(8,128)(2,1)S(1)} %add_convert_fusion.1), channel_id=1, source_target_pairs={{2,16},{3,17},{6,20},{7,21},{10,24},{11,25},{14,28},{15,29},{16,2}... | collective-permute-start | bytes 1572872 | tf_op jit(solution)/shard_map/ppermute | solution.py:422
  172.0 1.3 collective-permute-start.17
  173.3 5.0 %collective-permute-done.18 = bf16[1024,256]{1,0:T(8,128)(2,1)S(1)} collective-permute-done((bf16[1024,256]{1,0:T(8,128)(2,1)S(1)}, bf16[1024,256]{1,0:T(8,128)(2,1)S(1)}, u32[]{:S(2)}, u32[]{:S(2)}) %collective-permute-start.18) | collective-permute-done | bytes 524320 | tf_op jit(solution)/shard_map/ppermute | solution.py:416
  178.3 17.6 %collective-permute-done.19 = bf16[1024,256]{1,0:T(8,128)(2,1)S(1)} collective-permute-done((bf16[1024,256]{1,0:T(8,128)(2,1)S(1)}, bf16[1024,256]{1,0:T(8,128)(2,1)S(1)}, u32[]{:S(2)}, u32[]{:S(2)}) %collective-permute-start.19) | collective-permute-done | bytes 524320 | tf_op jit(solution)/shard_map/ppermute | solution.py:422
  195.9 3.2 %collective-permute-done.17 = bf16[1024,256]{1,0:T(8,128)(2,1)S(1)} collective-permute-done((bf16[1024,256]{1,0:T(8,128)(2,1)S(1)}, bf16[1024,256]{1,0:T(8,128)(2,1)S(1)}, u32[]{:S(2)}, u32[]{:S(2)}) %collective-permute-start.17) | collective-permute-done | bytes 524320 | tf_op jit(solution)/shard_map/ppermute | solution.py:419
  (88 shorter events, 18.8 us)
Async XLA Ops:
  1.9 4.2 %copy-start.22 = (bf16[512,16]{0,1:T(8,128)(2,1)S(1)}, bf16[512,16]{0,1:T(8,128)(2,1)}, u32[]{:S(2)}) copy-start(bf16[512,16]{0,1:T(8,128)(2,1)} %param.14) | copy-start | bytes 49156
  1.9 8.7 %copy-start.1 = (bf16[3,2048,256]{2,1,0:T(8,128)(2,1)S(1)}, bf16[3,2048,256]{2,1,0:T(8,128)(2,1)}, u32[]{:S(2)}) copy-start(bf16[3,2048,256]{2,1,0:T(8,128)(2,1)} %input_ref.3) | copy-start | bytes 9437188
  2.9 7.6 %collective-permute-start = (bf16[32,2048]{1,0:T(8,128)(2,1)S(1)}, bf16[32,2048]{1,0:T(8,128)(2,1)S(1)}, u32[]{:S(2)}, u32[]{:S(2)}) collective-permute-start(bf16[32,2048]{1,0:T(8,128)(2,1)S(1)} %last_tokens.1.refs_0_), channel_id=1, source_target_pairs={{0,4},{4,8},{8,12},{12,16},{16,20},{20,24},{24,28},{1,5},{5,9},{9,... | collective-permute-start | bytes 393224 | tf_op jit(solution)/shard_map/ppermute | solution.py:340
  9.5 6.4 %copy-start.9 = (bf16[192,2048]{1,0:T(8,128)(2,1)}, bf16[192,2048]{1,0:T(8,128)(2,1)S(1)}, u32[]{:S(2)}) copy-start(bf16[192,2048]{1,0:T(8,128)(2,1)S(1)} %get-tuple-element.36.refs_8_) | copy-start | bytes 2359300
  9.5 6.4 %copy-start.17 = (f32[512,128]{1,0:T(8,128)}, f32[512,128]{1,0:T(8,128)S(1)}, u32[]{:S(2)}) copy-start(f32[512,128]{1,0:T(8,128)S(1)} %get-tuple-element.29) | copy-start | bytes 786436
  10.5 37.2 %copy-start.23 = (f32[256]{0:T(256)S(1)}, f32[256]{0:T(256)}, u32[]{:S(2)}) copy-start(f32[256]{0:T(256)} %param.10) | copy-start | bytes 3076
  17.9 9.8 %copy-start.7 = (bf16[192,2048]{1,0:T(8,128)(2,1)S(1)}, bf16[192,2048]{1,0:T(8,128)(2,1)}, u32[]{:S(2)}) copy-start(bf16[192,2048]{1,0:T(8,128)(2,1)} %copy-done.6) | copy-start | bytes 2359300
  17.9 30.0 %copy-start.21 = (f32[16,2048]{1,0:T(8,128)S(1)}, f32[16,2048]{1,0:T(8,128)}, u32[]{:S(2)}) copy-start(f32[16,2048]{1,0:T(8,128)} %filters_ref.1) | copy-start | bytes 393220
  17.9 4.9 %copy-start.18 = (f32[512,128]{1,0:T(8,128)S(1)}, f32[512,128]{1,0:T(8,128)}, u32[]{:S(2)}) copy-start(f32[512,128]{1,0:T(8,128)} %copy-done.17) | copy-start | bytes 786436
  17.9 29.9 %all-to-all-start = ((bf16[8,256,256]{2,1,0:T(8,128)(2,1)}), bf16[8,256,256]{2,1,0:T(8,128)(2,1)S(1)}, u32[]{:S(2)}, u32[]{:S(2)}) async-start(bf16[8,256,256]{2,1,0:T(8,128)(2,1)} %copy-done.5), calls=%async_computation | async-start | bytes 2097152 | tf_op jit(solution)/shard_map/all_to_all | solution.py:350
  23.0 3.1 %collective-permute-start.4 = (f32[1,512]{1,0:T(1,128)S(1)}, f32[1,512]{1,0:T(1,128)S(1)}, u32[]{:S(2)}, u32[]{:S(2)}) collective-permute-start(f32[1,512]{1,0:T(1,128)S(1)} %bitcast.7), channel_id=1, source_target_pairs={{0,3},{1,2},{2,1},{3,0},{4,7},{5,6},{6,5},{7,4},{8,11},{9,10},{10,... | collective-permute-start | bytes 6152 | tf_op jit(solution)/shard_map/ppermute | solution.py:21
  24.9 2.7 %collective-permute-start.3 = (f32[1,512]{1,0:T(1,128)S(1)}, f32[1,512]{1,0:T(1,128)S(1)}, u32[]{:S(2)}, u32[]{:S(2)}) collective-permute-start(f32[1,512]{1,0:T(1,128)S(1)} %bitcast.8), channel_id=1, source_target_pairs={{0,2},{1,3},{2,0},{3,1},{4,6},{5,7},{6,4},{7,5},{8,10},{9,11},{10,... | collective-permute-start | bytes 6152 | tf_op jit(solution)/shard_map/ppermute | solution.py:21
  26.1 1.5 collective-permute-start.2
  27.7 30.5 %collective-permute-start.5 = (bf16[192,2048]{1,0:T(8,128)(2,1)S(1)}, bf16[192,2048]{1,0:T(8,128)(2,1)}, u32[]{:S(2)}, u32[]{:S(2)}) collective-permute-start(bf16[192,2048]{1,0:T(8,128)(2,1)S(1)} %copy-done.7), channel_id=1, source_target_pairs={{0,8},{4,12},{8,0},{12,4},{16,24},{20,28},{24,16},{28,20},{1,9},{5... | collective-permute-start | bytes 2359304 | tf_op jit(solution)/shard_map/ppermute | solution.py:21
  28.9 29.3 %collective-permute-start.1 = (bf16[192,2048]{1,0:T(8,128)(2,1)S(1)}, bf16[192,2048]{1,0:T(8,128)(2,1)}, u32[]{:S(2)}, u32[]{:S(2)}) collective-permute-start(bf16[192,2048]{1,0:T(8,128)(2,1)S(1)} %copy-done.7), channel_id=1, source_target_pairs={{0,4},{4,0},{8,12},{12,8},{16,20},{20,16},{24,28},{28,24},{1,5},{5... | collective-permute-start | bytes 2359304 | tf_op jit(solution)/shard_map/ppermute | solution.py:21
  57.6 35.9 %copy-start.4 = (bf16[8,256,256]{2,1,0:T(8,128)(2,1)S(1)}, bf16[8,256,256]{2,1,0:T(8,128)(2,1)}, u32[]{:S(2)}) copy-start(bf16[8,256,256]{2,1,0:T(8,128)(2,1)} %copy-done.3) | copy-start | bytes 3145732
  58.2 35.2 %all-to-all-start.1 = ((bf16[8,272,256]{2,1,0:T(8,128)(2,1)}), bf16[8,272,256]{2,1,0:T(8,128)(2,1)S(1)}, u32[]{:S(2)}, u32[]{:S(2)}) async-start(bf16[8,272,256]{2,1,0:T(8,128)(2,1)} %convolve.1), calls=%async_computation.1 | async-start | bytes 2228224 | tf_op jit(solution)/shard_map/all_to_all | solution.py:376
  62.4 30.1 %collective-permute-start.7 = (bf16[128,2048]{1,0:T(8,128)(2,1)}, bf16[128,2048]{1,0:T(8,128)(2,1)S(1)}, u32[]{:S(2)}, u32[]{:S(2)}) collective-permute-start(bf16[128,2048]{1,0:T(8,128)(2,1)} %copy-done.11), channel_id=1, source_target_pairs={{0,8},{4,12},{8,0},{12,4},{16,24},{20,28},{24,16},{28,20},{1,9},{5... | collective-permute-start | bytes 1572872 | tf_op jit(solution)/shard_map/ppermute | solution.py:21
  63.6 28.9 %collective-permute-start.6 = (bf16[128,2048]{1,0:T(8,128)(2,1)}, bf16[128,2048]{1,0:T(8,128)(2,1)S(1)}, u32[]{:S(2)}, u32[]{:S(2)}) collective-permute-start(bf16[128,2048]{1,0:T(8,128)(2,1)} %copy-done.11), channel_id=1, source_target_pairs={{0,4},{4,0},{8,12},{12,8},{16,20},{20,16},{24,28},{28,24},{1,5},{5... | collective-permute-start | bytes 1572872 | tf_op jit(solution)/shard_map/ppermute | solution.py:21
  93.9 51.4 %copy-start.12 = (bf16[128,2048]{1,0:T(8,128)(2,1)S(1)}, bf16[128,2048]{1,0:T(8,128)(2,1)}, u32[]{:S(2)}) copy-start(bf16[128,2048]{1,0:T(8,128)(2,1)} %copy-done.11) | copy-start | bytes 1572868
  93.9 17.3 %collective-permute-start.11 = (bf16[192,2048]{1,0:T(8,128)(2,1)}, bf16[192,2048]{1,0:T(8,128)(2,1)S(1)}, u32[]{:S(2)}, u32[]{:S(2)}) collective-permute-start(bf16[192,2048]{1,0:T(8,128)(2,1)} %copy-done.9), channel_id=1, source_target_pairs={{0,4},{4,0},{8,12},{12,8},{16,20},{20,16},{24,28},{28,24},{1,5},{5... | collective-permute-start | bytes 2359304 | tf_op jit(solution)/shard_map/ppermute | solution.py:21
  94.0 33.7 %collective-permute-start.10 = (bf16[192,2048]{1,0:T(8,128)(2,1)}, bf16[192,2048]{1,0:T(8,128)(2,1)}, u32[]{:S(2)}, u32[]{:S(2)}) collective-permute-start(bf16[192,2048]{1,0:T(8,128)(2,1)} %copy-done.9), channel_id=1, source_target_pairs={{0,8},{4,12},{8,0},{12,4},{16,24},{20,28},{24,16},{28,20},{1,9},{5... | collective-permute-start | bytes 2359304 | tf_op jit(solution)/shard_map/ppermute | solution.py:21
  94.1 45.3 %collective-permute-start.8 = (bf16[192,2048]{1,0:T(8,128)(2,1)}, bf16[192,2048]{1,0:T(8,128)(2,1)}, u32[]{:S(2)}, u32[]{:S(2)}) collective-permute-start(bf16[192,2048]{1,0:T(8,128)(2,1)} %collective-permute-done.5.refs_4_), channel_id=1, source_target_pairs={{0,4},{4,0},{8,12},{12,8},{16,20},{20,16},{24,28},{28,24},{1,5},{5... | collective-permute-start | bytes 2359304 | tf_op jit(solution)/shard_map/ppermute | solution.py:21
  95.5 64.6 %collective-permute-start.15 = (bf16[2048,256]{1,0:T(8,128)(2,1)S(1)}, bf16[2048,256]{1,0:T(8,128)(2,1)}, u32[]{:S(2)}, u32[]{:S(2)}) collective-permute-start(bf16[2048,256]{1,0:T(8,128)(2,1)S(1)} %gate.1.gating_ref), channel_id=1, source_target_pairs={{0,16},{4,20},{8,24},{12,28},{16,0},{20,4},{24,8},{28,12},{1,17},{... | collective-permute-start | bytes 3145736 | tf_op jit(solution)/shard_map/ppermute | solution.py:21
  97.9 41.4 %collective-permute-start.9 = (bf16[128,2048]{1,0:T(8,128)(2,1)}, bf16[128,2048]{1,0:T(8,128)(2,1)}, u32[]{:S(2)}, u32[]{:S(2)}) collective-permute-start(bf16[128,2048]{1,0:T(8,128)(2,1)} %copy-done.13), channel_id=1, source_target_pairs={{0,4},{4,0},{8,12},{12,8},{16,20},{20,16},{24,28},{28,24},{1,5},{5... | collective-permute-start | bytes 1572872 | tf_op jit(solution)/shard_map/ppermute | solution.py:21
  112.1 33.2 %collective-permute-start.13 = (bf16[128,2048]{1,0:T(8,128)(2,1)}, bf16[128,2048]{1,0:T(8,128)(2,1)}, u32[]{:S(2)}, u32[]{:S(2)}) collective-permute-start(bf16[128,2048]{1,0:T(8,128)(2,1)} %slice.29), channel_id=1, source_target_pairs={{0,8},{4,12},{8,0},{12,4},{16,24},{20,28},{24,16},{28,20},{1,9},{5... | collective-permute-start | bytes 1572872 | tf_op jit(solution)/shard_map/ppermute | solution.py:21
  128.7 16.2 %collective-permute-start.12 = (bf16[64,2048]{1,0:T(8,128)(2,1)S(1)}, bf16[64,2048]{1,0:T(8,128)(2,1)S(1)}, u32[]{:S(2)}, u32[]{:S(2)}) collective-permute-start(bf16[64,2048]{1,0:T(8,128)(2,1)S(1)} %slice.28), channel_id=1, source_target_pairs={{0,4},{4,0},{8,12},{12,8},{16,20},{20,16},{24,28},{28,24},{1,5},{5... | collective-permute-start | bytes 786440 | tf_op jit(solution)/shard_map/ppermute | solution.py:21
  155.6 4.4 %collective-permute-start.14 = (bf16[1024,256]{1,0:T(8,128)(2,1)S(1)}, bf16[1024,256]{1,0:T(8,128)(2,1)S(1)}, u32[]{:S(2)}, u32[]{:S(2)}) collective-permute-start(bf16[1024,256]{1,0:T(8,128)(2,1)S(1)} %get-tuple-element.38), channel_id=1, source_target_pairs={{0,1},{1,0},{2,3},{3,2},{4,5},{5,4},{6,7},{7,6},{8,9},{9,8},{10,11... | collective-permute-start | bytes 1572872 | tf_op jit(solution)/shard_map/ppermute | solution.py:21
  164.6 2.6 %collective-permute-start.16 = (bf16[1024,256]{1,0:T(8,128)(2,1)S(1)}, bf16[1024,256]{1,0:T(8,128)(2,1)S(1)}, u32[]{:S(2)}, u32[]{:S(2)}) collective-permute-start(bf16[1024,256]{1,0:T(8,128)(2,1)S(1)} %get-tuple-element.40), channel_id=1, source_target_pairs={{0,1},{1,0},{2,3},{3,2},{4,5},{5,4},{6,7},{7,6},{8,9},{9,8},{10,11... | collective-permute-start | bytes 1572872 | tf_op jit(solution)/shard_map/ppermute | solution.py:21
  165.0 13.3 %collective-permute-start.18 = (bf16[1024,256]{1,0:T(8,128)(2,1)S(1)}, bf16[1024,256]{1,0:T(8,128)(2,1)S(1)}, u32[]{:S(2)}, u32[]{:S(2)}) collective-permute-start(bf16[1024,256]{1,0:T(8,128)(2,1)S(1)} %add_convert_fusion.2.refs_0_), channel_id=1, source_target_pairs={{2,0},{3,1},{6,4},{7,5},{10,8},{11,9},{14,12},{15,13},{16,18},{17,... | collective-permute-start | bytes 1572872 | tf_op jit(solution)/shard_map/ppermute | solution.py:416
  167.4 28.5 %collective-permute-start.19 = (bf16[1024,256]{1,0:T(8,128)(2,1)S(1)}, bf16[1024,256]{1,0:T(8,128)(2,1)S(1)}, u32[]{:S(2)}, u32[]{:S(2)}) collective-permute-start(bf16[1024,256]{1,0:T(8,128)(2,1)S(1)} %add_convert_fusion.1), channel_id=1, source_target_pairs={{2,16},{3,17},{6,20},{7,21},{10,24},{11,25},{14,28},{15,29},{16,2}... | collective-permute-start | bytes 1572872 | tf_op jit(solution)/shard_map/ppermute | solution.py:422
  172.0 27.1 %collective-permute-start.17 = (bf16[1024,256]{1,0:T(8,128)(2,1)S(1)}, bf16[1024,256]{1,0:T(8,128)(2,1)S(1)}, u32[]{:S(2)}, u32[]{:S(2)}) collective-permute-start(bf16[1024,256]{1,0:T(8,128)(2,1)S(1)} %add_convert_fusion.1), channel_id=1, source_target_pairs={{0,16},{1,17},{4,20},{5,21},{8,24},{9,25},{12,28},{13,29},{18,2},{... | collective-permute-start | bytes 1572872 | tf_op jit(solution)/shard_map/ppermute | solution.py:419
  (14 other events, 16.3 us)

commit v3 on v2

v3 whole, which is shorter than its diff:
```python
import functools

import jax
import jax.numpy as jnp
from jax import lax
from jax.experimental import pallas as pl
from jax.experimental.pallas import tpu as pltpu
from jax.sharding import PartitionSpec as P

GROUP = 16
TAPS = 7
EPSILON = 1e-06
MIB = 1 << 20
VMEM_LIMIT = 24 * MIB
PROJECT_LIMIT = 56 * MIB
BF16 = jnp.bfloat16
F32 = jnp.float32


def exchange(block, axis, distance):
    count = lax.axis_size(axis)
    return lax.ppermute(block, axis, [(i, i ^ distance) for i in range(count)])


def whole_spec(shape):
    return pl.BlockSpec(shape, lambda *_: (0,) * len(shape))


def tail_kernel(input_ref, out_ref):
    rows = []
    for i in range(3):
        turned = input_ref[i].astype(F32).T
        rows.append(turned[turned.shape[0] - 8 :])
    rows.append(jnp.zeros_like(rows[0]))
    out_ref[...] = jnp.concatenate(rows, axis=0).astype(BF16)


def last_tokens(values):
    width, tokens = values.shape[1:]
    lanes = min(width, 512)
    return pl.pallas_call(
        tail_kernel,
        grid=(width // lanes,),
        in_specs=[pl.BlockSpec((3, lanes, 128), lambda c: (0, c, tokens // 128 - 1))],
        out_specs=pl.BlockSpec((32, lanes), lambda c: (0, c)),
        out_shape=jax.ShapeDtypeStruct((32, width), BF16),
        compiler_params=pltpu.CompilerParams(vmem_limit_bytes=VMEM_LIMIT),
        name="last_tokens",
    )(values)


def merge_kernel(cuts, frozen_ref, down_ref, up_ref, *refs):
    norms_ref, part_refs = refs[-1], refs[-1 - len(cuts) + 1 : -1]
    for part_ref, start, end in zip(part_refs, cuts, cuts[1:]):
        update = jnp.dot(up_ref[start:end, :], down_ref[...], preferred_element_type=F32)
        merged = (frozen_ref[start:end, :].astype(F32) + update).astype(BF16)
        part_ref[...] = merged
        squares = jnp.square(merged.astype(F32))
        norms_ref[start:end, :] = jnp.broadcast_to(
            jnp.sum(squares, axis=1, keepdims=True), (end - start, 128)
        )


def merge(cuts, frozen, down, up, *others):
    rows, width = frozen.shape
    return pl.pallas_call(
        functools.partial(merge_kernel, cuts),
        in_specs=[pl.BlockSpec(memory_space=pltpu.VMEM)] * 3
        + [pl.BlockSpec(memory_space=pl.ANY)] * len(others),
        out_shape=[
            jax.ShapeDtypeStruct((end - start, width), BF16) for start, end in zip(cuts, cuts[1:])
        ]
        + [jax.ShapeDtypeStruct((rows, 128), F32)],
        compiler_params=pltpu.CompilerParams(vmem_limit_bytes=VMEM_LIMIT),
        name="merge",
    )(frozen, down, up, *others)


def featurize_kernel(input_ref, taps_ref, halo_ref, mixture_ref, query_ref, held):
    block, tokens = mixture_ref.shape[1:]

    @pl.loop(0, input_ref.shape[1] // 128)
    def _(tile):
        channels = pl.ds(pl.multiple_of(tile * 128, 128), 128)
        weights = []
        for i in range(3):
            weights.append(taps_ref[i, :, channels])
            held[i, :8, :] = halo_ref[:, channels].astype(F32)[8 * i : 8 * i + 8]
            held[i, 8:, :] = input_ref[i, channels, :].T.astype(F32)
        for place in range(0, tokens, 128):
            sums = []
            for i in range(3):
                total = weights[i][0:1, :] * held[i, 8 + place : 136 + place, :]
                for j in range(1, TAPS):
                    total += weights[i][j : j + 1, :] * held[i, 8 + place - j : 136 + place - j, :]
                sums.append(total)
            columns = slice(place, place + 128)
            mixture = (sums[1] * sums[2]).astype(BF16).T
            query = sums[0].astype(BF16).T
            if block >= 128:
                rows = pl.ds(pl.multiple_of(lax.rem(tile * 128, block), 128), 128)
                mixture_ref[tile * 128 // block, rows, columns] = mixture
                query_ref[tile * 128 // block, rows, columns] = query
            else:
                for n in range(128 // block):
                    rows = slice(n * block, (n + 1) * block)
                    mixture_ref[tile * (128 // block) + n, :, columns] = mixture[rows]
                    query_ref[tile * (128 // block) + n, :, columns] = query[rows]


def featurize(values, taps, halo, ctx_count):
    width, tokens = values.shape[1:]
    shape = jax.ShapeDtypeStruct((ctx_count, width // ctx_count, tokens), BF16)
    return pl.pallas_call(
        featurize_kernel,
        in_specs=[pl.BlockSpec(memory_space=pltpu.VMEM)] * 3,
        out_specs=[pl.BlockSpec(memory_space=pltpu.VMEM)] * 2,
        out_shape=[shape] * 2,
        scratch_shapes=[pltpu.VMEM((3, 8 + tokens, 128), F32)],
        compiler_params=pltpu.CompilerParams(vmem_limit_bytes=VMEM_LIMIT),
        cost_estimate=pl.CostEstimate(
            flops=6 * TAPS * width * tokens, bytes_accessed=10 * MIB, transcendentals=0
        ),
        name="featurize",
    )(values, taps, halo)


def convolve_kernel(filters_ref, skip_ref, mixture_ref, added_ref, out_ref, total_ref):
    ctx_count, block, tokens = mixture_ref.shape
    rows = ctx_count * GROUP
    upper = lax.broadcasted_iota(jnp.int32, (tokens, tokens), 1) >= lax.broadcasted_iota(
        jnp.int32, (tokens, tokens), 0
    )

    @pl.loop(0, filters_ref.shape[0])
    def _(group):
        channels = pl.ds(pl.multiple_of(group * GROUP, GROUP), GROUP)
        here = pl.ds(group, 1)
        mixture = mixture_ref[:, channels, :]
        left = mixture.reshape(rows, tokens)

        def turned(start):
            taps = jnp.broadcast_to(filters_ref[here, pl.ds(start, tokens)], (tokens, tokens))
            return pltpu.roll(taps, 0, 1, stride=1, stride_axis=0)

        def product(count, these, before):
            matrix = jnp.where(upper, these, before).astype(BF16)
            return jnp.dot(left[:count], matrix, preferred_element_type=F32)

        before = turned(0)
        total_ref[:rows, :] = product(rows, before, 0.0)
        if ctx_count <= 8:
            for d in range(1, ctx_count):
                these = turned(d * tokens)
                total_ref[d * GROUP :, :] += product(rows - d * GROUP, these, before)
                before = these
        else:

            @pl.loop(1, ctx_count)
            def _(d):
                start = pl.multiple_of(d * tokens, tokens)
                place = pl.ds(pl.multiple_of(d * GROUP, GROUP), rows)
                matrices = turned(start), turned(start - tokens)
                total_ref[place, :] = total_ref[place, :] + product(rows, *matrices)

        skip = jnp.concatenate([skip_ref[channels, :]] * (tokens // 128), axis=1)
        for j in range(ctx_count):
            total = total_ref[j * GROUP : (j + 1) * GROUP, :]
            out_ref[j, channels, :] = (total + skip * mixture[j].astype(F32)).astype(BF16)

    for j in range(ctx_count):
        out_ref[j, block:, :] = added_ref[...]


def convolve(filters, skip, mixture, added):
    ctx_count, block, tokens = mixture.shape
    total_rows = ctx_count * GROUP * (1 if ctx_count <= 8 else 2)
    return pl.pallas_call(
        convolve_kernel,
        in_specs=[pl.BlockSpec(memory_space=pltpu.VMEM)] * 4,
        out_specs=pl.BlockSpec(memory_space=pltpu.VMEM),
        scratch_shapes=[pltpu.VMEM((total_rows, tokens), F32)],
        out_shape=jax.ShapeDtypeStruct((ctx_count, block + GROUP, tokens), BF16),
        compiler_params=pltpu.CompilerParams(vmem_limit_bytes=VMEM_LIMIT),
        cost_estimate=pl.CostEstimate(
            flops=8 * block * (ctx_count * tokens) ** 2, bytes_accessed=20 * MIB, transcendentals=0
        ),
        name="convolve",
    )(filters, skip, mixture, added)


def gate_kernel(query_ref, summed_ref, out_ref):
    ctx_count, block = query_ref.shape[:2]
    for d in range(ctx_count):
        product = query_ref[d].astype(F32) * summed_ref[d, :block, :].astype(F32)
        out_ref[d * block : (d + 1) * block, :] = product.astype(BF16)


def gate(query, summed):
    ctx_count, block, tokens = query.shape
    return pl.pallas_call(
        gate_kernel,
        in_specs=[pl.BlockSpec(memory_space=pltpu.VMEM)] * 2,
        out_specs=pl.BlockSpec(memory_space=pltpu.VMEM),
        out_shape=jax.ShapeDtypeStruct((ctx_count * block, tokens), BF16),
        compiler_params=pltpu.CompilerParams(vmem_limit_bytes=VMEM_LIMIT),
        name="gate",
    )(query, summed)


def project_kernel(layout, places, where_ref, gating_ref, far_gating_ref, *refs):
    arrays = len(layout)
    weight_refs = refs[:arrays]
    keep_refs, far_keep_refs = refs[arrays : arrays + 2]
    send_ref, held, gating_held, sems = refs[arrays + 2 :]
    low, core = where_ref[1], where_ref[2]
    tokens = gating_ref.shape[1]
    block = 2 * keep_refs.shape[0] // places
    copies, at = [], 0
    for n, source in enumerate((gating_ref, far_gating_ref)):
        target = gating_held.at[:, pl.ds(n * tokens, tokens)]
        copies.append(pltpu.make_async_copy(source, target, sems.at[n]))
    for n, weight_ref in enumerate(weight_refs):
        rows = weight_ref.shape[0]
        target = held.at[pl.ds(at, rows), :]
        copies.append(pltpu.make_async_copy(weight_ref, target, sems.at[n + 2]))
        at += rows
    for copy in copies:
        copy.start()
    copies[0].wait()
    copies[1].wait()
    pending, first, at = [], 0, 0
    total_rows = held.shape[0]
    for n, (copy, entries) in enumerate(zip(copies[2:], layout)):
        copy.wait()
        for entry in entries:
            pending.append((at, entry))
            at += entry[1]
        if at - first < total_rows // 4 and n + 1 < arrays:
            continue
        total = jnp.dot(held[first:at, :], gating_held[...], preferred_element_type=F32)
        for begin, (offset, rows, p) in pending:
            place = jnp.bitwise_xor(low, p)
            mine = place // (places // 2) == core
            start = (place & (places // 2 - 1)) * block + offset
            target = pl.ds(pl.multiple_of(start, 16), rows)
            piece = total[begin - first : begin - first + rows]

            @pl.when(mine)
            def _():
                keep_refs[target, :] = piece[:, :tokens]
                far_keep_refs[target, :] = piece[:, tokens:]

            @pl.when(jnp.logical_not(mine))
            def _():
                send_ref[0, target, :] = piece[:, :tokens].astype(BF16)
                send_ref[1, target, :] = piece[:, tokens:].astype(BF16)

        pending, first = [], at


def project(where, places, layout, weights, gating, far_gating):
    width, tokens = gating.shape
    total_rows = sum(weight.shape[0] for weight in weights)
    out = jax.ShapeDtypeStruct((total_rows // 2, tokens), F32)
    sent = jax.ShapeDtypeStruct((2, total_rows // 2, tokens), BF16)
    return pl.pallas_call(
        functools.partial(project_kernel, layout, places),
        grid_spec=pltpu.PrefetchScalarGridSpec(
            num_scalar_prefetch=1,
            grid=(1,),
            in_specs=[pl.BlockSpec(memory_space=pl.ANY)] * (2 + len(weights)),
            out_specs=[pl.BlockSpec(memory_space=pltpu.VMEM)] * 3,
            scratch_shapes=[
                pltpu.VMEM((total_rows, width), BF16),
                pltpu.VMEM((width, 2 * tokens), BF16),
                pltpu.SemaphoreType.DMA((len(weights) + 2,)),
            ],
        ),
        out_shape=[out, out, sent],
        compiler_params=pltpu.CompilerParams(vmem_limit_bytes=PROJECT_LIMIT),
        cost_estimate=pl.CostEstimate(
            flops=4 * total_rows * tokens * width, bytes_accessed=10 * MIB, transcendentals=0
        ),
        name="project",
    )(where, gating, far_gating, *weights)


def after(value, *others):
    return lax.optimization_barrier((value, *others))[0]


def rows_with(norms, tokens):
    flat = norms.reshape(-1)
    flat = jnp.pad(flat, (0, -flat.shape[0] % tokens)).reshape(-1, tokens)
    pieces = []
    for _ in range(3):
        piece = lax.optimization_barrier(flat.astype(BF16))
        pieces.append(piece)
        flat = flat - piece.astype(F32)
    added = jnp.concatenate(pieces)
    return jnp.pad(added, ((0, GROUP - added.shape[0]), (0, 0)))


def norms_of(received, block, rows):
    ctx_count, _, tokens = received.shape
    lines = -(-rows // tokens)
    added = received[:, block : block + 3 * lines].astype(F32)
    added = added.reshape(ctx_count, 3, lines * tokens)
    return (added[:, 0] + (added[:, 1] + added[:, 2]))[:, :rows].reshape(ctx_count * rows)


def on_device(
    query_key_value_input,
    featurizer_weights,
    channel_skip_scale,
    group_long_filters,
    frozen_weight,
    down_update_weight,
    up_update_weight,
    magnitude,
):
    width, tokens = query_key_value_input.shape[1:]
    ctx_count = lax.axis_size("ctx")
    tp_count = lax.axis_size("tp")
    half = ctx_count // 2
    rows = frozen_weight.shape[0]
    me = lax.axis_index("ctx")
    tp_index = lax.axis_index("tp")
    low = jnp.bitwise_and(me, half - 1)
    high = me // half
    core = jnp.bitwise_and(tp_index, 1)
    upper_tp = tp_index // 2
    where = jnp.stack([me, low, core, high]).astype(jnp.int32)

    tail = last_tokens(query_key_value_input)
    halo = lax.ppermute(tail, "ctx", [(i, i + 1) for i in range(ctx_count - 1)])

    mixture, query = featurize(query_key_value_input, featurizer_weights, halo, ctx_count)
    own_mixture = mixture
    mixture = lax.all_to_all(own_mixture, "ctx", split_axis=0, concat_axis=0, tiled=True)

    cuts = (0, rows * 3 // 8 // 16 * 16, rows * 5 // 8 // 16 * 16, rows)
    frozen = after(frozen_weight, own_mixture)
    *parts, norms = merge(cuts, frozen, down_update_weight, up_update_weight)
    norms = norms[:, 0][None, :]
    norms = norms + sum(exchange(norms, "tp", distance) for distance in range(1, tp_count))

    distances = []
    while 1 << len(distances) < half:
        distances.insert(0, 1 << len(distances))
    coarse, rest = distances[0], distances[1:]
    pieces, layout = [], []

    def finish(held, order, path, offset, length):
        for distance in path[:-1]:
            received = exchange(held, "ctx", distance)
            held = jnp.concatenate([held, received], axis=0)
            order = order + [index + distance for index in order]
        received = exchange(held, "ctx", path[-1])
        pieces.extend([held, received])
        layout.append(tuple((offset, length, index) for index in order))
        layout.append(tuple((offset, length, index + path[-1]) for index in order))
        return received

    part = parts[0]
    far_part = exchange(part, "ctx", coarse)
    got = finish(part, [0], rest, 0, cuts[1])
    block = width // ctx_count
    skip = jnp.broadcast_to(channel_skip_scale[:, None], (block, 128))
    summed = convolve(group_long_filters, skip, mixture, rows_with(norms, tokens))
    sent = after(summed, far_part, got)
    received = lax.all_to_all(sent, "ctx", split_axis=0, concat_axis=0, tiled=True)
    part = after(parts[1], sent)
    other_part = exchange(part, "ctx", coarse)
    got = finish(part, [0], rest, cuts[1], cuts[2] - cuts[1])
    gating = gate(after(query, received, got, other_part), received)
    far_gating = exchange(gating, "ctx", half)
    owned = half * rows // 2
    norms_here = norms_of(after(received, gating), block, rows)
    norms_here = lax.dynamic_slice_in_dim(norms_here, tp_index * owned, owned)
    magnitude_here = lax.dynamic_slice_in_dim(magnitude, tp_index * owned, owned)
    scaling = magnitude_here / jnp.sqrt(norms_here + EPSILON)

    finish(after(far_part, scaling), [coarse], rest, 0, cuts[1])
    finish(after(other_part, scaling), [coarse], rest, cuts[1], cuts[2] - cuts[1])
    part = after(parts[2], scaling)
    late_start, late_rows = cuts[2], cuts[3] - cuts[2]
    if len(rest) == 1:
        upper = late_rows // 3 // 16 * 16
        coarse_part, fine_part = exchange(part, "ctx", coarse), exchange(part, "ctx", rest[0])
        last = exchange(coarse_part[:upper], "ctx", rest[0])
        other = exchange(fine_part[upper:], "ctx", coarse)
        pieces += [part, coarse_part, fine_part, last, other]
        layout += [((late_start, late_rows, index),) for index in (0, coarse, rest[0])]
        layout.append(((late_start, upper, coarse + rest[0]),))
        layout.append(((late_start + upper, late_rows - upper, coarse + rest[0]),))
    else:
        finish(part, [0], distances, late_start, late_rows)
    layout = tuple(layout)

    def place(h, l, y, c):
        return (h * half + l) * tp_count + y * 2 + c

    sites = [(h, l, c) for h in range(2) for l in range(half) for c in range(2)]

    def send_on(value, route):
        pairs = [route(h, l, c) for h, l, c in sites]
        return lax.ppermute(value, ("ctx", "tp"), [(place(*a), place(*b)) for a, b in pairs])

    near, far, sent = project(where, half, layout, pieces, gating, far_gating)
    received = exchange(sent, "tp", 1).astype(F32)
    far = far + received[1]
    split = owned // 2
    mine = lax.dynamic_slice_in_dim(far, upper_tp * split, split)
    theirs = lax.dynamic_slice_in_dim(far, (1 - upper_tp) * split, split).astype(BF16)
    far = (mine + exchange(theirs, "tp", 2).astype(F32)).astype(BF16)
    straight = send_on(far, lambda h, l, c: ((h, l, h, c), (1 - h, l, h, c)))
    diagonal = send_on(far, lambda h, l, c: ((h, l, 1 - h, c), (1 - h, l, h, c)))
    near = (near + received[0]).astype(BF16)
    from_near = send_on(near, lambda h, l, c: ((h, l, 1 - h, c), (h, l, h, c)))
    from_far = jnp.where(
        upper_tp == 0,
        jnp.concatenate([straight, diagonal], axis=0),
        jnp.concatenate([diagonal, straight], axis=0),
    )
    near = near.astype(F32) + from_near.astype(F32)
    out = jnp.where(upper_tp == high, near, from_far.astype(F32))
    return (out * scaling[:, None]).astype(BF16)


def solution(mesh):
    placed = (
        P(None, "tp", "ctx"),
        P(None, None, "tp"),
        P(("tp", "ctx")),
        P(("tp", "ctx"), None),
        P("ctx", "tp"),
        P(None, "tp"),
        P("ctx", None),
        P(),
    )
    return jax.shard_map(
        on_device, mesh=mesh, in_specs=placed, out_specs=P("tp", "ctx"), check_vma=False
    )
```

time: 202 us -> 190 us (0.941)
  local copies, waits for them, and re-layouts: 15.3 us -> 6.8 us
  waiting for transfers between devices: 118 us -> 114 us
    ppermute x3, waiting for transfers between devices: 25.8 us -> 13.6 us  [send_on(): lax.ppermute(value, ('ctx', 'tp'), [(place(*a), place(*b)) for a, b in pa...]
    ppermute x16, waiting for transfers between devices: 73.7 us -> 81.1 us  [exchange(): return lax.ppermute(block, axis, [(i, i ^ distance) for i in range(count)])]
    unnamed x49 -> x41, local copies, waits for them, and re-layouts: 12.8 us -> 6.44 us
    pallas_call x4 -> x3, Pallas kernels: 17.8 us -> 14 us  [the longest x1 8.63 us: convolve(): pl.pallas_call(convolve_kernel, in_specs=[pl.BlockSpec(memory_space=pltpu...]
    ppermute x1, waiting for transfers between devices: 0.01 us -> 3.07 us  [on_device(): halo = lax.ppermute(tail, 'ctx', [(i, i + 1) for i in range(ctx_count - 1)])]
    all_to_all x1, waiting for transfers between devices: 18.6 us -> 16.1 us  [on_device(): lax.all_to_all(own_mixture, 'ctx', split_axis=0, concat_axis=0, tiled=True)]
    pallas_call x2 -> x1, Pallas kernels: 7.76 us -> 9.95 us  [project(): pl.pallas_call(functools.partial(project_kernel, layout, places), grid_sp...]
  transfers between devices with their start and end apart: 22 -> 22, of which waited for: 13 -> 15; matrix products, arithmetic and copies ran while one was open for 2% -> 1% of each run, Pallas kernels for 8% -> 5%
where the time goes in v3:
time: 190 us; the launch traced here: 188 us
  waiting for transfers between devices  114 us (60%)
  starting transfers between devices  37.7 us (20%)
  Pallas kernels  26.2 us (14%)
  local copies, waits for them, and re-layouts  6.8 us (4%)
  other arithmetic  3.11 us (2%)
    ppermute x16, waiting for transfers between devices, exchange(): return lax.ppermute(block, axis, [(i, i ^ distance) for i in range(count)])  81.1 us
    ppermute x16, starting transfers between devices, exchange(): return lax.ppermute(block, axis, [(i, i ^ distance) for i in range(count)])  16.2 us
    all_to_all x1, waiting for transfers between devices, on_device(): lax.all_to_all(own_mixture, 'ctx', split_axis=0, concat_axis=0, tiled=True)  16.1 us
    ppermute x3, waiting for transfers between devices, send_on(): lax.ppermute(value, ('ctx', 'tp'), [(place(*a), place(*b)) for a, b in pa...  13.6 us
    pallas_call x1, Pallas kernels, project(): pl.pallas_call(functools.partial(project_kernel, layout, places), grid_sp...  9.95 us
    pallas_call x1, Pallas kernels, convolve(): pl.pallas_call(convolve_kernel, in_specs=[pl.BlockSpec(memory_space=pltpu...  8.63 us
    ppermute x3, starting transfers between devices, send_on(): lax.ppermute(value, ('ctx', 'tp'), [(place(*a), place(*b)) for a, b in pa...  7.61 us
    unnamed x41, local copies, waits for them, and re-layouts  6.44 us
  transfers between devices with their start and end apart: 22, of which 15 were waited for; matrix products, arithmetic and copies ran while one was open for 1% of the time, Pallas kernels for 5%

profile of v3, /device:TPU:7, one launch (start us, length us, event | category | flops | bytes accessed | tf_op | source)
XLA Modules:
  0.0 188.0 jit_solution(13717393235279882964)
XLA Ops:
  0.0 1.9 %copy-done = bf16[3,2048,256]{2,1,0:T(8,128)(2,1)S(1)} copy-done((bf16[3,2048,256]{2,1,0:T(8,128)(2,1)S(1)}, bf16[3,2048,256]{2,1,0:T(8,128)(2,1)}, u32[]{:S(2)}) %copy-start) | copy-done | bytes 3145752
  3.0 3.3 %collective-permute-start = (bf16[32,2048]{1,0:T(8,128)(2,1)S(1)}, bf16[32,2048]{1,0:T(8,128)(2,1)S(1)}, u32[]{:S(2)}, u32[]{:S(2)}) collective-permute-start(bf16[32,2048]{1,0:T(8,128)(2,1)S(1)} %last_tokens.1), channel_id=1, source_target_pairs={{0,4},{4,8},{8,12},{12,16},{16,20},{20,24},{24,28},{1,5},{5,9},{9,... | collective-permute-start | bytes 393224 | tf_op jit(solution)/shard_map/ppermute | solution.py:337
  6.3 3.1 %collective-permute-done.halo_ref = bf16[32,2048]{1,0:T(8,128)(2,1)S(1)} collective-permute-done((bf16[32,2048]{1,0:T(8,128)(2,1)S(1)}, bf16[32,2048]{1,0:T(8,128)(2,1)S(1)}, u32[]{:S(2)}, u32[]{:S(2)}) %collective-permute-start) | collective-permute-done | bytes 131104 | tf_op jit(solution)/shard_map/ppermute | solution.py:337
  9.4 5.1 %featurize.1 = (bf16[8,256,256]{2,1,0:T(8,128)(2,1)S(1)}, bf16[8,256,256]{2,1,0:T(8,128)(2,1)S(1)}) custom-call(bf16[3,2048,256]{2,1,0:T(8,128)(2,1)S(1)} %copy-done, f32[3,7,2048]{2,1,0:T(8,128)S(1)} %copy-done.4, bf16[32,2048]{1,0:T(8,128)(2,1)S(1)} %collective-permute-done.halo_ref), custom_call_target="tpu_custom_call" | custom-call | flops 22020096 | bytes 10485760 | tf_op jit(solution)/shard_map/featurize/pallas_call | solution.py:114
  15.5 5.9 %all-to-all-start = ((bf16[8,256,256]{2,1,0:T(8,128)(2,1)}), bf16[8,256,256]{2,1,0:T(8,128)(2,1)}, u32[]{:S(2)}, u32[]{:S(2)}) async-start(bf16[8,256,256]{2,1,0:T(8,128)(2,1)} %copy-done.3), calls=%async_computation | async-start | bytes 2097152 | tf_op jit(solution)/shard_map/all_to_all | solution.py:341
  21.5 1.2 merge.1
  24.5 2.1 %collective-permute-start.1 = (f32[1,512]{1,0:T(1,128)S(1)}, f32[1,512]{1,0:T(1,128)S(1)}, u32[]{:S(2)}, u32[]{:S(2)}) collective-permute-start(f32[1,512]{1,0:T(1,128)S(1)} %bitcast.17), channel_id=1, source_target_pairs={{0,1},{1,0},{2,3},{3,2},{4,5},{5,4},{6,7},{7,6},{8,9},{9,8},{10,11... | collective-permute-start | bytes 6152 | tf_op jit(solution)/shard_map/ppermute | solution.py:22
  26.8 1.4 collective-permute-start.3
  28.2 1.2 collective-permute-start.4
  30.3 16.1 %all-to-all-done.mixture_ref = bf16[8,256,256]{2,1,0:T(8,128)(2,1)} async-done(((bf16[8,256,256]{2,1,0:T(8,128)(2,1)}), bf16[8,256,256]{2,1,0:T(8,128)(2,1)}, u32[]{:S(2)}, u32[]{:S(2)}) %all-to-all-start) | async-done | bytes 1048608 | tf_op jit(solution)/shard_map/all_to_all | solution.py:341
  46.5 8.6 %convolve.1 = bf16[8,272,256]{2,1,0:T(8,128)(2,1)} custom-call(f32[16,2048]{1,0:T(8,128)S(1)} %copy-done.9, f32[256,128]{1,0:T(8,128)S(1)} %broadcast_in_dim.2.skip_ref, bf16[8,256,256]{2,1,0:T(8,128)(2,1)} %all-to-all-done.mixture_ref, bf16[16,256]{1,0:T(8,128)(2,1)S(1)} %fusion.8.added_ref), custom_call_target="tpu_custom_call" | custom-call | flops 8589934592 | bytes 20971520 | tf_op jit(solution)/shard_map/convolve/pallas_call | solution.py:178
  55.2 1.3 collective-permute-done.4.refs_4_
  57.5 4.6 %all-to-all-start.1 = ((bf16[8,272,256]{2,1,0:T(8,128)(2,1)}), bf16[8,272,256]{2,1,0:T(8,128)(2,1)S(1)}, u32[]{:S(2)}, u32[]{:S(2)}) async-start(bf16[8,272,256]{2,1,0:T(8,128)(2,1)} %convolve.1), calls=%async_computation.1 | async-start | bytes 2228224 | tf_op jit(solution)/shard_map/all_to_all | solution.py:373
  62.2 1.3 collective-permute-start.7
  63.5 20.6 %collective-permute-done.6.refs_3_ = bf16[128,2048]{1,0:T(8,128)(2,1)S(1)} collective-permute-done((bf16[128,2048]{1,0:T(8,128)(2,1)S(1)}, bf16[128,2048]{1,0:T(8,128)(2,1)S(1)}, u32[]{:S(2)}, u32[]{:S(2)}) %collective-permute-start.6) | collective-permute-done | bytes 524320 | tf_op jit(solution)/shard_map/ppermute | solution.py:22
  84.1 8.2 %collective-permute-done.7.refs_6_ = bf16[128,2048]{1,0:T(8,128)(2,1)} collective-permute-done((bf16[128,2048]{1,0:T(8,128)(2,1)S(1)}, bf16[128,2048]{1,0:T(8,128)(2,1)}, u32[]{:S(2)}, u32[]{:S(2)}) %collective-permute-start.7) | collective-permute-done | bytes 524320 | tf_op jit(solution)/shard_map/ppermute | solution.py:22
  93.4 3.0 %collective-permute-start.8 = (bf16[2048,256]{1,0:T(8,128)(2,1)S(1)}, bf16[2048,256]{1,0:T(8,128)(2,1)}, u32[]{:S(2)}, u32[]{:S(2)}) collective-permute-start(bf16[2048,256]{1,0:T(8,128)(2,1)S(1)} %gate.1.gating_ref), channel_id=1, source_target_pairs={{0,16},{4,20},{8,24},{12,28},{16,0},{20,4},{24,8},{28,12},{1,17},{... | collective-permute-start | bytes 3145736 | tf_op jit(solution)/shard_map/ppermute | solution.py:22
  97.9 12.9 %collective-permute-done.12.refs_10_ = bf16[192,2048]{1,0:T(8,128)(2,1)S(1)} collective-permute-done((bf16[192,2048]{1,0:T(8,128)(2,1)}, bf16[192,2048]{1,0:T(8,128)(2,1)S(1)}, u32[]{:S(2)}, u32[]{:S(2)}) %collective-permute-start.12) | collective-permute-done | bytes 786464 | tf_op jit(solution)/shard_map/ppermute | solution.py:22
  110.9 18.0 %collective-permute-done.11.refs_9_ = bf16[192,2048]{1,0:T(8,128)(2,1)S(1)} collective-permute-done((bf16[192,2048]{1,0:T(8,128)(2,1)}, bf16[192,2048]{1,0:T(8,128)(2,1)S(1)}, u32[]{:S(2)}, u32[]{:S(2)}) %collective-permute-start.11) | collective-permute-done | bytes 786464 | tf_op jit(solution)/shard_map/ppermute | solution.py:22
  129.8 2.3 %collective-permute-start.13 = (bf16[64,2048]{1,0:T(8,128)(2,1)S(1)}, bf16[64,2048]{1,0:T(8,128)(2,1)S(1)}, u32[]{:S(2)}, u32[]{:S(2)}) collective-permute-start(bf16[64,2048]{1,0:T(8,128)(2,1)S(1)} %slice.39), channel_id=1, source_target_pairs={{0,4},{4,0},{8,12},{12,8},{16,20},{20,16},{24,28},{28,24},{1,5},{5... | collective-permute-start | bytes 786440 | tf_op jit(solution)/shard_map/ppermute | solution.py:22
  132.7 6.2 %collective-permute-done.10.refs_7_ = bf16[128,2048]{1,0:T(8,128)(2,1)S(1)} collective-permute-done((bf16[128,2048]{1,0:T(8,128)(2,1)}, bf16[128,2048]{1,0:T(8,128)(2,1)S(1)}, u32[]{:S(2)}, u32[]{:S(2)}) %collective-permute-start.10) | collective-permute-done | bytes 524320 | tf_op jit(solution)/shard_map/ppermute | solution.py:22
  138.9 5.6 %collective-permute-done.13.refs_11_ = bf16[64,2048]{1,0:T(8,128)(2,1)S(1)} collective-permute-done((bf16[64,2048]{1,0:T(8,128)(2,1)S(1)}, bf16[64,2048]{1,0:T(8,128)(2,1)S(1)}, u32[]{:S(2)}, u32[]{:S(2)}) %collective-permute-start.13) | collective-permute-done | bytes 262176 | tf_op jit(solution)/shard_map/ppermute | solution.py:22
  145.6 9.9 %project.1 = (f32[1024,256]{1,0:T(8,128)}, f32[1024,256]{1,0:T(8,128)}, bf16[2,1024,256]{2,1,0:T(8,128)(2,1)}) custom-call(s32[4]{0:T(128)} %pad_add_fusion.where_ref, bf16[2048,256]{1,0:T(8,128)(2,1)} %copy-done.2, bf16[2048,256]{1,0:T(8,128)(2,1)} %collective-permute-done.8.far_gating_ref, bf16[192,2048]{1,0:T(8,128)(2,1)} %get-tuple-element.26.refs_0_, ...), custom_call_target="tpu_custom_call" | custom-call | flops 4294967296 | bytes 10485760 | tf_op jit(solution)/shard_map/project/pallas_call | solution.py:267
  155.5 2.5 %collective-permute-start.15 = (bf16[2,1024,256]{2,1,0:T(8,128)(2,1)}, bf16[2,1024,256]{2,1,0:T(8,128)(2,1)S(1)}, u32[]{:S(2)}, u32[]{:S(2)}) collective-permute-start(bf16[2,1024,256]{2,1,0:T(8,128)(2,1)} %get-tuple-element.37), channel_id=1, source_target_pairs={{0,1},{1,0},{2,3},{3,2},{4,5},{5,4},{6,7},{7,6},{8,9},{9,8},{10,11... | collective-permute-start | bytes 3145736 | tf_op jit(solution)/shard_map/ppermute | solution.py:22
  158.0 2.5 %collective-permute-done.15 = bf16[2,1024,256]{2,1,0:T(8,128)(2,1)S(1)} collective-permute-done((bf16[2,1024,256]{2,1,0:T(8,128)(2,1)}, bf16[2,1024,256]{2,1,0:T(8,128)(2,1)S(1)}, u32[]{:S(2)}, u32[]{:S(2)}) %collective-permute-start.15) | collective-permute-done | bytes 1048608 | tf_op jit(solution)/shard_map/ppermute | solution.py:22
  161.4 3.2 %collective-permute-start.16 = (bf16[1024,256]{1,0:T(8,128)(2,1)S(1)}, bf16[1024,256]{1,0:T(8,128)(2,1)S(1)}, u32[]{:S(2)}, u32[]{:S(2)}) collective-permute-start(bf16[1024,256]{1,0:T(8,128)(2,1)S(1)} %get-tuple-element.40), channel_id=1, source_target_pairs={{2,0},{3,1},{6,4},{7,5},{10,8},{11,9},{14,12},{15,13},{16,18},{17,... | collective-permute-start | bytes 1572872 | tf_op jit(solution)/shard_map/ppermute | solution.py:409
  164.6 4.1 %collective-permute-done.17 = bf16[512,256]{1,0:T(8,128)(2,1)S(1)} collective-permute-done((bf16[512,256]{1,0:T(8,128)(2,1)S(1)}, bf16[512,256]{1,0:T(8,128)(2,1)S(1)}, u32[]{:S(2)}, u32[]{:S(2)}) %collective-permute-start.17) | collective-permute-done | bytes 262176 | tf_op jit(solution)/shard_map/ppermute | solution.py:22
  168.8 1.3 collective-permute-start.18
  170.1 3.1 %collective-permute-start.19 = (bf16[512,256]{1,0:T(8,128)(2,1)S(1)}, bf16[512,256]{1,0:T(8,128)(2,1)S(1)}, u32[]{:S(2)}, u32[]{:S(2)}) collective-permute-start(bf16[512,256]{1,0:T(8,128)(2,1)S(1)} %add_convert_fusion), channel_id=1, source_target_pairs={{2,16},{3,17},{6,20},{7,21},{10,24},{11,25},{14,28},{15,29},{16,2}... | collective-permute-start | bytes 786440 | tf_op jit(solution)/shard_map/ppermute | solution.py:409
  173.3 11.4 %collective-permute-done.18 = bf16[512,256]{1,0:T(8,128)(2,1)S(1)} collective-permute-done((bf16[512,256]{1,0:T(8,128)(2,1)S(1)}, bf16[512,256]{1,0:T(8,128)(2,1)S(1)}, u32[]{:S(2)}, u32[]{:S(2)}) %collective-permute-start.18) | collective-permute-done | bytes 262176 | tf_op jit(solution)/shard_map/ppermute | solution.py:409
  184.7 2.2 %collective-permute-done.19 = bf16[512,256]{1,0:T(8,128)(2,1)S(1)} collective-permute-done((bf16[512,256]{1,0:T(8,128)(2,1)S(1)}, bf16[512,256]{1,0:T(8,128)(2,1)S(1)}, u32[]{:S(2)}, u32[]{:S(2)}) %collective-permute-start.19) | collective-permute-done | bytes 262176 | tf_op jit(solution)/shard_map/ppermute | solution.py:409
  186.9 1.1 multiply_convert_fusion
  (79 shorter events, 12.3 us)
Async XLA Ops:
  1.9 7.5 %copy-start.4 = (f32[3,7,2048]{2,1,0:T(8,128)S(1)}, f32[3,7,2048]{2,1,0:T(8,128)}, u32[]{:S(2)}) copy-start(f32[3,7,2048]{2,1,0:T(8,128)} %taps_ref.1) | copy-start | bytes 516100
  2.9 18.5 %copy-start.14 = (bf16[512,16]{0,1:T(8,128)(2,1)S(1)}, bf16[512,16]{0,1:T(8,128)(2,1)}, u32[]{:S(2)}) copy-start(bf16[512,16]{0,1:T(8,128)(2,1)} %param.14) | copy-start | bytes 49156
  2.9 18.6 %copy-start.1 = (bf16[512,2048]{1,0:T(8,128)(2,1)S(1)}, bf16[512,2048]{1,0:T(8,128)(2,1)}, u32[]{:S(2)}) copy-start(bf16[512,2048]{1,0:T(8,128)(2,1)} %frozen_ref) | copy-start | bytes 6291460
  3.0 18.6 %copy-start.5 = (bf16[16,2048]{1,0:T(8,128)(2,1)S(1)}, bf16[16,2048]{1,0:T(8,128)(2,1)}, u32[]{:S(2)}) copy-start(bf16[16,2048]{1,0:T(8,128)(2,1)} %down_ref.1) | copy-start | bytes 196612
  3.0 6.4 %collective-permute-start = (bf16[32,2048]{1,0:T(8,128)(2,1)S(1)}, bf16[32,2048]{1,0:T(8,128)(2,1)S(1)}, u32[]{:S(2)}, u32[]{:S(2)}) collective-permute-start(bf16[32,2048]{1,0:T(8,128)(2,1)S(1)} %last_tokens.1), channel_id=1, source_target_pairs={{0,4},{4,8},{8,12},{12,16},{16,20},{20,24},{24,28},{1,5},{5,9},{9,... | collective-permute-start | bytes 393224 | tf_op jit(solution)/shard_map/ppermute | solution.py:337
  15.5 31.0 %copy-start.15 = (f32[256]{0:T(256)S(1)}, f32[256]{0:T(256)}, u32[]{:S(2)}) copy-start(f32[256]{0:T(256)} %param.10) | copy-start | bytes 3076
  15.5 31.1 %copy-start.9 = (f32[16,2048]{1,0:T(8,128)S(1)}, f32[16,2048]{1,0:T(8,128)}, u32[]{:S(2)}) copy-start(f32[16,2048]{1,0:T(8,128)} %filters_ref.1) | copy-start | bytes 393220
  15.5 30.9 %all-to-all-start = ((bf16[8,256,256]{2,1,0:T(8,128)(2,1)}), bf16[8,256,256]{2,1,0:T(8,128)(2,1)}, u32[]{:S(2)}, u32[]{:S(2)}) async-start(bf16[8,256,256]{2,1,0:T(8,128)(2,1)} %copy-done.3), calls=%async_computation | async-start | bytes 2097152 | tf_op jit(solution)/shard_map/all_to_all | solution.py:341
  24.5 5.2 %collective-permute-start.1 = (f32[1,512]{1,0:T(1,128)S(1)}, f32[1,512]{1,0:T(1,128)S(1)}, u32[]{:S(2)}, u32[]{:S(2)}) collective-permute-start(f32[1,512]{1,0:T(1,128)S(1)} %bitcast.17), channel_id=1, source_target_pairs={{0,1},{1,0},{2,3},{3,2},{4,5},{5,4},{6,7},{7,6},{8,9},{9,8},{10,11... | collective-permute-start | bytes 6152 | tf_op jit(solution)/shard_map/ppermute | solution.py:22
  26.6 3.1 %collective-permute-start.2 = (f32[1,512]{1,0:T(1,128)S(1)}, f32[1,512]{1,0:T(1,128)S(1)}, u32[]{:S(2)}, u32[]{:S(2)}) collective-permute-start(f32[1,512]{1,0:T(1,128)S(1)} %bitcast.18), channel_id=1, source_target_pairs={{0,2},{1,3},{2,0},{3,1},{4,6},{5,7},{6,4},{7,5},{8,10},{9,11},{10,... | collective-permute-start | bytes 6152 | tf_op jit(solution)/shard_map/ppermute | solution.py:22
  26.8 3.4 %collective-permute-start.3 = (f32[1,512]{1,0:T(1,128)S(1)}, f32[1,512]{1,0:T(1,128)S(1)}, u32[]{:S(2)}, u32[]{:S(2)}) collective-permute-start(f32[1,512]{1,0:T(1,128)S(1)} %bitcast.19), channel_id=1, source_target_pairs={{0,3},{1,2},{2,1},{3,0},{4,7},{5,6},{6,5},{7,4},{8,11},{9,10},{10,... | collective-permute-start | bytes 6152 | tf_op jit(solution)/shard_map/ppermute | solution.py:22
  28.2 28.3 %collective-permute-start.4 = (bf16[192,2048]{1,0:T(8,128)(2,1)}, bf16[192,2048]{1,0:T(8,128)(2,1)}, u32[]{:S(2)}, u32[]{:S(2)}) collective-permute-start(bf16[192,2048]{1,0:T(8,128)(2,1)} %get-tuple-element.26.refs_0_), channel_id=1, source_target_pairs={{0,8},{4,12},{8,0},{12,4},{16,24},{20,28},{24,16},{28,20},{1,9},{5... | collective-permute-start | bytes 2359304 | tf_op jit(solution)/shard_map/ppermute | solution.py:22
  29.4 27.1 %collective-permute-start.5 = (bf16[192,2048]{1,0:T(8,128)(2,1)}, bf16[192,2048]{1,0:T(8,128)(2,1)S(1)}, u32[]{:S(2)}, u32[]{:S(2)}) collective-permute-start(bf16[192,2048]{1,0:T(8,128)(2,1)} %get-tuple-element.26.refs_0_), channel_id=1, source_target_pairs={{0,4},{4,0},{8,12},{12,8},{16,20},{20,16},{24,28},{28,24},{1,5},{5... | collective-permute-start | bytes 2359304 | tf_op jit(solution)/shard_map/ppermute | solution.py:22
  55.2 6.9 %copy-start.8 = (bf16[128,2048]{1,0:T(8,128)(2,1)S(1)}, bf16[128,2048]{1,0:T(8,128)(2,1)}, u32[]{:S(2)}) copy-start(bf16[128,2048]{1,0:T(8,128)(2,1)} %copy-done.7) | copy-start | bytes 1572868
  57.5 34.9 %all-to-all-start.1 = ((bf16[8,272,256]{2,1,0:T(8,128)(2,1)}), bf16[8,272,256]{2,1,0:T(8,128)(2,1)S(1)}, u32[]{:S(2)}, u32[]{:S(2)}) async-start(bf16[8,272,256]{2,1,0:T(8,128)(2,1)} %convolve.1), calls=%async_computation.1 | async-start | bytes 2228224 | tf_op jit(solution)/shard_map/all_to_all | solution.py:373
  62.1 22.1 %collective-permute-start.6 = (bf16[128,2048]{1,0:T(8,128)(2,1)S(1)}, bf16[128,2048]{1,0:T(8,128)(2,1)S(1)}, u32[]{:S(2)}, u32[]{:S(2)}) collective-permute-start(bf16[128,2048]{1,0:T(8,128)(2,1)S(1)} %copy-done.8), channel_id=1, source_target_pairs={{0,4},{4,0},{8,12},{12,8},{16,20},{20,16},{24,28},{28,24},{1,5},{5... | collective-permute-start | bytes 1572872 | tf_op jit(solution)/shard_map/ppermute | solution.py:22
  62.2 30.1 %collective-permute-start.7 = (bf16[128,2048]{1,0:T(8,128)(2,1)S(1)}, bf16[128,2048]{1,0:T(8,128)(2,1)}, u32[]{:S(2)}, u32[]{:S(2)}) collective-permute-start(bf16[128,2048]{1,0:T(8,128)(2,1)S(1)} %copy-done.8), channel_id=1, source_target_pairs={{0,8},{4,12},{8,0},{12,4},{16,24},{20,28},{24,16},{28,20},{1,9},{5... | collective-permute-start | bytes 1572872 | tf_op jit(solution)/shard_map/ppermute | solution.py:22
  84.1 8.2 %copy-start.17 = (bf16[128,2048]{1,0:T(8,128)(2,1)}, bf16[128,2048]{1,0:T(8,128)(2,1)S(1)}, u32[]{:S(2)}) copy-start(bf16[128,2048]{1,0:T(8,128)(2,1)S(1)} %collective-permute-done.6.refs_3_) | copy-start | bytes 1572868
  92.6 53.0 %copy-start.2 = (bf16[2048,256]{1,0:T(8,128)(2,1)}, bf16[2048,256]{1,0:T(8,128)(2,1)S(1)}, u32[]{:S(2)}) copy-start(bf16[2048,256]{1,0:T(8,128)(2,1)S(1)} %gate.1.gating_ref) | copy-start | bytes 3145732
  93.4 17.4 %collective-permute-start.12 = (bf16[192,2048]{1,0:T(8,128)(2,1)}, bf16[192,2048]{1,0:T(8,128)(2,1)S(1)}, u32[]{:S(2)}, u32[]{:S(2)}) collective-permute-start(bf16[192,2048]{1,0:T(8,128)(2,1)} %copy-done.6), channel_id=1, source_target_pairs={{0,4},{4,0},{8,12},{12,8},{16,20},{20,16},{24,28},{28,24},{1,5},{5... | collective-permute-start | bytes 2359304 | tf_op jit(solution)/shard_map/ppermute | solution.py:22
  93.4 35.5 %collective-permute-start.11 = (bf16[192,2048]{1,0:T(8,128)(2,1)}, bf16[192,2048]{1,0:T(8,128)(2,1)S(1)}, u32[]{:S(2)}, u32[]{:S(2)}) collective-permute-start(bf16[192,2048]{1,0:T(8,128)(2,1)} %copy-done.6), channel_id=1, source_target_pairs={{0,8},{4,12},{8,0},{12,4},{16,24},{20,28},{24,16},{28,20},{1,9},{5... | collective-permute-start | bytes 2359304 | tf_op jit(solution)/shard_map/ppermute | solution.py:22
  93.4 51.1 %collective-permute-start.8 = (bf16[2048,256]{1,0:T(8,128)(2,1)S(1)}, bf16[2048,256]{1,0:T(8,128)(2,1)}, u32[]{:S(2)}, u32[]{:S(2)}) collective-permute-start(bf16[2048,256]{1,0:T(8,128)(2,1)S(1)} %gate.1.gating_ref), channel_id=1, source_target_pairs={{0,16},{4,20},{8,24},{12,28},{16,0},{20,4},{24,8},{28,12},{1,17},{... | collective-permute-start | bytes 3145736 | tf_op jit(solution)/shard_map/ppermute | solution.py:22
  96.4 42.5 %collective-permute-start.9 = (bf16[192,2048]{1,0:T(8,128)(2,1)}, bf16[192,2048]{1,0:T(8,128)(2,1)}, u32[]{:S(2)}, u32[]{:S(2)}) collective-permute-start(bf16[192,2048]{1,0:T(8,128)(2,1)} %collective-permute-done.4.refs_4_), channel_id=1, source_target_pairs={{0,4},{4,0},{8,12},{12,8},{16,20},{20,16},{24,28},{28,24},{1,5},{5... | collective-permute-start | bytes 2359304 | tf_op jit(solution)/shard_map/ppermute | solution.py:22
  97.2 41.6 %collective-permute-start.10 = (bf16[128,2048]{1,0:T(8,128)(2,1)}, bf16[128,2048]{1,0:T(8,128)(2,1)S(1)}, u32[]{:S(2)}, u32[]{:S(2)}) collective-permute-start(bf16[128,2048]{1,0:T(8,128)(2,1)} %collective-permute-done.7.refs_6_), channel_id=1, source_target_pairs={{0,4},{4,0},{8,12},{12,8},{16,20},{20,16},{24,28},{28,24},{1,5},{5... | collective-permute-start | bytes 1572872 | tf_op jit(solution)/shard_map/ppermute | solution.py:22
  110.8 34.8 %copy-start.12 = (bf16[192,2048]{1,0:T(8,128)(2,1)}, bf16[192,2048]{1,0:T(8,128)(2,1)S(1)}, u32[]{:S(2)}) copy-start(bf16[192,2048]{1,0:T(8,128)(2,1)S(1)} %collective-permute-done.12.refs_10_) | copy-start | bytes 2359300
  110.8 34.7 %collective-permute-start.14 = (bf16[128,2048]{1,0:T(8,128)(2,1)S(1)}, bf16[128,2048]{1,0:T(8,128)(2,1)}, u32[]{:S(2)}, u32[]{:S(2)}) collective-permute-start(bf16[128,2048]{1,0:T(8,128)(2,1)S(1)} %slice.40), channel_id=1, source_target_pairs={{0,8},{4,12},{8,0},{12,4},{16,24},{20,28},{24,16},{28,20},{1,9},{5... | collective-permute-start | bytes 1572872 | tf_op jit(solution)/shard_map/ppermute | solution.py:22
  129.8 14.6 %collective-permute-start.13 = (bf16[64,2048]{1,0:T(8,128)(2,1)S(1)}, bf16[64,2048]{1,0:T(8,128)(2,1)S(1)}, u32[]{:S(2)}, u32[]{:S(2)}) collective-permute-start(bf16[64,2048]{1,0:T(8,128)(2,1)S(1)} %slice.39), channel_id=1, source_target_pairs={{0,4},{4,0},{8,12},{12,8},{16,20},{20,16},{24,28},{28,24},{1,5},{5... | collective-permute-start | bytes 786440 | tf_op jit(solution)/shard_map/ppermute | solution.py:22
  155.5 5.0 %collective-permute-start.15 = (bf16[2,1024,256]{2,1,0:T(8,128)(2,1)}, bf16[2,1024,256]{2,1,0:T(8,128)(2,1)S(1)}, u32[]{:S(2)}, u32[]{:S(2)}) collective-permute-start(bf16[2,1024,256]{2,1,0:T(8,128)(2,1)} %get-tuple-element.37), channel_id=1, source_target_pairs={{0,1},{1,0},{2,3},{3,2},{4,5},{5,4},{6,7},{7,6},{8,9},{9,8},{10,11... | collective-permute-start | bytes 3145736 | tf_op jit(solution)/shard_map/ppermute | solution.py:22
  161.1 7.6 %collective-permute-start.17 = (bf16[512,256]{1,0:T(8,128)(2,1)S(1)}, bf16[512,256]{1,0:T(8,128)(2,1)S(1)}, u32[]{:S(2)}, u32[]{:S(2)}) collective-permute-start(bf16[512,256]{1,0:T(8,128)(2,1)S(1)} %dynamic-slice_convert_fusion), channel_id=1, source_target_pairs={{0,2},{1,3},{2,0},{3,1},{4,6},{5,7},{6,4},{7,5},{8,10},{9,11},{10,... | collective-permute-start | bytes 786440 | tf_op jit(solution)/shard_map/ppermute | solution.py:22
  161.4 25.4 %collective-permute-start.16 = (bf16[1024,256]{1,0:T(8,128)(2,1)S(1)}, bf16[1024,256]{1,0:T(8,128)(2,1)S(1)}, u32[]{:S(2)}, u32[]{:S(2)}) collective-permute-start(bf16[1024,256]{1,0:T(8,128)(2,1)S(1)} %get-tuple-element.40), channel_id=1, source_target_pairs={{2,0},{3,1},{6,4},{7,5},{10,8},{11,9},{14,12},{15,13},{16,18},{17,... | collective-permute-start | bytes 1572872 | tf_op jit(solution)/shard_map/ppermute | solution.py:409
  168.8 15.9 %collective-permute-start.18 = (bf16[512,256]{1,0:T(8,128)(2,1)S(1)}, bf16[512,256]{1,0:T(8,128)(2,1)S(1)}, u32[]{:S(2)}, u32[]{:S(2)}) collective-permute-start(bf16[512,256]{1,0:T(8,128)(2,1)S(1)} %add_convert_fusion), channel_id=1, source_target_pairs={{0,16},{1,17},{4,20},{5,21},{8,24},{9,25},{12,28},{13,29},{18,2},{... | collective-permute-start | bytes 786440 | tf_op jit(solution)/shard_map/ppermute | solution.py:409
  170.1 16.8 %collective-permute-start.19 = (bf16[512,256]{1,0:T(8,128)(2,1)S(1)}, bf16[512,256]{1,0:T(8,128)(2,1)S(1)}, u32[]{:S(2)}, u32[]{:S(2)}) collective-permute-start(bf16[512,256]{1,0:T(8,128)(2,1)S(1)} %add_convert_fusion), channel_id=1, source_target_pairs={{2,16},{3,17},{6,20},{7,21},{10,24},{11,25},{14,28},{15,29},{16,2}... | collective-permute-start | bytes 786440 | tf_op jit(solution)/shard_map/ppermute | solution.py:409
  (10 other events, 22.0 us)

commit v4 on v3

--- a/solution.py
+++ b/solution.py
@@ -1,4 +1,5 @@
 import functools
+import math
 
 import jax
 import jax.numpy as jnp
@@ -79,7 +80,7 @@
 def featurize_kernel(input_ref, taps_ref, halo_ref, mixture_ref, query_ref, held):
     block, tokens = mixture_ref.shape[1:]
 
-    @pl.loop(0, input_ref.shape[1] // 128)
+    @pl.loop(0, input_ref.shape[1] // 128, unroll=math.gcd(4, input_ref.shape[1] // 128))
     def _(tile):
         channels = pl.ds(pl.multiple_of(tile * 128, 128), 128)
         weights = []
@@ -125,14 +126,22 @@
     )(values, taps, halo)
 
 
-def convolve_kernel(filters_ref, skip_ref, mixture_ref, added_ref, out_ref, total_ref):
+def convolve_kernel(filters_ref, skip_ref, mixture_ref, added_ref, result_ref, total_ref, out_ref, sems):
     ctx_count, block, tokens = mixture_ref.shape
     rows = ctx_count * GROUP
+
+    def copy_out(group):
+        place = (slice(None), pl.ds(pl.multiple_of(group * GROUP, GROUP), GROUP))
+        return pltpu.make_async_copy(out_ref.at[place], result_ref.at[place], sems.at[group])
+
+    for j in range(ctx_count):
+        out_ref[j, block:, :] = added_ref[...]
+    copy_out(block // GROUP).start()
     upper = lax.broadcasted_iota(jnp.int32, (tokens, tokens), 1) >= lax.broadcasted_iota(
         jnp.int32, (tokens, tokens), 0
     )
 
-    @pl.loop(0, filters_ref.shape[0])
+    @pl.loop(0, filters_ref.shape[0], unroll=math.gcd(4, filters_ref.shape[0]))
     def _(group):
         channels = pl.ds(pl.multiple_of(group * GROUP, GROUP), GROUP)
         here = pl.ds(group, 1)
@@ -167,9 +176,11 @@
         for j in range(ctx_count):
             total = total_ref[j * GROUP : (j + 1) * GROUP, :]
             out_ref[j, channels, :] = (total + skip * mixture[j].astype(F32)).astype(BF16)
-
-    for j in range(ctx_count):
-        out_ref[j, block:, :] = added_ref[...]
+        copy_out(group).start()
+
+    @pl.loop(0, block // GROUP + 1)
+    def _(group):
+        copy_out(group).wait()
 
 
 def convolve(filters, skip, mixture, added):
@@ -178,8 +189,12 @@
     return pl.pallas_call(
         convolve_kernel,
         in_specs=[pl.BlockSpec(memory_space=pltpu.VMEM)] * 4,
-        out_specs=pl.BlockSpec(memory_space=pltpu.VMEM),
-        scratch_shapes=[pltpu.VMEM((total_rows, tokens), F32)],
+        out_specs=pl.BlockSpec(memory_space=pl.ANY),
+        scratch_shapes=[
+            pltpu.VMEM((total_rows, tokens), F32),
+            pltpu.VMEM((ctx_count, block + GROUP, tokens), BF16),
+            pltpu.SemaphoreType.DMA((block // GROUP + 1,)),
+        ],
         out_shape=jax.ShapeDtypeStruct((ctx_count, block + GROUP, tokens), BF16),
         compiler_params=pltpu.CompilerParams(vmem_limit_bytes=VMEM_LIMIT),
         cost_estimate=pl.CostEstimate(
@@ -211,8 +226,8 @@
 def project_kernel(layout, places, where_ref, gating_ref, far_gating_ref, *refs):
     arrays = len(layout)
     weight_refs = refs[:arrays]
-    keep_refs, far_keep_refs = refs[arrays : arrays + 2]
-    send_ref, held, gating_held, sems = refs[arrays + 2 :]
+    keep_refs, far_keep_refs, send_ref = refs[arrays : arrays + 3]
+    held, gating_held, kept, sent, sems, out_sems = refs[arrays + 3 :]
     low, core = where_ref[1], where_ref[2]
     tokens = gating_ref.shape[1]
     block = 2 * keep_refs.shape[0] // places
@@ -229,14 +244,14 @@
         copy.start()
     copies[0].wait()
     copies[1].wait()
-    pending, first, at = [], 0, 0
+    pending, outs, first, at = [], [], 0, 0
     total_rows = held.shape[0]
     for n, (copy, entries) in enumerate(zip(copies[2:], layout)):
         copy.wait()
         for entry in entries:
             pending.append((at, entry))
             at += entry[1]
-        if at - first < total_rows // 4 and n + 1 < arrays:
+        if at - first < (total_rows // 4 if first else total_rows // 8) and n + 1 < arrays:
             continue
         total = jnp.dot(held[first:at, :], gating_held[...], preferred_element_type=F32)
         for begin, (offset, rows, p) in pending:
@@ -245,18 +260,42 @@
             start = (place & (places // 2 - 1)) * block + offset
             target = pl.ds(pl.multiple_of(start, 16), rows)
             piece = total[begin - first : begin - first + rows]
+            here = slice(begin, begin + rows)
+            sem = [out_sems.at[len(outs), n] for n in range(2)]
+            keeping = [
+                pltpu.make_async_copy(kept.at[0, here, :], keep_refs.at[target, :], sem[0]),
+                pltpu.make_async_copy(kept.at[1, here, :], far_keep_refs.at[target, :], sem[1]),
+            ]
+            sending = [
+                pltpu.make_async_copy(sent.at[n, here, :], send_ref.at[n, target, :], sem[n])
+                for n in range(2)
+            ]
+            outs.append((mine, keeping, sending))
 
             @pl.when(mine)
             def _():
-                keep_refs[target, :] = piece[:, :tokens]
-                far_keep_refs[target, :] = piece[:, tokens:]
+                for n in range(2):
+                    kept[n, here, :] = piece[:, n * tokens : (n + 1) * tokens]
+                    keeping[n].start()
 
             @pl.when(jnp.logical_not(mine))
             def _():
-                send_ref[0, target, :] = piece[:, :tokens].astype(BF16)
-                send_ref[1, target, :] = piece[:, tokens:].astype(BF16)
+                for n in range(2):
+                    sent[n, here, :] = piece[:, n * tokens : (n + 1) * tokens].astype(BF16)
+                    sending[n].start()
 
         pending, first = [], at
+    for mine, keeping, sending in outs:
+
+        @pl.when(mine)
+        def _():
+            for copy in keeping:
+                copy.wait()
+
+        @pl.when(jnp.logical_not(mine))
+        def _():
+            for copy in sending:
+                copy.wait()
 
 
 def project(where, places, layout, weights, gating, far_gating):
@@ -270,11 +309,14 @@
             num_scalar_prefetch=1,
             grid=(1,),
             in_specs=[pl.BlockSpec(memory_space=pl.ANY)] * (2 + len(weights)),
-            out_specs=[pl.BlockSpec(memory_space=pltpu.VMEM)] * 3,
+            out_specs=[pl.BlockSpec(memory_space=pl.ANY)] * 3,
             scratch_shapes=[
                 pltpu.VMEM((total_rows, width), BF16),
                 pltpu.VMEM((width, 2 * tokens), BF16),
+                pltpu.VMEM((2, total_rows, tokens), F32),
+                pltpu.VMEM((2, total_rows, tokens), BF16),
                 pltpu.SemaphoreType.DMA((len(weights) + 2,)),
+                pltpu.SemaphoreType.DMA((sum(map(len, layout)), 2)),
             ],
         ),
         out_shape=[out, out, sent],
@@ -340,7 +382,7 @@
     own_mixture = mixture
     mixture = lax.all_to_all(own_mixture, "ctx", split_axis=0, concat_axis=0, tiled=True)
 
-    cuts = (0, rows * 3 // 8 // 16 * 16, rows * 5 // 8 // 16 * 16, rows)
+    cuts = (0, rows * 12 // 32 // 16 * 16, rows * 21 // 32 // 16 * 16, rows)
     frozen = after(frozen_weight, own_mixture)
     *parts, norms = merge(cuts, frozen, down_update_weight, up_update_weight)
     norms = norms[:, 0][None, :]
@@ -382,13 +424,14 @@
     magnitude_here = lax.dynamic_slice_in_dim(magnitude, tp_index * owned, owned)
     scaling = magnitude_here / jnp.sqrt(norms_here + EPSILON)
 
-    finish(after(far_part, scaling), [coarse], rest, 0, cuts[1])
-    finish(after(other_part, scaling), [coarse], rest, cuts[1], cuts[2] - cuts[1])
-    part = after(parts[2], scaling)
+    finish(after(far_part, received), [coarse], rest, 0, cuts[1])
+    finish(after(other_part, received), [coarse], rest, cuts[1], cuts[2] - cuts[1])
+    part = parts[2]
     late_start, late_rows = cuts[2], cuts[3] - cuts[2]
     if len(rest) == 1:
-        upper = late_rows // 3 // 16 * 16
-        coarse_part, fine_part = exchange(part, "ctx", coarse), exchange(part, "ctx", rest[0])
+        upper = late_rows // 2 // 16 * 16
+        coarse_part = exchange(after(part, scaling), "ctx", coarse)
+        fine_part = exchange(after(part, received), "ctx", rest[0])
         last = exchange(coarse_part[:upper], "ctx", rest[0])
         other = exchange(fine_part[upper:], "ctx", coarse)
         pieces += [part, coarse_part, fine_part, last, other]
@@ -396,7 +439,7 @@
         layout.append(((late_start, upper, coarse + rest[0]),))
         layout.append(((late_start + upper, late_rows - upper, coarse + rest[0]),))
     else:
-        finish(part, [0], distances, late_start, late_rows)
+        finish(after(part, scaling), [0], distances, late_start, late_rows)
     layout = tuple(layout)
 
     def place(h, l, y, c):

time: 190 us -> 185 us (0.974)
  Pallas kernels: 26.2 us -> 22.6 us
    ppermute x16, waiting for transfers between devices: 81.1 us -> 55.4 us  [exchange(): return lax.ppermute(block, axis, [(i, i ^ distance) for i in range(count)])]
    all_to_all x1, waiting for transfers between devices: 0.01 us -> 24.9 us  [on_device(): lax.all_to_all(sent, 'ctx', split_axis=0, concat_axis=0, tiled=True)]
  transfers between devices with their start and end apart: 22 -> 22, of which waited for: 15 -> 15; matrix products, arithmetic and copies ran while one was open for 1% -> 2% of each run, Pallas kernels for 5% -> 5%
where the time goes in v4:
time: 185 us; the launch traced here: 184 us
  waiting for transfers between devices  113 us (61%)
  starting transfers between devices  36.7 us (20%)
  Pallas kernels  22.6 us (12%)
  local copies, waits for them, and re-layouts  8.01 us (4%)
  other arithmetic  3.17 us (2%)
    ppermute x16, waiting for transfers between devices, exchange(): return lax.ppermute(block, axis, [(i, i ^ distance) for i in range(count)])  55.4 us
    all_to_all x1, waiting for transfers between devices, on_device(): lax.all_to_all(sent, 'ctx', split_axis=0, concat_axis=0, tiled=True)  24.9 us
    all_to_all x1, waiting for transfers between devices, on_device(): lax.all_to_all(own_mixture, 'ctx', split_axis=0, concat_axis=0, tiled=True)  15.9 us
    ppermute x16, starting transfers between devices, exchange(): return lax.ppermute(block, axis, [(i, i ^ distance) for i in range(count)])  15.1 us
    ppermute x3, waiting for transfers between devices, send_on(): lax.ppermute(value, ('ctx', 'tp'), [(place(*a), place(*b)) for a, b in pa...  14.1 us
    pallas_call x1, Pallas kernels, project(): pl.pallas_call(functools.partial(project_kernel, layout, places), grid_sp...  9.14 us
    ppermute x3, starting transfers between devices, send_on(): lax.ppermute(value, ('ctx', 'tp'), [(place(*a), place(*b)) for a, b in pa...  7.66 us
    pallas_call x1, Pallas kernels, convolve(): pl.pallas_call(convolve_kernel, in_specs=[pl.BlockSpec(memory_space=pltpu...  6.81 us
  transfers between devices with their start and end apart: 22, of which 15 were waited for; matrix products, arithmetic and copies ran while one was open for 2% of the time, Pallas kernels for 5%

profile of v4, /device:TPU:7, one launch (start us, length us, event | category | flops | bytes accessed | tf_op | source)
XLA Modules:
  0.0 184.2 jit_solution(3813005767411451191)
XLA Ops:
  0.0 1.9 %copy-done = bf16[3,2048,256]{2,1,0:T(8,128)(2,1)S(1)} copy-done((bf16[3,2048,256]{2,1,0:T(8,128)(2,1)S(1)}, bf16[3,2048,256]{2,1,0:T(8,128)(2,1)}, u32[]{:S(2)}) %copy-start) | copy-done | bytes 3145752
  1.9 1.0 last_tokens.1
  3.0 3.3 %collective-permute-start = (bf16[32,2048]{1,0:T(8,128)(2,1)S(1)}, bf16[32,2048]{1,0:T(8,128)(2,1)S(1)}, u32[]{:S(2)}, u32[]{:S(2)}) collective-permute-start(bf16[32,2048]{1,0:T(8,128)(2,1)S(1)} %last_tokens.1), channel_id=1, source_target_pairs={{0,4},{4,8},{8,12},{12,16},{16,20},{20,24},{24,28},{1,5},{5,9},{9,... | collective-permute-start | bytes 393224 | tf_op jit(solution)/shard_map/ppermute | solution.py:379
  6.3 3.1 %collective-permute-done.halo_ref = bf16[32,2048]{1,0:T(8,128)(2,1)S(1)} collective-permute-done((bf16[32,2048]{1,0:T(8,128)(2,1)S(1)}, bf16[32,2048]{1,0:T(8,128)(2,1)S(1)}, u32[]{:S(2)}, u32[]{:S(2)}) %collective-permute-start) | collective-permute-done | bytes 131104 | tf_op jit(solution)/shard_map/ppermute | solution.py:379
  9.4 4.1 %featurize.1 = (bf16[8,256,256]{2,1,0:T(8,128)(2,1)S(1)}, bf16[8,256,256]{2,1,0:T(8,128)(2,1)S(1)}) custom-call(bf16[3,2048,256]{2,1,0:T(8,128)(2,1)S(1)} %copy-done, f32[3,7,2048]{2,1,0:T(8,128)S(1)} %copy-done.4, bf16[32,2048]{1,0:T(8,128)(2,1)S(1)} %collective-permute-done.halo_ref), custom_call_target="tpu_custom_call" | custom-call | flops 22020096 | bytes 10485760 | tf_op jit(solution)/shard_map/featurize/pallas_call | solution.py:115
  14.5 5.9 %all-to-all-start = ((bf16[8,256,256]{2,1,0:T(8,128)(2,1)}), bf16[8,256,256]{2,1,0:T(8,128)(2,1)}, u32[]{:S(2)}, u32[]{:S(2)}) async-start(bf16[8,256,256]{2,1,0:T(8,128)(2,1)} %copy-done.3), calls=%async_computation | async-start | bytes 2097152 | tf_op jit(solution)/shard_map/all_to_all | solution.py:383
  20.5 1.2 merge.1
  23.6 2.2 %collective-permute-start.1 = (f32[1,512]{1,0:T(1,128)S(1)}, f32[1,512]{1,0:T(1,128)S(1)}, u32[]{:S(2)}, u32[]{:S(2)}) collective-permute-start(f32[1,512]{1,0:T(1,128)S(1)} %bitcast.17), channel_id=1, source_target_pairs={{0,1},{1,0},{2,3},{3,2},{4,5},{5,4},{6,7},{7,6},{8,9},{9,8},{10,11... | collective-permute-start | bytes 6152 | tf_op jit(solution)/shard_map/ppermute | solution.py:23
  26.1 1.5 collective-permute-start.3
  27.5 1.2 collective-permute-start.4
  29.5 15.9 %all-to-all-done.mixture_ref = bf16[8,256,256]{2,1,0:T(8,128)(2,1)} async-done(((bf16[8,256,256]{2,1,0:T(8,128)(2,1)}), bf16[8,256,256]{2,1,0:T(8,128)(2,1)}, u32[]{:S(2)}, u32[]{:S(2)}) %all-to-all-start) | async-done | bytes 1048608 | tf_op jit(solution)/shard_map/all_to_all | solution.py:383
  45.5 6.8 %convolve.1 = bf16[8,272,256]{2,1,0:T(8,128)(2,1)} custom-call(f32[16,2048]{1,0:T(8,128)S(1)} %copy-done.10, f32[256,128]{1,0:T(8,128)S(1)} %broadcast_in_dim.2.skip_ref, bf16[8,256,256]{2,1,0:T(8,128)(2,1)} %all-to-all-done.mixture_ref, bf16[16,256]{1,0:T(8,128)(2,1)S(1)} %fusion.8.added_ref), custom_call_target="tpu_custom_call" | custom-call | flops 8589934592 | bytes 20971520 | tf_op jit(solution)/shard_map/convolve/pallas_call | solution.py:189
  52.4 3.0 %collective-permute-done.4.refs_4_ = bf16[192,2048]{1,0:T(8,128)(2,1)S(1)} collective-permute-done((bf16[192,2048]{1,0:T(8,128)(2,1)}, bf16[192,2048]{1,0:T(8,128)(2,1)S(1)}, u32[]{:S(2)}, u32[]{:S(2)}) %collective-permute-start.4) | collective-permute-done | bytes 786464 | tf_op jit(solution)/shard_map/ppermute | solution.py:23
  56.3 4.8 %all-to-all-start.1 = ((bf16[8,272,256]{2,1,0:T(8,128)(2,1)}), bf16[8,272,256]{2,1,0:T(8,128)(2,1)S(1)}, u32[]{:S(2)}, u32[]{:S(2)}) async-start(bf16[8,272,256]{2,1,0:T(8,128)(2,1)} %convolve.1), calls=%async_computation.1 | async-start | bytes 2228224 | tf_op jit(solution)/shard_map/all_to_all | solution.py:415
  61.2 1.3 collective-permute-start.7
  62.5 24.9 %all-to-all-done.1.summed_ref = bf16[8,272,256]{2,1,0:T(8,128)(2,1)S(1)} async-done(((bf16[8,272,256]{2,1,0:T(8,128)(2,1)}), bf16[8,272,256]{2,1,0:T(8,128)(2,1)S(1)}, u32[]{:S(2)}, u32[]{:S(2)}) %all-to-all-start.1) | async-done | bytes 1114144 | tf_op jit(solution)/shard_map/all_to_all | solution.py:415
  87.4 5.5 %collective-permute-done.7.refs_6_ = bf16[144,2048]{1,0:T(8,128)(2,1)} collective-permute-done((bf16[144,2048]{1,0:T(8,128)(2,1)S(1)}, bf16[144,2048]{1,0:T(8,128)(2,1)}, u32[]{:S(2)}, u32[]{:S(2)}) %collective-permute-start.7) | collective-permute-done | bytes 589856 | tf_op jit(solution)/shard_map/ppermute | solution.py:23
  94.9 2.2 %collective-permute-start.8 = (bf16[2048,256]{1,0:T(8,128)(2,1)}, bf16[2048,256]{1,0:T(8,128)(2,1)}, u32[]{:S(2)}, u32[]{:S(2)}) collective-permute-start(bf16[2048,256]{1,0:T(8,128)(2,1)} %copy-done.2), channel_id=1, source_target_pairs={{0,16},{4,20},{8,24},{12,28},{16,0},{20,4},{24,8},{28,12},{1,17},{... | collective-permute-start | bytes 3145736 | tf_op jit(solution)/shard_map/ppermute | solution.py:23
  98.6 5.0 %collective-permute-done.12.refs_10_ = bf16[176,2048]{1,0:T(8,128)(2,1)} collective-permute-done((bf16[176,2048]{1,0:T(8,128)(2,1)S(1)}, bf16[176,2048]{1,0:T(8,128)(2,1)}, u32[]{:S(2)}, u32[]{:S(2)}) %collective-permute-start.12) | collective-permute-done | bytes 720928 | tf_op jit(solution)/shard_map/ppermute | solution.py:23
  105.3 22.0 %collective-permute-done.11.refs_9_ = bf16[176,2048]{1,0:T(8,128)(2,1)S(1)} collective-permute-done((bf16[176,2048]{1,0:T(8,128)(2,1)S(1)}, bf16[176,2048]{1,0:T(8,128)(2,1)S(1)}, u32[]{:S(2)}, u32[]{:S(2)}) %collective-permute-start.11) | collective-permute-done | bytes 720928 | tf_op jit(solution)/shard_map/ppermute | solution.py:23
  128.1 5.0 %collective-permute-done.10.refs_7_ = bf16[144,2048]{1,0:T(8,128)(2,1)S(1)} collective-permute-done((bf16[144,2048]{1,0:T(8,128)(2,1)}, bf16[144,2048]{1,0:T(8,128)(2,1)S(1)}, u32[]{:S(2)}, u32[]{:S(2)}) %collective-permute-start.10) | collective-permute-done | bytes 589856 | tf_op jit(solution)/shard_map/ppermute | solution.py:23
  133.1 7.0 %collective-permute-done.13.refs_11_ = bf16[80,2048]{1,0:T(8,128)(2,1)S(1)} collective-permute-done((bf16[80,2048]{1,0:T(8,128)(2,1)S(1)}, bf16[80,2048]{1,0:T(8,128)(2,1)S(1)}, u32[]{:S(2)}, u32[]{:S(2)}) %collective-permute-start.13) | collective-permute-done | bytes 327712 | tf_op jit(solution)/shard_map/ppermute | solution.py:23
  140.9 9.1 %project.1 = (f32[1024,256]{1,0:T(8,128)}, f32[1024,256]{1,0:T(8,128)}, bf16[2,1024,256]{2,1,0:T(8,128)(2,1)}) custom-call(s32[4]{0:T(128)} %pad_add_fusion.where_ref, bf16[2048,256]{1,0:T(8,128)(2,1)} %copy-done.2, bf16[2048,256]{1,0:T(8,128)(2,1)} %collective-permute-done.8.far_gating_ref, bf16[192,2048]{1,0:T(8,128)(2,1)} %get-tuple-element.27.refs_0_, ...), custom_call_target="tpu_custom_call" | custom-call | flops 4294967296 | bytes 10485760 | tf_op jit(solution)/shard_map/project/pallas_call | solution.py:306
  150.1 3.6 %collective-permute-start.15 = (bf16[2,1024,256]{2,1,0:T(8,128)(2,1)}, bf16[2,1024,256]{2,1,0:T(8,128)(2,1)S(1)}, u32[]{:S(2)}, u32[]{:S(2)}) collective-permute-start(bf16[2,1024,256]{2,1,0:T(8,128)(2,1)} %get-tuple-element.39), channel_id=1, source_target_pairs={{0,1},{1,0},{2,3},{3,2},{4,5},{5,4},{6,7},{7,6},{8,9},{9,8},{10,11... | collective-permute-start | bytes 3145736 | tf_op jit(solution)/shard_map/ppermute | solution.py:23
  153.7 2.5 %collective-permute-done.15 = bf16[2,1024,256]{2,1,0:T(8,128)(2,1)S(1)} collective-permute-done((bf16[2,1024,256]{2,1,0:T(8,128)(2,1)}, bf16[2,1024,256]{2,1,0:T(8,128)(2,1)S(1)}, u32[]{:S(2)}, u32[]{:S(2)}) %collective-permute-start.15) | collective-permute-done | bytes 1048608 | tf_op jit(solution)/shard_map/ppermute | solution.py:23
  157.1 3.2 %collective-permute-start.16 = (bf16[1024,256]{1,0:T(8,128)(2,1)S(1)}, bf16[1024,256]{1,0:T(8,128)(2,1)S(1)}, u32[]{:S(2)}, u32[]{:S(2)}) collective-permute-start(bf16[1024,256]{1,0:T(8,128)(2,1)S(1)} %get-tuple-element.42), channel_id=1, source_target_pairs={{2,0},{3,1},{6,4},{7,5},{10,8},{11,9},{14,12},{15,13},{16,18},{17,... | collective-permute-start | bytes 1572872 | tf_op jit(solution)/shard_map/ppermute | solution.py:452
  160.3 4.1 %collective-permute-done.17 = bf16[512,256]{1,0:T(8,128)(2,1)S(1)} collective-permute-done((bf16[512,256]{1,0:T(8,128)(2,1)S(1)}, bf16[512,256]{1,0:T(8,128)(2,1)S(1)}, u32[]{:S(2)}, u32[]{:S(2)}) %collective-permute-start.17) | collective-permute-done | bytes 262176 | tf_op jit(solution)/shard_map/ppermute | solution.py:23
  164.4 1.3 collective-permute-start.18
  165.7 3.2 %collective-permute-start.19 = (bf16[512,256]{1,0:T(8,128)(2,1)S(1)}, bf16[512,256]{1,0:T(8,128)(2,1)S(1)}, u32[]{:S(2)}, u32[]{:S(2)}) collective-permute-start(bf16[512,256]{1,0:T(8,128)(2,1)S(1)} %add_convert_fusion), channel_id=1, source_target_pairs={{2,16},{3,17},{6,20},{7,21},{10,24},{11,25},{14,28},{15,29},{16,2}... | collective-permute-start | bytes 786440 | tf_op jit(solution)/shard_map/ppermute | solution.py:452
  168.9 11.9 %collective-permute-done.18 = bf16[512,256]{1,0:T(8,128)(2,1)S(1)} collective-permute-done((bf16[512,256]{1,0:T(8,128)(2,1)S(1)}, bf16[512,256]{1,0:T(8,128)(2,1)S(1)}, u32[]{:S(2)}, u32[]{:S(2)}) %collective-permute-start.18) | collective-permute-done | bytes 262176 | tf_op jit(solution)/shard_map/ppermute | solution.py:452
  180.9 2.2 %collective-permute-done.19 = bf16[512,256]{1,0:T(8,128)(2,1)S(1)} collective-permute-done((bf16[512,256]{1,0:T(8,128)(2,1)S(1)}, bf16[512,256]{1,0:T(8,128)(2,1)S(1)}, u32[]{:S(2)}, u32[]{:S(2)}) %collective-permute-start.19) | collective-permute-done | bytes 262176 | tf_op jit(solution)/shard_map/ppermute | solution.py:452
  183.1 1.1 multiply_convert_fusion
  (79 shorter events, 12.9 us)
Async XLA Ops:
  2.9 17.5 %copy-start.14 = (bf16[512,16]{0,1:T(8,128)(2,1)S(1)}, bf16[512,16]{0,1:T(8,128)(2,1)}, u32[]{:S(2)}) copy-start(bf16[512,16]{0,1:T(8,128)(2,1)} %param.14) | copy-start | bytes 49156
  2.9 17.6 %copy-start.1 = (bf16[512,2048]{1,0:T(8,128)(2,1)S(1)}, bf16[512,2048]{1,0:T(8,128)(2,1)}, u32[]{:S(2)}) copy-start(bf16[512,2048]{1,0:T(8,128)(2,1)} %frozen_ref) | copy-start | bytes 6291460
  3.0 17.6 %copy-start.5 = (bf16[16,2048]{1,0:T(8,128)(2,1)S(1)}, bf16[16,2048]{1,0:T(8,128)(2,1)}, u32[]{:S(2)}) copy-start(bf16[16,2048]{1,0:T(8,128)(2,1)} %down_ref.1) | copy-start | bytes 196612
  3.0 6.4 %collective-permute-start = (bf16[32,2048]{1,0:T(8,128)(2,1)S(1)}, bf16[32,2048]{1,0:T(8,128)(2,1)S(1)}, u32[]{:S(2)}, u32[]{:S(2)}) collective-permute-start(bf16[32,2048]{1,0:T(8,128)(2,1)S(1)} %last_tokens.1), channel_id=1, source_target_pairs={{0,4},{4,8},{8,12},{12,16},{16,20},{20,24},{24,28},{1,5},{5,9},{9,... | collective-permute-start | bytes 393224 | tf_op jit(solution)/shard_map/ppermute | solution.py:379
  14.5 31.0 %copy-start.15 = (f32[256]{0:T(256)S(1)}, f32[256]{0:T(256)}, u32[]{:S(2)}) copy-start(f32[256]{0:T(256)} %param.10) | copy-start | bytes 3076
  14.5 31.1 %copy-start.10 = (f32[16,2048]{1,0:T(8,128)S(1)}, f32[16,2048]{1,0:T(8,128)}, u32[]{:S(2)}) copy-start(f32[16,2048]{1,0:T(8,128)} %filters_ref.1) | copy-start | bytes 393220
  14.5 30.9 %all-to-all-start = ((bf16[8,256,256]{2,1,0:T(8,128)(2,1)}), bf16[8,256,256]{2,1,0:T(8,128)(2,1)}, u32[]{:S(2)}, u32[]{:S(2)}) async-start(bf16[8,256,256]{2,1,0:T(8,128)(2,1)} %copy-done.3), calls=%async_computation | async-start | bytes 2097152 | tf_op jit(solution)/shard_map/all_to_all | solution.py:383
  23.6 5.4 %collective-permute-start.1 = (f32[1,512]{1,0:T(1,128)S(1)}, f32[1,512]{1,0:T(1,128)S(1)}, u32[]{:S(2)}, u32[]{:S(2)}) collective-permute-start(f32[1,512]{1,0:T(1,128)S(1)} %bitcast.17), channel_id=1, source_target_pairs={{0,1},{1,0},{2,3},{3,2},{4,5},{5,4},{6,7},{7,6},{8,9},{9,8},{10,11... | collective-permute-start | bytes 6152 | tf_op jit(solution)/shard_map/ppermute | solution.py:23
  25.8 3.2 %collective-permute-start.2 = (f32[1,512]{1,0:T(1,128)S(1)}, f32[1,512]{1,0:T(1,128)S(1)}, u32[]{:S(2)}, u32[]{:S(2)}) collective-permute-start(f32[1,512]{1,0:T(1,128)S(1)} %bitcast.18), channel_id=1, source_target_pairs={{0,2},{1,3},{2,0},{3,1},{4,6},{5,7},{6,4},{7,5},{8,10},{9,11},{10,... | collective-permute-start | bytes 6152 | tf_op jit(solution)/shard_map/ppermute | solution.py:23
  26.1 3.4 %collective-permute-start.3 = (f32[1,512]{1,0:T(1,128)S(1)}, f32[1,512]{1,0:T(1,128)S(1)}, u32[]{:S(2)}, u32[]{:S(2)}) collective-permute-start(f32[1,512]{1,0:T(1,128)S(1)} %bitcast.19), channel_id=1, source_target_pairs={{0,3},{1,2},{2,1},{3,0},{4,7},{5,6},{6,5},{7,4},{8,11},{9,10},{10,... | collective-permute-start | bytes 6152 | tf_op jit(solution)/shard_map/ppermute | solution.py:23
  27.5 27.9 %collective-permute-start.4 = (bf16[192,2048]{1,0:T(8,128)(2,1)}, bf16[192,2048]{1,0:T(8,128)(2,1)S(1)}, u32[]{:S(2)}, u32[]{:S(2)}) collective-permute-start(bf16[192,2048]{1,0:T(8,128)(2,1)} %get-tuple-element.27.refs_0_), channel_id=1, source_target_pairs={{0,8},{4,12},{8,0},{12,4},{16,24},{20,28},{24,16},{28,20},{1,9},{5... | collective-permute-start | bytes 2359304 | tf_op jit(solution)/shard_map/ppermute | solution.py:23
  28.7 26.7 %collective-permute-start.5 = (bf16[192,2048]{1,0:T(8,128)(2,1)}, bf16[192,2048]{1,0:T(8,128)(2,1)}, u32[]{:S(2)}, u32[]{:S(2)}) collective-permute-start(bf16[192,2048]{1,0:T(8,128)(2,1)} %get-tuple-element.27.refs_0_), channel_id=1, source_target_pairs={{0,4},{4,0},{8,12},{12,8},{16,20},{20,16},{24,28},{28,24},{1,5},{5... | collective-permute-start | bytes 2359304 | tf_op jit(solution)/shard_map/ppermute | solution.py:23
  52.3 8.7 %copy-start.9 = (bf16[144,2048]{1,0:T(8,128)(2,1)S(1)}, bf16[144,2048]{1,0:T(8,128)(2,1)}, u32[]{:S(2)}) copy-start(bf16[144,2048]{1,0:T(8,128)(2,1)} %copy-done.8) | copy-start | bytes 1769476
  52.4 35.0 %copy-start.7 = (bf16[176,2048]{1,0:T(8,128)(2,1)S(1)}, bf16[176,2048]{1,0:T(8,128)(2,1)}, u32[]{:S(2)}) copy-start(bf16[176,2048]{1,0:T(8,128)(2,1)} %copy-done.6) | copy-start | bytes 2162692
  56.3 31.1 %all-to-all-start.1 = ((bf16[8,272,256]{2,1,0:T(8,128)(2,1)}), bf16[8,272,256]{2,1,0:T(8,128)(2,1)S(1)}, u32[]{:S(2)}, u32[]{:S(2)}) async-start(bf16[8,272,256]{2,1,0:T(8,128)(2,1)} %convolve.1), calls=%async_computation.1 | async-start | bytes 2228224 | tf_op jit(solution)/shard_map/all_to_all | solution.py:415
  61.0 26.4 %collective-permute-start.6 = (bf16[144,2048]{1,0:T(8,128)(2,1)S(1)}, bf16[144,2048]{1,0:T(8,128)(2,1)}, u32[]{:S(2)}, u32[]{:S(2)}) collective-permute-start(bf16[144,2048]{1,0:T(8,128)(2,1)S(1)} %copy-done.9), channel_id=1, source_target_pairs={{0,4},{4,0},{8,12},{12,8},{16,20},{20,16},{24,28},{28,24},{1,5},{5... | collective-permute-start | bytes 1769480 | tf_op jit(solution)/shard_map/ppermute | solution.py:23
  61.2 31.7 %collective-permute-start.7 = (bf16[144,2048]{1,0:T(8,128)(2,1)S(1)}, bf16[144,2048]{1,0:T(8,128)(2,1)}, u32[]{:S(2)}, u32[]{:S(2)}) collective-permute-start(bf16[144,2048]{1,0:T(8,128)(2,1)S(1)} %copy-done.9), channel_id=1, source_target_pairs={{0,8},{4,12},{8,0},{12,4},{16,24},{20,28},{24,16},{28,20},{1,9},{5... | collective-permute-start | bytes 1769480 | tf_op jit(solution)/shard_map/ppermute | solution.py:23
  87.4 16.2 %collective-permute-start.12 = (bf16[176,2048]{1,0:T(8,128)(2,1)S(1)}, bf16[176,2048]{1,0:T(8,128)(2,1)}, u32[]{:S(2)}, u32[]{:S(2)}) collective-permute-start(bf16[176,2048]{1,0:T(8,128)(2,1)S(1)} %copy-done.7), channel_id=1, source_target_pairs={{0,4},{4,0},{8,12},{12,8},{16,20},{20,16},{24,28},{28,24},{1,5},{5... | collective-permute-start | bytes 2162696 | tf_op jit(solution)/shard_map/ppermute | solution.py:23
  94.9 32.4 %collective-permute-start.11 = (bf16[176,2048]{1,0:T(8,128)(2,1)S(1)}, bf16[176,2048]{1,0:T(8,128)(2,1)S(1)}, u32[]{:S(2)}, u32[]{:S(2)}) collective-permute-start(bf16[176,2048]{1,0:T(8,128)(2,1)S(1)} %copy-done.7), channel_id=1, source_target_pairs={{0,8},{4,12},{8,0},{12,4},{16,24},{20,28},{24,16},{28,20},{1,9},{5... | collective-permute-start | bytes 2162696 | tf_op jit(solution)/shard_map/ppermute | solution.py:23
  94.9 46.0 %collective-permute-start.8 = (bf16[2048,256]{1,0:T(8,128)(2,1)}, bf16[2048,256]{1,0:T(8,128)(2,1)}, u32[]{:S(2)}, u32[]{:S(2)}) collective-permute-start(bf16[2048,256]{1,0:T(8,128)(2,1)} %copy-done.2), channel_id=1, source_target_pairs={{0,16},{4,20},{8,24},{12,28},{16,0},{20,4},{24,8},{28,12},{1,17},{... | collective-permute-start | bytes 3145736 | tf_op jit(solution)/shard_map/ppermute | solution.py:23
  97.1 36.0 %collective-permute-start.9 = (bf16[192,2048]{1,0:T(8,128)(2,1)}, bf16[192,2048]{1,0:T(8,128)(2,1)S(1)}, u32[]{:S(2)}, u32[]{:S(2)}) collective-permute-start(bf16[192,2048]{1,0:T(8,128)(2,1)} %copy-done.16), channel_id=1, source_target_pairs={{0,4},{4,0},{8,12},{12,8},{16,20},{20,16},{24,28},{28,24},{1,5},{5... | collective-permute-start | bytes 2359304 | tf_op jit(solution)/shard_map/ppermute | solution.py:23
  97.9 35.2 %collective-permute-start.10 = (bf16[144,2048]{1,0:T(8,128)(2,1)}, bf16[144,2048]{1,0:T(8,128)(2,1)S(1)}, u32[]{:S(2)}, u32[]{:S(2)}) collective-permute-start(bf16[144,2048]{1,0:T(8,128)(2,1)} %collective-permute-done.7.refs_6_), channel_id=1, source_target_pairs={{0,4},{4,0},{8,12},{12,8},{16,20},{20,16},{24,28},{28,24},{1,5},{5... | collective-permute-start | bytes 1769480 | tf_op jit(solution)/shard_map/ppermute | solution.py:23
  104.6 36.3 %collective-permute-start.14 = (bf16[96,2048]{1,0:T(8,128)(2,1)S(1)}, bf16[96,2048]{1,0:T(8,128)(2,1)}, u32[]{:S(2)}, u32[]{:S(2)}) collective-permute-start(bf16[96,2048]{1,0:T(8,128)(2,1)S(1)} %slice.40), channel_id=1, source_target_pairs={{0,8},{4,12},{8,0},{12,4},{16,24},{20,28},{24,16},{28,20},{1,9},{5... | collective-permute-start | bytes 1179656 | tf_op jit(solution)/shard_map/ppermute | solution.py:23
  127.3 13.6 %copy-start.13 = (bf16[176,2048]{1,0:T(8,128)(2,1)}, bf16[176,2048]{1,0:T(8,128)(2,1)S(1)}, u32[]{:S(2)}) copy-start(bf16[176,2048]{1,0:T(8,128)(2,1)S(1)} %collective-permute-done.11.refs_9_) | copy-start | bytes 2162692
  127.3 12.8 %collective-permute-start.13 = (bf16[80,2048]{1,0:T(8,128)(2,1)S(1)}, bf16[80,2048]{1,0:T(8,128)(2,1)S(1)}, u32[]{:S(2)}, u32[]{:S(2)}) collective-permute-start(bf16[80,2048]{1,0:T(8,128)(2,1)S(1)} %slice.39), channel_id=1, source_target_pairs={{0,4},{4,0},{8,12},{12,8},{16,20},{20,16},{24,28},{28,24},{1,5},{5... | collective-permute-start | bytes 983048 | tf_op jit(solution)/shard_map/ppermute | solution.py:23
  133.1 7.8 %copy-start.18 = (bf16[144,2048]{1,0:T(8,128)(2,1)}, bf16[144,2048]{1,0:T(8,128)(2,1)S(1)}, u32[]{:S(2)}) copy-start(bf16[144,2048]{1,0:T(8,128)(2,1)S(1)} %collective-permute-done.10.refs_7_) | copy-start | bytes 1769476
  133.1 7.8 %copy-start.17 = (bf16[192,2048]{1,0:T(8,128)(2,1)}, bf16[192,2048]{1,0:T(8,128)(2,1)S(1)}, u32[]{:S(2)}) copy-start(bf16[192,2048]{1,0:T(8,128)(2,1)S(1)} %collective-permute-done.9.refs_5_) | copy-start | bytes 2359300
  150.1 6.1 %collective-permute-start.15 = (bf16[2,1024,256]{2,1,0:T(8,128)(2,1)}, bf16[2,1024,256]{2,1,0:T(8,128)(2,1)S(1)}, u32[]{:S(2)}, u32[]{:S(2)}) collective-permute-start(bf16[2,1024,256]{2,1,0:T(8,128)(2,1)} %get-tuple-element.39), channel_id=1, source_target_pairs={{0,1},{1,0},{2,3},{3,2},{4,5},{5,4},{6,7},{7,6},{8,9},{9,8},{10,11... | collective-permute-start | bytes 3145736 | tf_op jit(solution)/shard_map/ppermute | solution.py:23
  156.8 7.6 %collective-permute-start.17 = (bf16[512,256]{1,0:T(8,128)(2,1)S(1)}, bf16[512,256]{1,0:T(8,128)(2,1)S(1)}, u32[]{:S(2)}, u32[]{:S(2)}) collective-permute-start(bf16[512,256]{1,0:T(8,128)(2,1)S(1)} %dynamic-slice_convert_fusion), channel_id=1, source_target_pairs={{0,2},{1,3},{2,0},{3,1},{4,6},{5,7},{6,4},{7,5},{8,10},{9,11},{10,... | collective-permute-start | bytes 786440 | tf_op jit(solution)/shard_map/ppermute | solution.py:23
  157.1 26.0 %collective-permute-start.16 = (bf16[1024,256]{1,0:T(8,128)(2,1)S(1)}, bf16[1024,256]{1,0:T(8,128)(2,1)S(1)}, u32[]{:S(2)}, u32[]{:S(2)}) collective-permute-start(bf16[1024,256]{1,0:T(8,128)(2,1)S(1)} %get-tuple-element.42), channel_id=1, source_target_pairs={{2,0},{3,1},{6,4},{7,5},{10,8},{11,9},{14,12},{15,13},{16,18},{17,... | collective-permute-start | bytes 1572872 | tf_op jit(solution)/shard_map/ppermute | solution.py:452
  164.4 16.5 %collective-permute-start.18 = (bf16[512,256]{1,0:T(8,128)(2,1)S(1)}, bf16[512,256]{1,0:T(8,128)(2,1)S(1)}, u32[]{:S(2)}, u32[]{:S(2)}) collective-permute-start(bf16[512,256]{1,0:T(8,128)(2,1)S(1)} %add_convert_fusion), channel_id=1, source_target_pairs={{0,16},{1,17},{4,20},{5,21},{8,24},{9,25},{12,28},{13,29},{18,2},{... | collective-permute-start | bytes 786440 | tf_op jit(solution)/shard_map/ppermute | solution.py:452
  165.7 17.4 %collective-permute-start.19 = (bf16[512,256]{1,0:T(8,128)(2,1)S(1)}, bf16[512,256]{1,0:T(8,128)(2,1)S(1)}, u32[]{:S(2)}, u32[]{:S(2)}) collective-permute-start(bf16[512,256]{1,0:T(8,128)(2,1)S(1)} %add_convert_fusion), channel_id=1, source_target_pairs={{2,16},{3,17},{6,20},{7,21},{10,24},{11,25},{14,28},{15,29},{16,2}... | collective-permute-start | bytes 786440 | tf_op jit(solution)/shard_map/ppermute | solution.py:452
  (10 other events, 23.7 us)

commit v5 on v4

--- a/solution.py
+++ b/solution.py
@@ -416,7 +416,7 @@
     part = after(parts[1], sent)
     other_part = exchange(part, "ctx", coarse)
     got = finish(part, [0], rest, cuts[1], cuts[2] - cuts[1])
-    gating = gate(after(query, received, got, other_part), received)
+    gating = gate(after(query, received, got), received)
     far_gating = exchange(gating, "ctx", half)
     owned = half * rows // 2
     norms_here = norms_of(after(received, gating), block, rows)

time: 185 us -> 182 us (0.984)
  local copies, waits for them, and re-layouts: 8.01 us -> 5.32 us
    unnamed x41 -> x31, local copies, waits for them, and re-layouts: 6.66 us -> 3.97 us
    ppermute x16, waiting for transfers between devices: 55.4 us -> 53.5 us  [exchange(): return lax.ppermute(block, axis, [(i, i ^ distance) for i in range(count)])]
  transfers between devices with their start and end apart: 22 -> 22, of which waited for: 15 -> 13; matrix products, arithmetic and copies ran while one was open for 2% -> 2% of each run, Pallas kernels for 5% -> 5%
where the time goes in v5:
time: 182 us
  waiting for transfers between devices  112 us (62%)
  starting transfers between devices  37 us (20%)
  Pallas kernels  23.3 us (13%)
  local copies, waits for them, and re-layouts  5.32 us (3%)
  other arithmetic  3.22 us (2%)
    ppermute x16, waiting for transfers between devices, exchange(): return lax.ppermute(block, axis, [(i, i ^ distance) for i in range(count)])  53.5 us
    all_to_all x1, waiting for transfers between devices, on_device(): lax.all_to_all(sent, 'ctx', split_axis=0, concat_axis=0, tiled=True)  24.5 us
    all_to_all x1, waiting for transfers between devices, on_device(): lax.all_to_all(own_mixture, 'ctx', split_axis=0, concat_axis=0, tiled=True)  16.8 us
    ppermute x16, starting transfers between devices, exchange(): return lax.ppermute(block, axis, [(i, i ^ distance) for i in range(count)])  16.2 us
    ppermute x3, waiting for transfers between devices, send_on(): lax.ppermute(value, ('ctx', 'tp'), [(place(*a), place(*b)) for a, b in pa...  14.5 us
    pallas_call x1, Pallas kernels, project(): pl.pallas_call(functools.partial(project_kernel, layout, places), grid_sp...  9.11 us
    ppermute x3, starting transfers between devices, send_on(): lax.ppermute(value, ('ctx', 'tp'), [(place(*a), place(*b)) for a, b in pa...  7.21 us
    pallas_call x1, Pallas kernels, convolve(): pl.pallas_call(convolve_kernel, in_specs=[pl.BlockSpec(memory_space=pltpu...  6.81 us
  transfers between devices with their start and end apart: 22, of which 13 were waited for; matrix products, arithmetic and copies ran while one was open for 2% of the time, Pallas kernels for 5%

profile of v5, /device:TPU:7, one launch (start us, length us, event | category | flops | bytes accessed | tf_op | source)
XLA Modules:
  0.0 181.6 jit_solution(7014675364336497430)
XLA Ops:
  0.0 1.9 %copy-done = bf16[3,2048,256]{2,1,0:T(8,128)(2,1)S(1)} copy-done((bf16[3,2048,256]{2,1,0:T(8,128)(2,1)S(1)}, bf16[3,2048,256]{2,1,0:T(8,128)(2,1)}, u32[]{:S(2)}) %copy-start) | copy-done | bytes 3145752
  3.0 3.3 %collective-permute-start = (bf16[32,2048]{1,0:T(8,128)(2,1)S(1)}, bf16[32,2048]{1,0:T(8,128)(2,1)S(1)}, u32[]{:S(2)}, u32[]{:S(2)}) collective-permute-start(bf16[32,2048]{1,0:T(8,128)(2,1)S(1)} %last_tokens.1), channel_id=1, source_target_pairs={{0,4},{4,8},{8,12},{12,16},{16,20},{20,24},{24,28},{1,5},{5,9},{9,... | collective-permute-start | bytes 393224 | tf_op jit(solution)/shard_map/ppermute | solution.py:379
  6.3 3.1 %collective-permute-done.halo_ref = bf16[32,2048]{1,0:T(8,128)(2,1)S(1)} collective-permute-done((bf16[32,2048]{1,0:T(8,128)(2,1)S(1)}, bf16[32,2048]{1,0:T(8,128)(2,1)S(1)}, u32[]{:S(2)}, u32[]{:S(2)}) %collective-permute-start) | collective-permute-done | bytes 131104 | tf_op jit(solution)/shard_map/ppermute | solution.py:379
  9.4 4.1 %featurize.1 = (bf16[8,256,256]{2,1,0:T(8,128)(2,1)S(1)}, bf16[8,256,256]{2,1,0:T(8,128)(2,1)S(1)}) custom-call(bf16[3,2048,256]{2,1,0:T(8,128)(2,1)S(1)} %copy-done, f32[3,7,2048]{2,1,0:T(8,128)S(1)} %copy-done.4, bf16[32,2048]{1,0:T(8,128)(2,1)S(1)} %collective-permute-done.halo_ref), custom_call_target="tpu_custom_call" | custom-call | flops 22020096 | bytes 10485760 | tf_op jit(solution)/shard_map/featurize/pallas_call | solution.py:115
  14.5 5.9 %all-to-all-start = ((bf16[8,256,256]{2,1,0:T(8,128)(2,1)}), bf16[8,256,256]{2,1,0:T(8,128)(2,1)}, u32[]{:S(2)}, u32[]{:S(2)}) async-start(bf16[8,256,256]{2,1,0:T(8,128)(2,1)} %copy-done.3), calls=%async_computation | async-start | bytes 2097152 | tf_op jit(solution)/shard_map/all_to_all | solution.py:383
  20.5 2.1 %merge.1 = (bf16[192,2048]{1,0:T(8,128)(2,1)}, bf16[144,2048]{1,0:T(8,128)(2,1)}, bf16[176,2048]{1,0:T(8,128)(2,1)}, f32[512,128]{1,0:T(8,128)S(1)}) custom-call(bf16[512,2048]{1,0:T(8,128)(2,1)S(1)} %copy-done.1, bf16[16,2048]{1,0:T(8,128)(2,1)S(1)} %copy-done.5, bf16[512,16]{1,0:T(8,128)(2,1)S(1)} %copy.10.up_ref), custom_call_target="tpu_custom_call" | custom-call | tf_op jit(solution)/shard_map/merge/pallas_call | solution.py:67
  22.7 2.2 %collective-permute-start.1 = (f32[1,512]{1,0:T(1,128)S(1)}, f32[1,512]{1,0:T(1,128)S(1)}, u32[]{:S(2)}, u32[]{:S(2)}) collective-permute-start(f32[1,512]{1,0:T(1,128)S(1)} %bitcast.17), channel_id=1, source_target_pairs={{0,1},{1,0},{2,3},{3,2},{4,5},{5,4},{6,7},{7,6},{8,9},{9,8},{10,11... | collective-permute-start | bytes 6152 | tf_op jit(solution)/shard_map/ppermute | solution.py:23
  25.1 1.5 collective-permute-start.3
  26.6 1.2 collective-permute-start.4
  28.6 16.8 %all-to-all-done.mixture_ref = bf16[8,256,256]{2,1,0:T(8,128)(2,1)} async-done(((bf16[8,256,256]{2,1,0:T(8,128)(2,1)}), bf16[8,256,256]{2,1,0:T(8,128)(2,1)}, u32[]{:S(2)}, u32[]{:S(2)}) %all-to-all-start) | async-done | bytes 1048608 | tf_op jit(solution)/shard_map/all_to_all | solution.py:383
  45.5 6.8 %convolve.1 = bf16[8,272,256]{2,1,0:T(8,128)(2,1)} custom-call(f32[16,2048]{1,0:T(8,128)S(1)} %copy-done.6, f32[256,128]{1,0:T(8,128)S(1)} %broadcast_in_dim.2.skip_ref, bf16[8,256,256]{2,1,0:T(8,128)(2,1)} %all-to-all-done.mixture_ref, bf16[16,256]{1,0:T(8,128)(2,1)S(1)} %fusion.8.added_ref), custom_call_target="tpu_custom_call" | custom-call | flops 8589934592 | bytes 20971520 | tf_op jit(solution)/shard_map/convolve/pallas_call | solution.py:189
  52.3 3.0 %collective-permute-done.4.refs_4_ = bf16[192,2048]{1,0:T(8,128)(2,1)S(1)} collective-permute-done((bf16[192,2048]{1,0:T(8,128)(2,1)}, bf16[192,2048]{1,0:T(8,128)(2,1)S(1)}, u32[]{:S(2)}, u32[]{:S(2)}) %collective-permute-start.4) | collective-permute-done | bytes 786464 | tf_op jit(solution)/shard_map/ppermute | solution.py:23
  56.3 4.3 %all-to-all-start.1 = ((bf16[8,272,256]{2,1,0:T(8,128)(2,1)}), bf16[8,272,256]{2,1,0:T(8,128)(2,1)S(1)}, u32[]{:S(2)}, u32[]{:S(2)}) async-start(bf16[8,272,256]{2,1,0:T(8,128)(2,1)} %convolve.1), calls=%async_computation.1 | async-start | bytes 2228224 | tf_op jit(solution)/shard_map/all_to_all | solution.py:415
  60.8 1.3 collective-permute-start.9
  62.1 24.5 %all-to-all-done.1.summed_ref = bf16[8,272,256]{2,1,0:T(8,128)(2,1)S(1)} async-done(((bf16[8,272,256]{2,1,0:T(8,128)(2,1)}), bf16[8,272,256]{2,1,0:T(8,128)(2,1)S(1)}, u32[]{:S(2)}, u32[]{:S(2)}) %all-to-all-start.1) | async-done | bytes 1114144 | tf_op jit(solution)/shard_map/all_to_all | solution.py:415
  88.2 2.8 %collective-permute-start.7 = (bf16[2048,256]{1,0:T(8,128)(2,1)S(1)}, bf16[2048,256]{1,0:T(8,128)(2,1)}, u32[]{:S(2)}, u32[]{:S(2)}) collective-permute-start(bf16[2048,256]{1,0:T(8,128)(2,1)S(1)} %gate.1.gating_ref), channel_id=1, source_target_pairs={{0,16},{4,20},{8,24},{12,28},{16,0},{20,4},{24,8},{28,12},{1,17},{... | collective-permute-start | bytes 3145736 | tf_op jit(solution)/shard_map/ppermute | solution.py:23
  91.0 1.1 collective-permute-start.8
  92.5 10.2 %collective-permute-done.12.refs_10_ = bf16[176,2048]{1,0:T(8,128)(2,1)} collective-permute-done((bf16[176,2048]{1,0:T(8,128)(2,1)}, bf16[176,2048]{1,0:T(8,128)(2,1)}, u32[]{:S(2)}, u32[]{:S(2)}) %collective-permute-start.12) | collective-permute-done | bytes 720928 | tf_op jit(solution)/shard_map/ppermute | solution.py:23
  103.7 1.4 collective-permute-start.14
  105.2 21.3 %collective-permute-done.11.refs_9_ = bf16[176,2048]{1,0:T(8,128)(2,1)S(1)} collective-permute-done((bf16[176,2048]{1,0:T(8,128)(2,1)}, bf16[176,2048]{1,0:T(8,128)(2,1)S(1)}, u32[]{:S(2)}, u32[]{:S(2)}) %collective-permute-start.11) | collective-permute-done | bytes 720928 | tf_op jit(solution)/shard_map/ppermute | solution.py:23
  127.3 4.9 %collective-permute-done.10.refs_7_ = bf16[144,2048]{1,0:T(8,128)(2,1)} collective-permute-done((bf16[144,2048]{1,0:T(8,128)(2,1)}, bf16[144,2048]{1,0:T(8,128)(2,1)}, u32[]{:S(2)}, u32[]{:S(2)}) %collective-permute-start.10) | collective-permute-done | bytes 589856 | tf_op jit(solution)/shard_map/ppermute | solution.py:23
  132.2 7.0 %collective-permute-done.13.refs_11_ = bf16[80,2048]{1,0:T(8,128)(2,1)} collective-permute-done((bf16[80,2048]{1,0:T(8,128)(2,1)S(1)}, bf16[80,2048]{1,0:T(8,128)(2,1)}, u32[]{:S(2)}, u32[]{:S(2)}) %collective-permute-start.13) | collective-permute-done | bytes 327712 | tf_op jit(solution)/shard_map/ppermute | solution.py:23
  139.2 9.1 %project.1 = (f32[1024,256]{1,0:T(8,128)}, f32[1024,256]{1,0:T(8,128)}, bf16[2,1024,256]{2,1,0:T(8,128)(2,1)}) custom-call(s32[4]{0:T(128)} %pad_add_fusion.where_ref, bf16[2048,256]{1,0:T(8,128)(2,1)} %copy-done.2, bf16[2048,256]{1,0:T(8,128)(2,1)} %collective-permute-done.7.far_gating_ref, bf16[192,2048]{1,0:T(8,128)(2,1)} %get-tuple-element.27.refs_0_, ...), custom_call_target="tpu_custom_call" | custom-call | flops 4294967296 | bytes 10485760 | tf_op jit(solution)/shard_map/project/pallas_call | solution.py:306
  148.4 2.8 %collective-permute-start.15 = (bf16[2,1024,256]{2,1,0:T(8,128)(2,1)}, bf16[2,1024,256]{2,1,0:T(8,128)(2,1)S(1)}, u32[]{:S(2)}, u32[]{:S(2)}) collective-permute-start(bf16[2,1024,256]{2,1,0:T(8,128)(2,1)} %get-tuple-element.39), channel_id=1, source_target_pairs={{0,1},{1,0},{2,3},{3,2},{4,5},{5,4},{6,7},{7,6},{8,9},{9,8},{10,11... | collective-permute-start | bytes 3145736 | tf_op jit(solution)/shard_map/ppermute | solution.py:23
  151.2 2.5 %collective-permute-done.15 = bf16[2,1024,256]{2,1,0:T(8,128)(2,1)S(1)} collective-permute-done((bf16[2,1024,256]{2,1,0:T(8,128)(2,1)}, bf16[2,1024,256]{2,1,0:T(8,128)(2,1)S(1)}, u32[]{:S(2)}, u32[]{:S(2)}) %collective-permute-start.15) | collective-permute-done | bytes 1048608 | tf_op jit(solution)/shard_map/ppermute | solution.py:23
  154.6 3.2 %collective-permute-start.16 = (bf16[1024,256]{1,0:T(8,128)(2,1)S(1)}, bf16[1024,256]{1,0:T(8,128)(2,1)S(1)}, u32[]{:S(2)}, u32[]{:S(2)}) collective-permute-start(bf16[1024,256]{1,0:T(8,128)(2,1)S(1)} %get-tuple-element.42), channel_id=1, source_target_pairs={{2,0},{3,1},{6,4},{7,5},{10,8},{11,9},{14,12},{15,13},{16,18},{17,... | collective-permute-start | bytes 1572872 | tf_op jit(solution)/shard_map/ppermute | solution.py:452
  157.8 4.1 %collective-permute-done.17 = bf16[512,256]{1,0:T(8,128)(2,1)S(1)} collective-permute-done((bf16[512,256]{1,0:T(8,128)(2,1)S(1)}, bf16[512,256]{1,0:T(8,128)(2,1)S(1)}, u32[]{:S(2)}, u32[]{:S(2)}) %collective-permute-start.17) | collective-permute-done | bytes 262176 | tf_op jit(solution)/shard_map/ppermute | solution.py:23
  161.9 1.3 collective-permute-start.18
  163.2 2.8 %collective-permute-start.19 = (bf16[512,256]{1,0:T(8,128)(2,1)S(1)}, bf16[512,256]{1,0:T(8,128)(2,1)S(1)}, u32[]{:S(2)}, u32[]{:S(2)}) collective-permute-start(bf16[512,256]{1,0:T(8,128)(2,1)S(1)} %add_convert_fusion), channel_id=1, source_target_pairs={{2,16},{3,17},{6,20},{7,21},{10,24},{11,25},{14,28},{15,29},{16,2}... | collective-permute-start | bytes 786440 | tf_op jit(solution)/shard_map/ppermute | solution.py:452
  166.0 12.3 %collective-permute-done.18 = bf16[512,256]{1,0:T(8,128)(2,1)S(1)} collective-permute-done((bf16[512,256]{1,0:T(8,128)(2,1)S(1)}, bf16[512,256]{1,0:T(8,128)(2,1)S(1)}, u32[]{:S(2)}, u32[]{:S(2)}) %collective-permute-start.18) | collective-permute-done | bytes 262176 | tf_op jit(solution)/shard_map/ppermute | solution.py:452
  178.3 2.2 %collective-permute-done.19 = bf16[512,256]{1,0:T(8,128)(2,1)S(1)} collective-permute-done((bf16[512,256]{1,0:T(8,128)(2,1)S(1)}, bf16[512,256]{1,0:T(8,128)(2,1)S(1)}, u32[]{:S(2)}, u32[]{:S(2)}) %collective-permute-start.19) | collective-permute-done | bytes 262176 | tf_op jit(solution)/shard_map/ppermute | solution.py:452
  180.5 1.1 multiply_convert_fusion
  (69 shorter events, 9.3 us)
Async XLA Ops:
  1.9 7.5 %copy-start.4 = (f32[3,7,2048]{2,1,0:T(8,128)S(1)}, f32[3,7,2048]{2,1,0:T(8,128)}, u32[]{:S(2)}) copy-start(f32[3,7,2048]{2,1,0:T(8,128)} %taps_ref.1) | copy-start | bytes 516100
  2.9 17.4 %copy-start.10 = (bf16[512,16]{0,1:T(8,128)(2,1)S(1)}, bf16[512,16]{0,1:T(8,128)(2,1)}, u32[]{:S(2)}) copy-start(bf16[512,16]{0,1:T(8,128)(2,1)} %param.14) | copy-start | bytes 49156
  2.9 17.5 %copy-start.1 = (bf16[512,2048]{1,0:T(8,128)(2,1)S(1)}, bf16[512,2048]{1,0:T(8,128)(2,1)}, u32[]{:S(2)}) copy-start(bf16[512,2048]{1,0:T(8,128)(2,1)} %frozen_ref) | copy-start | bytes 6291460
  3.0 17.5 %copy-start.5 = (bf16[16,2048]{1,0:T(8,128)(2,1)S(1)}, bf16[16,2048]{1,0:T(8,128)(2,1)}, u32[]{:S(2)}) copy-start(bf16[16,2048]{1,0:T(8,128)(2,1)} %down_ref.1) | copy-start | bytes 196612
  3.0 6.4 %collective-permute-start = (bf16[32,2048]{1,0:T(8,128)(2,1)S(1)}, bf16[32,2048]{1,0:T(8,128)(2,1)S(1)}, u32[]{:S(2)}, u32[]{:S(2)}) collective-permute-start(bf16[32,2048]{1,0:T(8,128)(2,1)S(1)} %last_tokens.1), channel_id=1, source_target_pairs={{0,4},{4,8},{8,12},{12,16},{16,20},{20,24},{24,28},{1,5},{5,9},{9,... | collective-permute-start | bytes 393224 | tf_op jit(solution)/shard_map/ppermute | solution.py:379
  14.4 31.0 %copy-start.11 = (f32[256]{0:T(256)S(1)}, f32[256]{0:T(256)}, u32[]{:S(2)}) copy-start(f32[256]{0:T(256)} %param.10) | copy-start | bytes 3076
  14.4 31.1 %copy-start.6 = (f32[16,2048]{1,0:T(8,128)S(1)}, f32[16,2048]{1,0:T(8,128)}, u32[]{:S(2)}) copy-start(f32[16,2048]{1,0:T(8,128)} %filters_ref.1) | copy-start | bytes 393220
  14.5 30.9 %all-to-all-start = ((bf16[8,256,256]{2,1,0:T(8,128)(2,1)}), bf16[8,256,256]{2,1,0:T(8,128)(2,1)}, u32[]{:S(2)}, u32[]{:S(2)}) async-start(bf16[8,256,256]{2,1,0:T(8,128)(2,1)} %copy-done.3), calls=%async_computation | async-start | bytes 2097152 | tf_op jit(solution)/shard_map/all_to_all | solution.py:383
  22.7 5.4 %collective-permute-start.1 = (f32[1,512]{1,0:T(1,128)S(1)}, f32[1,512]{1,0:T(1,128)S(1)}, u32[]{:S(2)}, u32[]{:S(2)}) collective-permute-start(f32[1,512]{1,0:T(1,128)S(1)} %bitcast.17), channel_id=1, source_target_pairs={{0,1},{1,0},{2,3},{3,2},{4,5},{5,4},{6,7},{7,6},{8,9},{9,8},{10,11... | collective-permute-start | bytes 6152 | tf_op jit(solution)/shard_map/ppermute | solution.py:23
  24.9 3.2 %collective-permute-start.2 = (f32[1,512]{1,0:T(1,128)S(1)}, f32[1,512]{1,0:T(1,128)S(1)}, u32[]{:S(2)}, u32[]{:S(2)}) collective-permute-start(f32[1,512]{1,0:T(1,128)S(1)} %bitcast.18), channel_id=1, source_target_pairs={{0,2},{1,3},{2,0},{3,1},{4,6},{5,7},{6,4},{7,5},{8,10},{9,11},{10,... | collective-permute-start | bytes 6152 | tf_op jit(solution)/shard_map/ppermute | solution.py:23
  25.1 3.4 %collective-permute-start.3 = (f32[1,512]{1,0:T(1,128)S(1)}, f32[1,512]{1,0:T(1,128)S(1)}, u32[]{:S(2)}, u32[]{:S(2)}) collective-permute-start(f32[1,512]{1,0:T(1,128)S(1)} %bitcast.19), channel_id=1, source_target_pairs={{0,3},{1,2},{2,1},{3,0},{4,7},{5,6},{6,5},{7,4},{8,11},{9,10},{10,... | collective-permute-start | bytes 6152 | tf_op jit(solution)/shard_map/ppermute | solution.py:23
  26.6 28.8 %collective-permute-start.4 = (bf16[192,2048]{1,0:T(8,128)(2,1)}, bf16[192,2048]{1,0:T(8,128)(2,1)S(1)}, u32[]{:S(2)}, u32[]{:S(2)}) collective-permute-start(bf16[192,2048]{1,0:T(8,128)(2,1)} %get-tuple-element.27.refs_0_), channel_id=1, source_target_pairs={{0,8},{4,12},{8,0},{12,4},{16,24},{20,28},{24,16},{28,20},{1,9},{5... | collective-permute-start | bytes 2359304 | tf_op jit(solution)/shard_map/ppermute | solution.py:23
  27.8 27.6 %collective-permute-start.5 = (bf16[192,2048]{1,0:T(8,128)(2,1)}, bf16[192,2048]{1,0:T(8,128)(2,1)S(1)}, u32[]{:S(2)}, u32[]{:S(2)}) collective-permute-start(bf16[192,2048]{1,0:T(8,128)(2,1)} %get-tuple-element.27.refs_0_), channel_id=1, source_target_pairs={{0,4},{4,0},{8,12},{12,8},{16,20},{20,16},{24,28},{28,24},{1,5},{5... | collective-permute-start | bytes 2359304 | tf_op jit(solution)/shard_map/ppermute | solution.py:23
  55.3 31.3 %copy-start.12 = (bf16[192,2048]{1,0:T(8,128)(2,1)}, bf16[192,2048]{1,0:T(8,128)(2,1)S(1)}, u32[]{:S(2)}) copy-start(bf16[192,2048]{1,0:T(8,128)(2,1)S(1)} %collective-permute-done.4.refs_4_) | copy-start | bytes 2359300
  56.3 30.3 %all-to-all-start.1 = ((bf16[8,272,256]{2,1,0:T(8,128)(2,1)}), bf16[8,272,256]{2,1,0:T(8,128)(2,1)S(1)}, u32[]{:S(2)}, u32[]{:S(2)}) async-start(bf16[8,272,256]{2,1,0:T(8,128)(2,1)} %convolve.1), calls=%async_computation.1 | async-start | bytes 2228224 | tf_op jit(solution)/shard_map/all_to_all | solution.py:415
  60.6 26.0 %collective-permute-start.6 = (bf16[144,2048]{1,0:T(8,128)(2,1)}, bf16[144,2048]{1,0:T(8,128)(2,1)}, u32[]{:S(2)}, u32[]{:S(2)}) collective-permute-start(bf16[144,2048]{1,0:T(8,128)(2,1)} %get-tuple-element.30.refs_2_), channel_id=1, source_target_pairs={{0,4},{4,0},{8,12},{12,8},{16,20},{20,16},{24,28},{28,24},{1,5},{5... | collective-permute-start | bytes 1769480 | tf_op jit(solution)/shard_map/ppermute | solution.py:23
  60.8 31.3 %collective-permute-start.9 = (bf16[144,2048]{1,0:T(8,128)(2,1)}, bf16[144,2048]{1,0:T(8,128)(2,1)}, u32[]{:S(2)}, u32[]{:S(2)}) collective-permute-start(bf16[144,2048]{1,0:T(8,128)(2,1)} %get-tuple-element.30.refs_2_), channel_id=1, source_target_pairs={{0,8},{4,12},{8,0},{12,4},{16,24},{20,28},{24,16},{28,20},{1,9},{5... | collective-permute-start | bytes 1769480 | tf_op jit(solution)/shard_map/ppermute | solution.py:23
  86.6 16.1 %collective-permute-start.12 = (bf16[176,2048]{1,0:T(8,128)(2,1)}, bf16[176,2048]{1,0:T(8,128)(2,1)}, u32[]{:S(2)}, u32[]{:S(2)}) collective-permute-start(bf16[176,2048]{1,0:T(8,128)(2,1)} %get-tuple-element.37.refs_8_), channel_id=1, source_target_pairs={{0,4},{4,0},{8,12},{12,8},{16,20},{20,16},{24,28},{28,24},{1,5},{5... | collective-permute-start | bytes 2162696 | tf_op jit(solution)/shard_map/ppermute | solution.py:23
  86.9 52.3 %copy-start.2 = (bf16[2048,256]{1,0:T(8,128)(2,1)}, bf16[2048,256]{1,0:T(8,128)(2,1)S(1)}, u32[]{:S(2)}) copy-start(bf16[2048,256]{1,0:T(8,128)(2,1)S(1)} %gate.1.gating_ref) | copy-start | bytes 3145732
  87.7 38.7 %collective-permute-start.11 = (bf16[176,2048]{1,0:T(8,128)(2,1)}, bf16[176,2048]{1,0:T(8,128)(2,1)S(1)}, u32[]{:S(2)}, u32[]{:S(2)}) collective-permute-start(bf16[176,2048]{1,0:T(8,128)(2,1)} %get-tuple-element.37.refs_8_), channel_id=1, source_target_pairs={{0,8},{4,12},{8,0},{12,4},{16,24},{20,28},{24,16},{28,20},{1,9},{5... | collective-permute-start | bytes 2162696 | tf_op jit(solution)/shard_map/ppermute | solution.py:23
  88.2 51.0 %collective-permute-start.7 = (bf16[2048,256]{1,0:T(8,128)(2,1)S(1)}, bf16[2048,256]{1,0:T(8,128)(2,1)}, u32[]{:S(2)}, u32[]{:S(2)}) collective-permute-start(bf16[2048,256]{1,0:T(8,128)(2,1)S(1)} %gate.1.gating_ref), channel_id=1, source_target_pairs={{0,16},{4,20},{8,24},{12,28},{16,0},{20,4},{24,8},{28,12},{1,17},{... | collective-permute-start | bytes 3145736 | tf_op jit(solution)/shard_map/ppermute | solution.py:23
  91.0 41.2 %collective-permute-start.8 = (bf16[192,2048]{1,0:T(8,128)(2,1)}, bf16[192,2048]{1,0:T(8,128)(2,1)S(1)}, u32[]{:S(2)}, u32[]{:S(2)}) collective-permute-start(bf16[192,2048]{1,0:T(8,128)(2,1)} %copy-done.12), channel_id=1, source_target_pairs={{0,4},{4,0},{8,12},{12,8},{16,20},{20,16},{24,28},{28,24},{1,5},{5... | collective-permute-start | bytes 2359304 | tf_op jit(solution)/shard_map/ppermute | solution.py:23
  92.1 40.1 %collective-permute-start.10 = (bf16[144,2048]{1,0:T(8,128)(2,1)}, bf16[144,2048]{1,0:T(8,128)(2,1)}, u32[]{:S(2)}, u32[]{:S(2)}) collective-permute-start(bf16[144,2048]{1,0:T(8,128)(2,1)} %collective-permute-done.9.refs_6_), channel_id=1, source_target_pairs={{0,4},{4,0},{8,12},{12,8},{16,20},{20,16},{24,28},{28,24},{1,5},{5... | collective-permute-start | bytes 1769480 | tf_op jit(solution)/shard_map/ppermute | solution.py:23
  103.7 35.5 %collective-permute-start.14 = (bf16[96,2048]{1,0:T(8,128)(2,1)S(1)}, bf16[96,2048]{1,0:T(8,128)(2,1)}, u32[]{:S(2)}, u32[]{:S(2)}) collective-permute-start(bf16[96,2048]{1,0:T(8,128)(2,1)S(1)} %slice.40), channel_id=1, source_target_pairs={{0,8},{4,12},{8,0},{12,4},{16,24},{20,28},{24,16},{28,20},{1,9},{5... | collective-permute-start | bytes 1179656 | tf_op jit(solution)/shard_map/ppermute | solution.py:23
  126.4 12.8 %copy-start.9 = (bf16[176,2048]{1,0:T(8,128)(2,1)}, bf16[176,2048]{1,0:T(8,128)(2,1)S(1)}, u32[]{:S(2)}) copy-start(bf16[176,2048]{1,0:T(8,128)(2,1)S(1)} %collective-permute-done.11.refs_9_) | copy-start | bytes 2162692
  126.5 12.7 %collective-permute-start.13 = (bf16[80,2048]{1,0:T(8,128)(2,1)S(1)}, bf16[80,2048]{1,0:T(8,128)(2,1)}, u32[]{:S(2)}, u32[]{:S(2)}) collective-permute-start(bf16[80,2048]{1,0:T(8,128)(2,1)S(1)} %slice.39), channel_id=1, source_target_pairs={{0,4},{4,0},{8,12},{12,8},{16,20},{20,16},{24,28},{28,24},{1,5},{5... | collective-permute-start | bytes 983048 | tf_op jit(solution)/shard_map/ppermute | solution.py:23
  132.2 7.0 %copy-start.14 = (bf16[192,2048]{1,0:T(8,128)(2,1)}, bf16[192,2048]{1,0:T(8,128)(2,1)S(1)}, u32[]{:S(2)}) copy-start(bf16[192,2048]{1,0:T(8,128)(2,1)S(1)} %collective-permute-done.8.refs_5_) | copy-start | bytes 2359300
  148.4 5.3 %collective-permute-start.15 = (bf16[2,1024,256]{2,1,0:T(8,128)(2,1)}, bf16[2,1024,256]{2,1,0:T(8,128)(2,1)S(1)}, u32[]{:S(2)}, u32[]{:S(2)}) collective-permute-start(bf16[2,1024,256]{2,1,0:T(8,128)(2,1)} %get-tuple-element.39), channel_id=1, source_target_pairs={{0,1},{1,0},{2,3},{3,2},{4,5},{5,4},{6,7},{7,6},{8,9},{9,8},{10,11... | collective-permute-start | bytes 3145736 | tf_op jit(solution)/shard_map/ppermute | solution.py:23
  154.3 7.6 %collective-permute-start.17 = (bf16[512,256]{1,0:T(8,128)(2,1)S(1)}, bf16[512,256]{1,0:T(8,128)(2,1)S(1)}, u32[]{:S(2)}, u32[]{:S(2)}) collective-permute-start(bf16[512,256]{1,0:T(8,128)(2,1)S(1)} %dynamic-slice_convert_fusion), channel_id=1, source_target_pairs={{0,2},{1,3},{2,0},{3,1},{4,6},{5,7},{6,4},{7,5},{8,10},{9,11},{10,... | collective-permute-start | bytes 786440 | tf_op jit(solution)/shard_map/ppermute | solution.py:23
  154.6 25.9 %collective-permute-start.16 = (bf16[1024,256]{1,0:T(8,128)(2,1)S(1)}, bf16[1024,256]{1,0:T(8,128)(2,1)S(1)}, u32[]{:S(2)}, u32[]{:S(2)}) collective-permute-start(bf16[1024,256]{1,0:T(8,128)(2,1)S(1)} %get-tuple-element.42), channel_id=1, source_target_pairs={{2,0},{3,1},{6,4},{7,5},{10,8},{11,9},{14,12},{15,13},{16,18},{17,... | collective-permute-start | bytes 1572872 | tf_op jit(solution)/shard_map/ppermute | solution.py:452
  161.9 16.3 %collective-permute-start.18 = (bf16[512,256]{1,0:T(8,128)(2,1)S(1)}, bf16[512,256]{1,0:T(8,128)(2,1)S(1)}, u32[]{:S(2)}, u32[]{:S(2)}) collective-permute-start(bf16[512,256]{1,0:T(8,128)(2,1)S(1)} %add_convert_fusion), channel_id=1, source_target_pairs={{0,16},{1,17},{4,20},{5,21},{8,24},{9,25},{12,28},{13,29},{18,2},{... | collective-permute-start | bytes 786440 | tf_op jit(solution)/shard_map/ppermute | solution.py:452
  163.2 17.2 %collective-permute-start.19 = (bf16[512,256]{1,0:T(8,128)(2,1)S(1)}, bf16[512,256]{1,0:T(8,128)(2,1)S(1)}, u32[]{:S(2)}, u32[]{:S(2)}) collective-permute-start(bf16[512,256]{1,0:T(8,128)(2,1)S(1)} %add_convert_fusion), channel_id=1, source_target_pairs={{2,16},{3,17},{6,20},{7,21},{10,24},{11,25},{14,28},{15,29},{16,2}... | collective-permute-start | bytes 786440 | tf_op jit(solution)/shard_map/ppermute | solution.py:452
  (5 other events, 12.0 us)
